TPU v7x, 256 devices: a whole 4x4x8 slice. The times are simulated.
256 devices in a mesh: ga: 8 (over z_lo, core), ba: 32 (over x, y, z_hi).
Axes of the slice: x: 4, y: 4, z: 8 (z_hi: 2, z_lo: 4; z = z_hi * 4 + z_lo), core: 2. Of those that a mesh axis runs over, the one named last changes fastest.
Arguments:
- white_noise: float32 [256, 512, 512], P('ba', 'ga'), may hold values from -6 to 6
- amplitude: float32 [512, 512, 256], P('ba', 'ga'), may hold values from 0.2 to 2, as said below
- recharge: float32 [256, 256, 128], P('ga', 'ba'), may hold values from -6 to 6
- head_guess: float32 [256, 256, 128], P('ga', 'ba'), may hold values from -6 to 6
Outputs:
- conductivity: float32 [256, 256, 128], P('ga', 'ba')
- pressure: float32 [256, 256, 128], P('ga', 'ba')
Inputs may be any that keep to these rules, and one draw needn't show every extreme that they name: amplitude is even in the frequencies: its entry at (ky, kx, kz) equals its entry at ((-ky) mod 512, (-kx) mod 512, (-kz) mod 256).
All inputs are finite; a program needn't handle non-finite values.
Results may differ from a plain program's by a relative error of at most 0.00029.
Values sent between devices are 32-bit elements; how exact they have to be, the bound alone decides.
No kernel may reach another device: no remote copies, remote signals or barrier semaphores. Data moves between devices by JAX's collectives and lax.ppermute only.
A program may use at most 64 MiB of HBM per device.

v0:
```python
import math

import jax
import jax.numpy as jnp
from jax import lax
from jax.sharding import PartitionSpec as P

AX = 256
AY = 256
AZ = 128
SWEEPS = 2
EX = 512
EY = 512
EZ = 256


highest = lax.Precision.HIGHEST


def with_halo(value, sides, width):
    for axis, dim in sides:
        peers, length = (lax.axis_size(axis), value.shape[dim])
        up = [(i, (i + 1) % peers) for i in range(peers - 1)]
        down = [(j, i) for i, j in up]
        last = lax.slice_in_dim(value, length - width, length, axis=dim)
        leading = lax.slice_in_dim(value, 0, width, axis=dim)
        before = lax.ppermute(last, axis, up)
        after = lax.ppermute(leading, axis, down)
        value = jnp.concatenate([before, value, after], axis=dim)
    return value


def tables(row_ids, col_ids, period):
    product = row_ids[:, None] * col_ids[None, :] % period
    angles = product.astype(jnp.float32) * (2.0 * math.pi / period)
    return (jnp.cos(angles), jnp.sin(angles))


def neighbours(padded):
    return [
        padded[2:, 1:-1, 1:-1],
        padded[:-2, 1:-1, 1:-1],
        padded[1:-1, 2:, 1:-1],
        padded[1:-1, :-2, 1:-1],
        padded[1:-1, 1:-1, 2:],
        padded[1:-1, 1:-1, :-2],
    ]


def forward_y(in_block):
    length = in_block.shape[1]
    positions = jnp.arange(length, dtype=jnp.int32)
    cosine, sine = tables(positions, positions, length)
    cos_part = jnp.einsum("zyxc,yk->zkxc", in_block, cosine, precision=highest)
    sin_part = jnp.einsum("zyxc,yk->zkxc", in_block, sine, precision=highest)
    return jnp.stack([cos_part[..., 0] + sin_part[..., 1], cos_part[..., 1] - sin_part[..., 0]], -1)


def forward_z(in_block):
    length = in_block.shape[0]
    positions = jnp.arange(length, dtype=jnp.int32)
    cosine, sine = tables(positions, positions, length)
    cos_part = jnp.einsum("zyxc,zk->yxck", in_block, cosine, precision=highest)
    sin_part = jnp.einsum("zyxc,zk->yxck", in_block, sine, precision=highest)
    return jnp.stack(
        [cos_part[:, :, 0] + sin_part[:, :, 1], cos_part[:, :, 1] - sin_part[:, :, 0]], 2
    )


def inverse_y(in_block):
    length = in_block.shape[0]
    cosine, sine = tables(
        jnp.arange(length, dtype=jnp.int32), jnp.arange(AY, dtype=jnp.int32), length
    )
    cos_part = jnp.einsum("kxcz,ky->yxcz", in_block, cosine, precision=highest)
    sin_part = jnp.einsum("kxcz,ky->yxcz", in_block, sine, precision=highest)
    return jnp.stack(
        [cos_part[:, :, 0] - sin_part[:, :, 1], cos_part[:, :, 1] + sin_part[:, :, 0]], 2
    )


def body(white_noise, amplitude, recharge, head_guess):
    planes, height, extent = white_noise.shape
    indices = jnp.arange(extent, dtype=jnp.int32)
    cos_x, sin_x = tables(indices, indices, extent)
    flattened = white_noise.reshape(planes * height, extent)
    real_part = jnp.dot(flattened, cos_x, precision=highest)
    imag_part = -jnp.dot(flattened, sin_x, precision=highest)
    spectrum = jnp.stack([real_part, imag_part], -1).reshape(planes, height, extent, 2)
    spectrum = forward_y(lax.all_to_all(spectrum, "ga", split_axis=2, concat_axis=1, tiled=True))
    spectrum = forward_z(lax.all_to_all(spectrum, "ba", split_axis=1, concat_axis=0, tiled=True))
    spectrum = spectrum * amplitude[:, :, None, :]
    full_z = spectrum.shape[3]
    cos_z, sin_z = tables(
        jnp.arange(full_z, dtype=jnp.int32), jnp.arange(AZ, dtype=jnp.int32), full_z
    )
    cos_part = jnp.einsum("yxck,kz->yxcz", spectrum, cos_z, precision=highest)
    sin_part = jnp.einsum("yxck,kz->yxcz", spectrum, sin_z, precision=highest)
    spectrum = jnp.stack(
        [cos_part[:, :, 0] - sin_part[:, :, 1], cos_part[:, :, 1] + sin_part[:, :, 0]], 2
    )
    spectrum = inverse_y(lax.all_to_all(spectrum, "ba", split_axis=1, concat_axis=0, tiled=True))
    spectrum = lax.all_to_all(spectrum, "ba", split_axis=0, concat_axis=1, tiled=True)
    rows_own = AX // lax.axis_size("ga")
    own_x = lax.axis_index("ga") * rows_own + jnp.arange(rows_own, dtype=jnp.int32)
    in_block = lax.all_gather(spectrum, "ga", axis=1, tiled=True)
    freq_ids = jnp.arange(in_block.shape[1], dtype=jnp.int32)
    cosine, sine = tables(freq_ids, own_x, EX)
    added = jnp.einsum("ykz,kx->xyz", in_block[:, :, 0], cosine, precision=highest)
    added = added - jnp.einsum("ykz,kx->xyz", in_block[:, :, 1], sine, precision=highest)
    log_field = added
    log_field = log_field * (1.0 / (EX * EY * EZ))
    conductivity = jnp.exp(log_field)
    cond_padded = with_halo(conductivity, (("ga", 0), ("ba", 1)), 1)
    cond_padded = jnp.pad(cond_padded, ((0, 0), (0, 0), (1, 1)))
    face_terms = [0.5 * (conductivity + side) for side in neighbours(cond_padded)]
    diagonal = face_terms[0]
    for term in face_terms[1:]:
        diagonal = diagonal + term
    pressure = head_guess
    for sweep_index in range(SWEEPS):
        padded = with_halo(pressure, (("ga", 0), ("ba", 1)), 1)
        padded = jnp.pad(padded, ((0, 0), (0, 0), (1, 1)))
        sides = neighbours(padded)
        pushed = face_terms[0] * sides[0]
        for term, side in zip(face_terms[1:], sides[1:]):
            pushed = pushed + term * side
        pressure = (recharge + pushed) / diagonal
    return (conductivity, pressure)


def solution(mesh):
    placed = (P("ba", "ga", None), P("ba", "ga", None), P("ga", "ba", None), P("ga", "ba", None))
    return jax.shard_map(
        body,
        mesh=mesh,
        in_specs=placed,
        out_specs=(P("ga", "ba", None), P("ga", "ba", None)),
        check_vma=False,
    )
```

profile of v0, /device:TPU:38, one launch (start us, length us, event | category | flops | bytes accessed | tf_op | source)
XLA Modules:
  0.0 423.2 jit_solution(3604326097866909044)
XLA Ops:
  8.4 6.6 %fusion.28 = f32[512,512]{0,1:T(8,128)} fusion(f32[512,512]{1,0:T(8,128)S(1)} %bitcast.104), kind=kOutput, calls=%fused_computation.52 | convolution fusion | flops 1614282752 | bytes 2097152 | tf_op jit(solution)/shard_map/dot_general | solution.py:87
  15.0 6.7 %convolution_negate_fusion = f32[512,512]{0,1:T(8,128)} fusion(f32[512,512]{1,0:T(8,128)S(1)} %bitcast.105), kind=kOutput, calls=%fused_computation.15 | convolution fusion | flops 1614544896 | bytes 2097152 | tf_op jit(solution)/shard_map/dot_general | solution.py:88
  25.8 3.8 fusion.162
  29.7 5.9 %reshape.28 = f32[8,1,65536]{2,1,0:T(1,128)S(1)} reshape(f32[512,2,8,64]{3,2,1,0:T(8,128)} %fusion.162) | data formatting | bytes 4194304
  35.6 52.8 %all_to_all.72 = f32[8,1,65536]{2,1,0:T(1,128)} all-to-all(f32[8,1,65536]{2,1,0:T(1,128)S(1)} %reshape.28), channel_id=1, replica_groups=mesh['ga'=8,'ba'=32] {'ga'}, dimensions={0} | all-to-all | bytes 4194304 | tf_op jit(solution)/shard_map/all_to_all | solution.py:90
  88.9 7.2 %reduce = f32[8,65536]{1,0:T(8,128)S(1)} reduce(f32[8,1,65536]{2,1,0:T(1,128)} %all_to_all.72, f32[]{:T(128)} %broadcast.185), dimensions={1}, to_apply=%all_to_all.52.reduce_sub_computation | reduce | bytes 4194308 | tf_op jit(solution)/shard_map/all_to_all | solution.py:90
  96.1 3.6 reshape.29
  99.7 6.6 %copy.67 = f32[8,64,8,64,2]{1,2,3,4,0:T(8,128)} copy(f32[8,64,8,64,2]{1,0,4,3,2:T(8,128)} %bitcast.107) | data formatting | bytes 4194304 | tf_op jit(solution)/shard_map/all_to_all | solution.py:90
  106.4 3.4 all_to_all.55
  109.8 8.8 %convolution_bitcast_fusion = f32[8,512,64,2]{1,2,3,0:T(8,128)S(1)} fusion(f32[8,512,64,2]{1,2,3,0:T(8,128)S(1)} %all_to_all.55), kind=kOutput, calls=%fused_computation.8 | convolution fusion | flops 3224895488 | bytes 4194304 | tf_op jit(solution)/shard_map/zyxc,yk->zkxc/dot_general | solution.py:55
  118.5 8.3 %convolution_bitcast_fusion.1 = f32[8,512,64,2]{1,2,3,0:T(8,128)S(1)} fusion(f32[8,512,64,2]{1,2,3,0:T(8,128)S(1)} %all_to_all.55), kind=kOutput, calls=%fused_computation.9 | convolution fusion | flops 3224895488 | bytes 4194304 | tf_op jit(solution)/shard_map/zyxc,yk->zkxc/dot_general | solution.py:54
  127.6 4.5 %copy.38 = f32[8,512,64,2]{2,3,0,1:T(2,128)} copy(f32[8,512,64,2]{1,2,3,0:T(8,128)S(1)} %pad_maximum_fusion.1) | data formatting | bytes 4194304 | tf_op jit(solution)/shard_map/stack | solution.py:56
  132.1 5.6 %reshape.30 = f32[32,1,16384]{2,1,0:T(1,128)S(1)} reshape(f32[512,8,2,64]{3,2,1,0:T(2,128)} %bitcast.106) | data formatting | bytes 4194304
  137.7 63.0 %all_to_all.73 = f32[32,1,16384]{2,1,0:T(1,128)} all-to-all(f32[32,1,16384]{2,1,0:T(1,128)S(1)} %reshape.30), channel_id=1, replica_groups=mesh['ga'=8,'ba'=32] {'ba'}, dimensions={0} | all-to-all | bytes 4194304 | tf_op jit(solution)/shard_map/all_to_all | solution.py:91
  200.7 7.4 %reduce.1 = f32[32,16384]{1,0:T(8,128)S(1)} reduce(f32[32,1,16384]{2,1,0:T(1,128)} %all_to_all.73, f32[]{:T(128)} %broadcast.185), dimensions={1}, to_apply=%all_to_all.56.reduce_sub_computation | reduce | bytes 4194308 | tf_op jit(solution)/shard_map/all_to_all | solution.py:91
  208.1 4.4 %reshape.31 = f32[512,8,2,64]{3,2,1,0:T(2,128)} reshape(f32[32,16384]{1,0:T(8,128)S(1)} %reduce.1) | data formatting | bytes 4194304
  212.5 3.5 copy.39
  218.6 3.7 copy.41
  235.0 21.3 %all_to_all.74 = f32[16,64,2,128]{3,2,0,1:T(2,128)S(1)} all-to-all(f32[16,64,2,128]{3,2,0,1:T(2,128)S(1)} %copy.43), channel_id=1, replica_groups=mesh['ga'=8,'ba'=32] {'ba'}, dimensions={1} | all-to-all | bytes 2097152 | tf_op jit(solution)/shard_map/all_to_all | solution.py:102
  256.5 3.0 fusion.20
  259.5 3.0 fusion.22
  263.1 17.9 %all_to_all.75 = f32[256,2,2,128]{3,2,1,0:T(2,128)S(1)} all-to-all(f32[256,2,2,128]{3,2,1,0:T(2,128)S(1)} %copy.45), channel_id=1, replica_groups=mesh['ga'=8,'ba'=32] {'ba'}, dimensions={0} | all-to-all | bytes 1048576 | tf_op jit(solution)/shard_map/all_to_all | solution.py:103
  282.1 11.8 %collective-permute-start.1 = (f32[1,8,128]{2,0,1:T(1,128)S(1)}, f32[1,8,128]{2,0,1:T(1,128)S(1)}, u32[]{:S(2)}, u32[]{:S(2)}) collective-permute-start(f32[1,8,128]{2,0,1:T(1,128)S(1)} %bitcast.120), channel_id=1, source_target_pairs={{32,0},{64,32},{96,64},{128,96},{160,128},{192,160},{224,192},{33,... | collective-permute-start | bytes 12296 | tf_op jit(solution)/shard_map/ppermute | solution.py:28
  295.9 49.8 %all-gather.2.cloned.1.call-done = f32[8,512,2,128]{3,1,0,2:T(8,128)} async-done(((f32[8,64,2,128]{3,1,0,2:T(8,128)}), f32[8,512,2,128]{3,1,0,2:T(8,128)}) %all-gather.2.cloned.1.call-update) | async-done | bytes 4194320 | tf_op jit(solution)/shard_map/all_gather | solution.py:106
  345.7 3.2 fusion
  348.9 3.2 fusion.6
  352.1 3.2 collective-permute-start
  357.9 9.4 %collective-permute-start.5 = (f32[34,1,128]{2,0,1:T(8,128)S(1)}, f32[34,1,128]{2,0,1:T(8,128)S(1)}, u32[]{:S(2)}, u32[]{:S(2)}) collective-permute-start(f32[34,1,128]{2,0,1:T(8,128)S(1)} %get-tuple-element.21), channel_id=1, source_target_pairs={{1,0},{2,1},{3,2},{4,3},{5,4},{6,5},{7,6},{8,7},{9,8},{10,9},{11,1... | collective-permute-start | bytes 52232 | tf_op jit(solution)/shard_map/ppermute | solution.py:28
  369.3 10.8 %collective-permute-start.4 = (f32[34,1,128]{2,0,1:T(8,128)S(1)}, f32[34,1,128]{2,0,1:T(8,128)S(1)}, u32[]{:S(2)}, u32[]{:S(2)}) collective-permute-start(f32[34,1,128]{2,0,1:T(8,128)S(1)} %get-tuple-element.19), channel_id=1, source_target_pairs={{1,0},{2,1},{3,2},{4,3},{5,4},{6,5},{7,6},{8,7},{9,8},{10,9},{11,1... | collective-permute-start | bytes 52232 | tf_op jit(solution)/shard_map/ppermute | solution.py:28
  382.3 10.4 %collective-permute-done.6 = f32[34,1,128]{2,0,1:T(8,128)S(1)} collective-permute-done((f32[34,1,128]{2,0,1:T(8,128)S(1)}, f32[34,1,128]{2,0,1:T(8,128)S(1)}, u32[]{:S(2)}, u32[]{:S(2)}) %collective-permute-start.6) | collective-permute-done | bytes 17440 | tf_op jit(solution)/shard_map/ppermute | solution.py:27
  402.1 7.8 %collective-permute-start.11 = (f32[34,1,128]{2,0,1:T(8,128)S(1)}, f32[34,1,128]{2,0,1:T(8,128)S(1)}, u32[]{:S(2)}, u32[]{:S(2)}) collective-permute-start(f32[34,1,128]{2,0,1:T(8,128)S(1)} %get-tuple-element.16), channel_id=1, source_target_pairs={{0,1},{1,2},{2,3},{3,4},{4,5},{5,6},{6,7},{7,8},{8,9},{9,10},{10,1... | collective-permute-start | bytes 52232 | tf_op jit(solution)/shard_map/ppermute | solution.py:27
  410.6 4.0 collective-permute-done.11
  (65 shorter events, 43.3 us)
Async XLA Ops:
  7.2 1.2 copy-start
  7.2 338.5 %all-gather.2.cloned.1.call-start = ((), (), s32[]{:S(2)}) async-start(), calls=%async_computation.4 | async-start | bytes 4718592 | tf_op jit(solution)/shard_map/all_gather | solution.py:106
  21.7 2.1 copy-start.3
  228.1 1.2 copy-start.2
  262.6 19.4 %copy-start.5 = (f32[32,8,128]{2,1,0:T(8,128)S(1)}, f32[32,8,128]{2,1,0:T(8,128)}, u32[]{:S(2)}) copy-start(f32[32,8,128]{2,1,0:T(8,128)} %param.7) | copy-start | bytes 393220
  282.1 75.8 %collective-permute-start.1 = (f32[1,8,128]{2,0,1:T(1,128)S(1)}, f32[1,8,128]{2,0,1:T(1,128)S(1)}, u32[]{:S(2)}, u32[]{:S(2)}) collective-permute-start(f32[1,8,128]{2,0,1:T(1,128)S(1)} %bitcast.120), channel_id=1, source_target_pairs={{32,0},{64,32},{96,64},{128,96},{160,128},{192,160},{224,192},{33,... | collective-permute-start | bytes 12296 | tf_op jit(solution)/shard_map/ppermute | solution.py:28
  293.9 64.0 %collective-permute-start.3 = (f32[1,8,128]{2,0,1:T(1,128)S(1)}, f32[1,8,128]{2,0,1:T(1,128)S(1)}, u32[]{:S(2)}, u32[]{:S(2)}) collective-permute-start(f32[1,8,128]{2,0,1:T(1,128)S(1)} %bitcast.119), channel_id=1, source_target_pairs={{0,32},{32,64},{64,96},{96,128},{128,160},{160,192},{192,224},{1,3... | collective-permute-start | bytes 12296 | tf_op jit(solution)/shard_map/ppermute | solution.py:27
  348.9 44.1 %copy-start.4 = (f32[32,8,128]{2,1,0:T(8,128)S(1)}, f32[32,8,128]{2,1,0:T(8,128)}, u32[]{:S(2)}) copy-start(f32[32,8,128]{2,1,0:T(8,128)} %param.6) | copy-start | bytes 393220
  352.1 17.1 %collective-permute-start = (f32[1,8,128]{2,0,1:T(1,128)S(1)}, f32[1,8,128]{2,0,1:T(1,128)S(1)}, u32[]{:S(2)}, u32[]{:S(2)}) collective-permute-start(f32[1,8,128]{2,0,1:T(1,128)S(1)} %get-tuple-element.25), channel_id=1, source_target_pairs={{32,0},{64,32},{96,64},{128,96},{160,128},{192,160},{224,192},{33,... | collective-permute-start | bytes 12296 | tf_op jit(solution)/shard_map/ppermute | solution.py:28
  355.3 13.9 %collective-permute-start.2 = (f32[1,8,128]{2,0,1:T(1,128)S(1)}, f32[1,8,128]{2,0,1:T(1,128)S(1)}, u32[]{:S(2)}, u32[]{:S(2)}) collective-permute-start(f32[1,8,128]{2,0,1:T(1,128)S(1)} %get-tuple-element.24), channel_id=1, source_target_pairs={{0,32},{32,64},{64,96},{96,128},{128,160},{160,192},{192,224},{1,3... | collective-permute-start | bytes 12296 | tf_op jit(solution)/shard_map/ppermute | solution.py:27
  357.9 24.2 %collective-permute-start.5 = (f32[34,1,128]{2,0,1:T(8,128)S(1)}, f32[34,1,128]{2,0,1:T(8,128)S(1)}, u32[]{:S(2)}, u32[]{:S(2)}) collective-permute-start(f32[34,1,128]{2,0,1:T(8,128)S(1)} %get-tuple-element.21), channel_id=1, source_target_pairs={{1,0},{2,1},{3,2},{4,3},{5,4},{6,5},{7,6},{8,7},{9,8},{10,9},{11,1... | collective-permute-start | bytes 52232 | tf_op jit(solution)/shard_map/ppermute | solution.py:28
  367.3 14.8 %collective-permute-start.7 = (f32[34,1,128]{2,0,1:T(8,128)S(1)}, f32[34,1,128]{2,0,1:T(8,128)S(1)}, u32[]{:S(2)}, u32[]{:S(2)}) collective-permute-start(f32[34,1,128]{2,0,1:T(8,128)S(1)} %get-tuple-element.20), channel_id=1, source_target_pairs={{0,1},{1,2},{2,3},{3,4},{4,5},{5,6},{6,7},{7,8},{8,9},{9,10},{10,1... | collective-permute-start | bytes 52232 | tf_op jit(solution)/shard_map/ppermute | solution.py:27
  369.3 13.0 %collective-permute-start.4 = (f32[34,1,128]{2,0,1:T(8,128)S(1)}, f32[34,1,128]{2,0,1:T(8,128)S(1)}, u32[]{:S(2)}, u32[]{:S(2)}) collective-permute-start(f32[34,1,128]{2,0,1:T(8,128)S(1)} %get-tuple-element.19), channel_id=1, source_target_pairs={{1,0},{2,1},{3,2},{4,3},{5,4},{6,5},{7,6},{8,7},{9,8},{10,9},{11,1... | collective-permute-start | bytes 52232 | tf_op jit(solution)/shard_map/ppermute | solution.py:28
  380.1 12.6 %collective-permute-start.6 = (f32[34,1,128]{2,0,1:T(8,128)S(1)}, f32[34,1,128]{2,0,1:T(8,128)S(1)}, u32[]{:S(2)}, u32[]{:S(2)}) collective-permute-start(f32[34,1,128]{2,0,1:T(8,128)S(1)} %get-tuple-element.18), channel_id=1, source_target_pairs={{0,1},{1,2},{2,3},{3,4},{4,5},{5,6},{6,7},{7,8},{8,9},{9,10},{10,1... | collective-permute-start | bytes 52232 | tf_op jit(solution)/shard_map/ppermute | solution.py:27
  382.1 33.8 %copy-start.1 = (f32[8,64,512]{2,1,0:T(8,128)S(1)}, f32[8,64,512]{2,1,0:T(8,128)}, u32[]{:S(2)}) copy-start(f32[8,64,512]{2,1,0:T(8,128)} %param.4) | copy-start | bytes 3145732
  393.3 4.3 %collective-permute-start.8 = (f32[1,8,128]{2,0,1:T(1,128)S(1)}, f32[1,8,128]{2,0,1:T(1,128)S(1)}, u32[]{:S(2)}, u32[]{:S(2)}) collective-permute-start(f32[1,8,128]{2,0,1:T(1,128)S(1)} %get-tuple-element.23), channel_id=1, source_target_pairs={{32,0},{64,32},{96,64},{128,96},{160,128},{192,160},{224,192},{33,... | collective-permute-start | bytes 12296 | tf_op jit(solution)/shard_map/ppermute | solution.py:28
  395.2 4.9 %collective-permute-start.9 = (f32[1,8,128]{2,0,1:T(1,128)S(1)}, f32[1,8,128]{2,0,1:T(1,128)S(1)}, u32[]{:S(2)}, u32[]{:S(2)}) collective-permute-start(f32[1,8,128]{2,0,1:T(1,128)S(1)} %get-tuple-element.22), channel_id=1, source_target_pairs={{0,32},{32,64},{64,96},{96,128},{128,160},{160,192},{192,224},{1,3... | collective-permute-start | bytes 12296 | tf_op jit(solution)/shard_map/ppermute | solution.py:27
  400.1 10.5 %collective-permute-start.10 = (f32[34,1,128]{2,0,1:T(8,128)S(1)}, f32[34,1,128]{2,0,1:T(8,128)S(1)}, u32[]{:S(2)}, u32[]{:S(2)}) collective-permute-start(f32[34,1,128]{2,0,1:T(8,128)S(1)} %get-tuple-element.17), channel_id=1, source_target_pairs={{1,0},{2,1},{3,2},{4,3},{5,4},{6,5},{7,6},{8,7},{9,8},{10,9},{11,1... | collective-permute-start | bytes 52232 | tf_op jit(solution)/shard_map/ppermute | solution.py:28
  402.1 12.6 %collective-permute-start.11 = (f32[34,1,128]{2,0,1:T(8,128)S(1)}, f32[34,1,128]{2,0,1:T(8,128)S(1)}, u32[]{:S(2)}, u32[]{:S(2)}) collective-permute-start(f32[34,1,128]{2,0,1:T(8,128)S(1)} %get-tuple-element.16), channel_id=1, source_target_pairs={{0,1},{1,2},{2,3},{3,4},{4,5},{5,6},{6,7},{7,8},{8,9},{9,10},{10,1... | collective-permute-start | bytes 52232 | tf_op jit(solution)/shard_map/ppermute | solution.py:27
Sparse Core Ops, SparseCore 0:
  282.2 63.4 all-gather.1
where the time goes:
time: 430 us; the launch traced here: 423 us
  blocking collectives  155 us (36%)
  waiting for transfers between devices  66.8 us (16%)
  starting transfers between devices  57.6 us (13%)
  local copies, waits for them, and re-layouts  54.5 us (13%)
  matrix products  53.2 us (12%)
  other arithmetic  21.1 us (5%)
  between operations  15 us (3%)
    all_to_all x2, blocking collectives, body(): lax.all_to_all(spectrum, 'ba', split_axis=1, concat_axis=0, tiled=True)  84.3 us
    all_to_all x1, blocking collectives, body(): lax.all_to_all(spectrum, 'ga', split_axis=2, concat_axis=1, tiled=True)  52.8 us
    all_gather x1, waiting for transfers between devices, body(): in_block = lax.all_gather(spectrum, 'ga', axis=1, tiled=True)  49.8 us
    ppermute x6, starting transfers between devices, with_halo(): after = lax.ppermute(leading, axis, down)  39 us
    unnamed x19, local copies, waits for them, and re-layouts  23.1 us
    ppermute x6, starting transfers between devices, with_halo(): before = lax.ppermute(last, axis, up)  18.5 us
    all_to_all x1, blocking collectives, body(): lax.all_to_all(spectrum, 'ba', split_axis=0, concat_axis=1, tiled=True)  17.9 us
    ppermute x6, waiting for transfers between devices, with_halo(): before = lax.ppermute(last, axis, up)  16.9 us
  transfers between devices with their start and end apart: 13, of which 4 were waited for; matrix products, arithmetic and copies ran while one was open for 2% of the time, Pallas kernels for 0%

commit v1 on v0

v1 whole, which is shorter than its diff:
```python
import functools
import math

import jax
import jax.numpy as jnp
import ml_dtypes
import numpy as np
from jax import lax
from jax.experimental import pallas as pl
from jax.experimental.pallas import tpu as pltpu
from jax.sharding import PartitionSpec as P

AX, AY, AZ = 256, 256, 128
EX, EY, EZ = 512, 512, 256
GA, BA = 8, 32
DEVS = GA * BA
PACKED_GA = 4
XROWS = 40
CHUNK = XROWS + 32
VMEM = 48 * 2**20
f32, bf16 = jnp.float32, jnp.bfloat16


def split_np(table):
    high = table.astype(np.float32).astype(ml_dtypes.bfloat16)
    low = (table - high.astype(np.float64)).astype(np.float32).astype(ml_dtypes.bfloat16)
    return np.stack([high, low])


def trig(rows, cols, period):
    angles = (np.outer(rows, cols) % period) * (2.0 * math.pi / period)
    return np.cos(angles), np.sin(angles)


def kx_of():
    ids = np.zeros(DEVS, np.int64)
    for b in range(BA):
        for g in range(GA):
            if b:
                kx = 64 * g + b
            elif g < PACKED_GA:
                kx = 64 * g + 32
            else:
                kx = -1 if g == PACKED_GA else 64 * g
            ids[b * GA + g] = kx
    return ids


@functools.cache
def tables():
    kx = kx_of()
    packed = kx < 0
    alternating = 1.0 - 2.0 * (np.arange(EX) % 2)
    cos, sin = trig(np.maximum(kx, 0), np.arange(EX), EX)
    wide_re, wide_im = cos.copy(), -sin
    wide_re[packed], wide_im[packed] = alternating, 1.0
    x_fwd = np.concatenate([wide_re, wide_im])

    y_fwd = np.stack(trig(np.arange(EY), np.arange(EY), EY))

    half, quarter, block = np.meshgrid(np.arange(2), np.arange(4), np.arange(BA), indexing="ij")
    z_order = (8 * block + 2 * quarter + half).reshape(-1)
    z_fwd = np.concatenate(trig(z_order, np.arange(EZ), EZ), 1)
    z_inv = np.concatenate(trig(np.arange(EZ), np.arange(AZ), EZ), 1)

    cos, sin = trig(np.arange(AY), np.arange(EY), EY)
    y_inv = np.concatenate(
        [np.stack([cos, sin], 1).reshape(2 * AY, EY), np.stack([-sin, cos], 1).reshape(2 * AY, EY)], 1
    )

    xs = np.clip((32 * np.arange(GA)[:, None] - 4 + np.arange(XROWS)).reshape(-1), 0, AX - 1)
    cos, sin = trig(xs, np.maximum(kx, 0), EX)
    back_re, back_im = 2.0 * cos, -2.0 * sin
    back_re[:, packed] = alternating[xs][:, None]
    back_im[:, packed] = 1.0
    x_inv = np.stack([back_re, back_im], 2).reshape(xs.size, 2 * DEVS) / (EX * EY * EZ)
    return tuple(split_np(t) for t in (x_fwd, y_fwd, z_fwd, z_inv, y_inv, x_inv))


def split(value):
    high = value.astype(bf16)
    return high, (value - high.astype(f32)).astype(bf16)


def dot3(a, b, rhs_dim=0):
    dims = (((1,), (rhs_dim,)), ((), ()))
    mul = functools.partial(lax.dot_general, dimension_numbers=dims, preferred_element_type=f32)
    return mul(a[0], b[0]) + (mul(a[0], b[1]) + mul(a[1], b[0]))


def enter_kernel(where, noise, table, amp, head, rech, sent, amp_sent, amp_dc, below, above):
    ga = where[0]
    for part in range(2):
        rows = split(noise[256 * part : 256 * part + 256, :])
        for c in range(2):
            own = slice(256 * c, 256 * c + 256)
            result = dot3((table[0, own, :], table[1, own, :]), rows, 1)
            for q in range(2):
                sent[pl.ds(4 * c + 2 * part + q, DEVS, stride=8), :] = result[:, 128 * q : 128 * q + 128]
    for half in range(2):
        lanes = slice(128 * half, 128 * half + 128)
        first = amp[:, 0, lanes]
        amp_dc[:, lanes] = first
        middle = amp[:, 32, lanes]
        amp_sent[0:16, lanes] = jnp.where(ga < PACKED_GA, middle, first)
        for b in range(1, BA):
            amp_sent[16 * b : 16 * b + 16, lanes] = amp[:, b, lanes]
    for out, near in ((below, (0, 1, 0)), (above, (6, 7, 7))):
        for i, (ref, y) in enumerate(zip((head, head, rech), near)):
            out[32 * i : 32 * i + 32, :] = ref[pl.ds(y, 32, stride=8), :]


def middle_kernel(where, got, amp, amp_dc, y_fwd, z_fwd, z_inv, y_inv, sent, rows, lines):
    low_half = lax.broadcasted_iota(jnp.int32, (BA, 128), 1) < 64
    for c in range(2):
        for q in range(4):
            for p in range(4):
                even = got[pl.ds(16 * p + 4 * c + q, BA, stride=64), :]
                odd = got[pl.ds(16 * p + 8 + 4 * c + q, BA, stride=64), :]
                first = jnp.where(low_half, even, pltpu.roll(odd, 64, 1))
                second = jnp.where(low_half, pltpu.roll(even, 64, 1), odd)
                for half, value in enumerate((first, second)):
                    at = slice(256 * c + 128 * half + 32 * q, 256 * c + 128 * half + 32 * q + 32)
                    high, low = split(value)
                    rows[0, at, 128 * p : 128 * p + 128] = high
                    rows[1, at, 128 * p : 128 * p + 128] = low

    def spectral(amp_ref, keep):
        for part in range(2):
            ky = slice(256 * part, 256 * part + 256)
            data = (rows[0], rows[1])
            by_cos = dot3((y_fwd[0, 0, ky, :], y_fwd[1, 0, ky, :]), data, 1)
            by_sin = dot3((y_fwd[0, 1, ky, :], y_fwd[1, 1, ky, :]), data, 1)
            real = by_cos[:, :256] + by_sin[:, 256:]
            imag = by_cos[:, 256:] - by_sin[:, :256]
            forward = (z_fwd[0], z_fwd[1])
            real, imag = dot3(split(real), forward), dot3(split(imag), forward)
            scale = amp_ref[ky, :]
            new_real = (real[:, :256] + imag[:, 256:]) * scale
            new_imag = (imag[:, :256] - real[:, 256:]) * scale
            back = (z_inv[0], z_inv[1])
            real, imag = dot3(split(new_real), back), dot3(split(new_imag), back)
            for c, value in enumerate((real[:, :128] - imag[:, 128:], imag[:, :128] + real[:, 128:])):
                high, low = split(value)
                at = slice(512 * c + 256 * part, 512 * c + 256 * part + 256)
                lines[0, at, :] = high
                lines[1, at, :] = low

    spectral(amp, None)
    sent[...] = dot3((y_inv[0], y_inv[1]), (lines[0], lines[1]))

    @pl.when(where[1] == 1)
    def _():
        spectral(amp_dc, None)
        other = dot3((y_inv[0], y_inv[1]), (lines[0], lines[1]))
        odd_row = lax.broadcasted_iota(jnp.int32, (2 * AY, AZ), 0) % 2 == 1
        sent[...] = jnp.where(odd_row, other, sent[...])


def field_kernel(where, got, table, head, rech, lo_halo, hi_halo, sent):
    ga = where[0]
    log_field = dot3((table[0], table[1]), split(got[...]))
    row = lax.broadcasted_iota(jnp.int32, (XROWS, AZ), 0)
    corner = lax.broadcasted_iota(jnp.int32, (8, AZ), 0)

    def pack(far, near):
        edges = jnp.where(
            corner == 0, lo_halo[32 + near : 33 + near, :], hi_halo[near : near + 1, :]
        )
        return (head[8 * far : 8 * far + 8, :], head[8 * near : 8 * near + 8, :],
                rech[8 * near : 8 * near + 8, :], edges)

    up, down = pack(30, 31), pack(1, 0)
    for g in range(GA):
        x = row + (32 * g - 4)
        inside = (x >= 0) & (x < AX)
        value = jnp.exp(log_field[XROWS * g : XROWS * g + XROWS, :])
        sent[CHUNK * g : CHUNK * g + XROWS, :] = jnp.where(inside, value, 0.0)
        for i in range(4):
            at = CHUNK * g + XROWS + 8 * i
            sent[at : at + 8, :] = jnp.where(ga + 1 == g, up[i], down[i])


def sweep_kernel(where, got, lo_cond, hi_cond, head, rech, lo_halo, hi_halo, cond_out, press_out,
                 head_ext, rech_ext, staged):
    ga, ba = where[0], where[2]
    head_ext[...] = jnp.zeros_like(head_ext)
    rech_ext[...] = jnp.zeros_like(rech_ext)
    for y in range(8):
        at = XROWS * (y + 2)
        head_ext[at + 4 : at + 36, :] = head[pl.ds(y, 32, stride=8), :]
        rech_ext[at + 4 : at + 36, :] = rech[pl.ds(y, 32, stride=8), :]
    for halo, (first, second, only) in ((lo_halo, (0, 1, 1)), (hi_halo, (10, 11, 10))):
        for ref, y, i in ((head_ext, first, 0), (head_ext, second, 1), (rech_ext, only, 2)):
            ref[XROWS * y + 4 : XROWS * y + 36, :] = halo[32 * i : 32 * i + 32, :]
    for side, peer, present, far, near in (
        (0, jnp.maximum(ga - 1, 0), ga > 0, 2, 3), (1, jnp.minimum(ga + 1, GA - 1), ga < GA - 1, 37, 36)
    ):
        block = got[pl.ds(pl.multiple_of(peer * CHUNK + XROWS, 8), 32), :]
        block = jnp.where(present, block, 0.0)
        for y in range(8):
            at = XROWS * (y + 2)
            head_ext[at + far : at + far + 1, :] = block[y : y + 1, :]
            head_ext[at + near : at + near + 1, :] = block[8 + y : 9 + y, :]
            rech_ext[at + near : at + near + 1, :] = block[16 + y : 17 + y, :]
        head_ext[XROWS + near : XROWS + near + 1, :] = block[24:25, :]
        head_ext[10 * XROWS + near : 10 * XROWS + near + 1, :] = block[25:26, :]

    lane = lax.broadcasted_iota(jnp.int32, (XROWS, AZ), 1)
    row = lax.broadcasted_iota(jnp.int32, (XROWS, AZ), 0)
    x = row + (32 * ga - 4)
    inside_x = (x >= 0) & (x < AX)

    def in_plane(value):
        total = pltpu.roll(value, 1, 0) + pltpu.roll(value, XROWS - 1, 0)
        total = total + jnp.where(lane > 0, pltpu.roll(value, 1, 1), 0.0)
        return total + jnp.where(lane < AZ - 1, pltpu.roll(value, AZ - 1, 1), 0.0)

    cond = [lo_cond[0:XROWS, :], lo_cond[CHUNK : CHUNK + XROWS, :]]
    cond += [got[CHUNK * y : CHUNK * y + XROWS, :] for y in range(8)]
    cond += [hi_cond[0:XROWS, :], hi_cond[CHUNK : CHUNK + XROWS, :]]
    planes = [head_ext[XROWS * y : XROWS * y + XROWS, :] for y in range(12)]
    weight = {y: 6.0 * cond[y] + (in_plane(cond[y]) + (cond[y - 1] + cond[y + 1])) for y in range(1, 11)}
    source = {y: 2.0 * rech_ext[XROWS * y : XROWS * y + XROWS, :] for y in range(1, 11)}
    for sweep in range(2):
        flow = {y: cond[y] * planes[y] for y in range(sweep, 12 - sweep)}
        new = dict()
        for y in range(sweep + 1, 11 - sweep):
            heads = in_plane(planes[y]) + (planes[y - 1] + planes[y + 1])
            flows = in_plane(flow[y]) + (flow[y - 1] + flow[y + 1])
            new[y] = (source[y] + (cond[y] * heads + flows)) / weight[y]
            if sweep == 0:
                inside = inside_x
                if y == 1:
                    inside = inside & (ba > 0)
                if y == 10:
                    inside = inside & (ba < BA - 1)
                new[y] = jnp.where(inside, new[y], 0.0)
        planes = new
    for y in range(8):
        cond_out[pl.ds(y, 32, stride=8), :] = got[CHUNK * y + 4 : CHUNK * y + 36, :]
        staged[...] = planes[y + 2]
        press_out[pl.ds(y, 32, stride=8), :] = staged[4:36, :]


def kernel_call(kernel, outs, inputs, scratch=()):
    vmem = pl.BlockSpec(memory_space=pltpu.VMEM)
    smem = pl.BlockSpec(memory_space=pltpu.SMEM)
    return pl.pallas_call(
        kernel,
        out_shape=[jax.ShapeDtypeStruct(shape, f32) for shape in outs],
        in_specs=[smem] + [vmem] * (len(inputs) - 1),
        out_specs=[vmem] * len(outs),
        scratch_shapes=list(scratch),
        compiler_params=pltpu.CompilerParams(vmem_limit_bytes=VMEM),
    )(*inputs)


def body(noise, amplitude, recharge, head_guess):
    x_fwd, y_fwd, z_fwd, z_inv, y_inv, x_inv = (jnp.asarray(t) for t in tables())
    ga, ba = lax.axis_index("ga"), lax.axis_index("ba")
    packed = ((ga == PACKED_GA) & (ba == 0)).astype(jnp.int32)
    where = jnp.stack([ga.astype(jnp.int32), packed, ba.astype(jnp.int32)])
    noise = noise.reshape(512, EX)
    recharge = recharge.reshape(256, AZ)
    head = head_guess.reshape(256, AZ)
    sent, amp_sent, amp_dc, below, above = kernel_call(
        enter_kernel, [(8 * DEVS, 128), (512, EZ), (16, EZ), (96, AZ), (96, AZ)],
        [where, noise, x_fwd, amplitude, head, recharge],
    )
    up = [(i, i + 1) for i in range(BA - 1)]
    down = [(j, i) for i, j in up]
    hi_halo = lax.ppermute(below, "ba", down)
    lo_halo = lax.ppermute(above, "ba", up)
    amp_dc = lax.ppermute(amp_dc, "ga", [(0, PACKED_GA)])
    amp_dc = lax.all_gather(amp_dc, "ba", axis=0, tiled=True)
    amp_got = lax.all_to_all(amp_sent, "ba", 0, 0, tiled=True)
    got = lax.all_to_all(sent, ("ba", "ga"), 0, 0, tiled=True)
    (sent,) = kernel_call(
        middle_kernel, [(2 * AY, AZ)],
        [where, got, amp_got, amp_dc, y_fwd, z_fwd, z_inv, y_inv],
        [pltpu.VMEM((2, 512, 512), bf16), pltpu.VMEM((2, 1024, AZ), bf16)],
    )
    got = lax.all_to_all(sent, ("ba", "ga"), 0, 0, tiled=True)
    (sent,) = kernel_call(
        field_kernel, [(CHUNK * GA, AZ)], [where, got, x_inv, head, recharge, lo_halo, hi_halo]
    )
    got = lax.all_to_all(sent, "ga", 0, 0, tiled=True)
    lo_cond = lax.ppermute(got[6 * CHUNK :], "ba", up)
    hi_cond = lax.ppermute(got[: 2 * CHUNK], "ba", down)
    ext = pltpu.VMEM((12 * XROWS, AZ), f32)
    conductivity, pressure = kernel_call(
        sweep_kernel, [(256, AZ), (256, AZ)],
        [where, got, lo_cond, hi_cond, head, recharge, lo_halo, hi_halo],
        [ext, ext, pltpu.VMEM((XROWS, AZ), f32)],
    )
    return conductivity.reshape(32, 8, AZ), pressure.reshape(32, 8, AZ)


def solution(mesh):
    placed = (P("ba", "ga", None), P("ba", "ga", None), P("ga", "ba", None), P("ga", "ba", None))
    return jax.shard_map(
        body,
        mesh=mesh,
        in_specs=placed,
        out_specs=(P("ga", "ba", None), P("ga", "ba", None)),
        check_vma=False,
    )
```

time: 430 us -> 276 us (0.64)
  the two profiles are of different devices: /device:TPU:38 before, /device:TPU:1 now
where the time goes in v1:
time: 276 us; the launch traced here: 273 us
  blocking collectives  168 us (61%)
  starting transfers between devices  64.8 us (23%)
  waiting for transfers between devices  15.3 us (6%)
  Pallas kernels  12.5 us (5%)
  local copies, waits for them, and re-layouts  11.4 us (4%)
    all_gather x1, blocking collectives, body(): amp_dc = lax.all_gather(amp_dc, 'ba', axis=0, tiled=True)  122 us
    all_to_all x2, starting transfers between devices, body(): got = lax.all_to_all(sent, ('ba', 'ga'), 0, 0, tiled=True)  48.1 us
    all_to_all x1, blocking collectives, body(): amp_got = lax.all_to_all(amp_sent, 'ba', 0, 0, tiled=True)  30.9 us
    all_to_all x1, blocking collectives, body(): got = lax.all_to_all(sent, 'ga', 0, 0, tiled=True)  14.3 us
    pallas_call x4, Pallas kernels, kernel_call(): pl.pallas_call(kernel, out_shape=[jax.ShapeDtypeStruct(shape, f32) for sh...  12.5 us
    unnamed x30, local copies, waits for them, and re-layouts  11.4 us
    ppermute x1, starting transfers between devices, body(): lo_halo = lax.ppermute(above, 'ba', up)  8.13 us
    ppermute x1, waiting for transfers between devices, body(): hi_halo = lax.ppermute(below, 'ba', down)  7.53 us
  transfers between devices with their start and end apart: 7, of which 3 were waited for; matrix products, arithmetic and copies ran while one was open for 0% of the time, Pallas kernels for 0%

profile of v1, /device:TPU:1, one launch (start us, length us, event | category | flops | bytes accessed | tf_op | source)
XLA Modules:
  0.0 272.5 jit_solution(131034090784649297)
XLA Ops:
  0.6 0.1 pad_add_fusion.where
  0.7 0.9 copy-done.3
  1.6 0.9 copy-done.5
  2.5 1.2 copy-done.7
  3.8 1.2 copy-done.8
  5.0 1.2 copy-done.9
  6.2 1.8 shard_map.113
  8.0 0.0 copy-start
  8.0 30.9 %all_to_all.44 = f32[32,16,256]{2,1,0:T(8,128)} all-to-all(f32[32,16,256]{2,1,0:T(8,128)S(1)} %bitcast.32), channel_id=1, replica_groups=mesh['ga'=8,'ba'=32] {'ba'}, dimensions={0} | all-to-all | bytes 1048576 | tf_op jit(solution)/shard_map/all_to_all | solution.py:277
  39.0 11.1 %all-to-all-start = ((f32[256,8,128]{2,1,0:T(8,128)}), f32[256,8,128]{2,1,0:T(8,128)S(1)}, u32[]{:S(2)}, u32[]{:S(2)}) async-start(f32[256,8,128]{2,1,0:T(8,128)} %bitcast.29), calls=%async_computation | async-start | bytes 2097152 | tf_op jit(solution)/shard_map/all_to_all | solution.py:278
  50.1 0.7 collective-permute-start
  50.8 122.4 %all_gather.3.amp_dc = f32[512,256]{1,0:T(8,128)} all-gather(f32[16,256]{1,0:T(8,128)S(1)} %collective-permute-done), channel_id=1, replica_groups=mesh['ga'=8,'ba'=32] {'ba'}, dimensions={0}, use_global_device_ids=true | all-gather | bytes 540672 | tf_op jit(solution)/shard_map/all_gather | solution.py:276
  173.2 0.0 all-to-all-done
  173.2 1.0 copy-done.1
  174.3 1.0 copy-done.2
  175.3 1.0 copy-done.13
  176.3 0.9 copy-done.14
  177.3 7.8 %shard_map.114 = f32[512,128]{1,0:T(8,128)S(1)} custom-call(s32[3]{0:T(128)S(1)} %pad_add_fusion.where, f32[2048,128]{1,0:T(8,128)S(1)} %bitcast.18, f32[512,256]{1,0:T(8,128)S(1)} %bitcast.19, f32[512,256]{1,0:T(8,128)S(1)} %copy-done.2, bf16[2,2,512,512]{3,2,1,0:T(8,128)(2,1)S(1)} %copy-done, bf16[2,256,512]{2,1,0:T(8,128)(2,1)S(1)} %copy-done.13, ...), custom_call_target="tpu_custom_call" | custom-call | tf_op jit(solution)/shard_map/pallas_call | solution.py:249
  185.1 0.7 copy-done.11
  185.8 36.9 %all-to-all-start.2 = ((f32[256,2,128]{2,1,0:T(2,128)}), f32[256,2,128]{2,1,0:T(2,128)S(1)}, u32[]{:S(2)}, u32[]{:S(2)}) async-start(f32[256,2,128]{2,1,0:T(2,128)} %bitcast.31), calls=%async_computation.2 | async-start | bytes 524288 | tf_op jit(solution)/shard_map/all_to_all | solution.py:284
  222.8 8.1 %collective-permute-start.1 = (f32[96,128]{1,0:T(8,128)S(1)}, f32[96,128]{1,0:T(8,128)S(1)}, u32[]{:S(2)}, u32[]{:S(2)}) collective-permute-start(f32[96,128]{1,0:T(8,128)S(1)} %get-tuple-element.12), channel_id=1, source_target_pairs={{0,1},{1,2},{2,3},{3,4},{4,5},{5,6},{6,7},{7,8},{8,9},{9,10},{10,1... | collective-permute-start | bytes 147464 | tf_op jit(solution)/shard_map/ppermute | solution.py:274
  230.9 1.3 collective-permute-start.2
  232.2 7.5 %collective-permute-done.2.hi_halo = f32[96,128]{1,0:T(8,128)S(1)} collective-permute-done((f32[96,128]{1,0:T(8,128)S(1)}, f32[96,128]{1,0:T(8,128)S(1)}, u32[]{:S(2)}, u32[]{:S(2)}) %collective-permute-start.2) | collective-permute-done | bytes 49184 | tf_op jit(solution)/shard_map/ppermute | solution.py:273
  239.8 0.0 copy-start.12
  239.8 1.1 copy-done.12
  240.9 1.0 shard_map.115
  241.8 14.3 %all_to_all.45 = f32[8,72,128]{2,1,0:T(8,128)S(1)} all-to-all(f32[8,72,128]{2,1,0:T(8,128)S(1)} %bitcast.27), channel_id=1, replica_groups=mesh['ga'=8,'ba'=32] {'ga'}, dimensions={0} | all-to-all | bytes 589824 | tf_op jit(solution)/shard_map/all_to_all | solution.py:288
  256.1 5.4 %collective-permute-start.3 = (f32[144,128]{1,0:T(8,128)S(1)}, f32[144,128]{1,0:T(8,128)S(1)}, u32[]{:S(2)}, u32[]{:S(2)}) collective-permute-start(f32[144,128]{1,0:T(8,128)S(1)} %bitcast.34), channel_id=1, source_target_pairs={{0,1},{1,2},{2,3},{3,4},{4,5},{5,6},{6,7},{7,8},{8,9},{9,10},{10,1... | collective-permute-start | bytes 221192 | tf_op jit(solution)/shard_map/ppermute | solution.py:289
  261.5 1.3 collective-permute-start.4
  262.8 0.8 collective-permute-done.3.lo_cond
  263.7 7.0 %collective-permute-done.4.hi_cond = f32[144,128]{1,0:T(8,128)S(1)} collective-permute-done((f32[144,128]{1,0:T(8,128)S(1)}, f32[144,128]{1,0:T(8,128)S(1)}, u32[]{:S(2)}, u32[]{:S(2)}) %collective-permute-start.4) | collective-permute-done | bytes 73760 | tf_op jit(solution)/shard_map/ppermute | solution.py:290
  270.6 1.9 shard_map.116
  (21 shorter events, 0.0 us)
Async XLA Ops:
  0.7 0.9 copy-start.3
  1.6 0.9 copy-start.5
  2.5 1.2 copy-start.7
  3.8 1.2 copy-start.8
  5.0 1.2 copy-start.9
  8.0 31.0 %copy-start.10 = (f32[2048,128]{1,0:T(8,128)}, f32[2048,128]{1,0:T(8,128)S(1)}, u32[]{:S(2)}) copy-start(f32[2048,128]{1,0:T(8,128)S(1)} %get-tuple-element.9) | copy-start | bytes 3145732
  8.0 165.2 %copy-start = (bf16[2,2,512,512]{3,2,1,0:T(8,128)(2,1)S(1)}, bf16[2,2,512,512]{3,2,1,0:T(8,128)(2,1)}, u32[]{:S(2)}) copy-start(bf16[2,2,512,512]{3,2,1,0:T(8,128)(2,1)} %constant.26.clone.y_fwd) | copy-start | bytes 6291460
  39.0 134.2 %all-to-all-start = ((f32[256,8,128]{2,1,0:T(8,128)}), f32[256,8,128]{2,1,0:T(8,128)S(1)}, u32[]{:S(2)}, u32[]{:S(2)}) async-start(f32[256,8,128]{2,1,0:T(8,128)} %bitcast.29), calls=%async_computation | async-start | bytes 2097152 | tf_op jit(solution)/shard_map/all_to_all | solution.py:278
  50.1 0.7 collective-permute-start
  173.2 1.0 copy-start.1
  174.3 1.0 copy-start.2
  175.3 1.0 copy-start.13
  176.3 0.9 copy-start.14
  177.3 62.5 %copy-start.4 = (f32[32,8,128]{2,1,0:T(8,128)S(1)}, f32[32,8,128]{2,1,0:T(8,128)}, u32[]{:S(2)}) copy-start(f32[32,8,128]{2,1,0:T(8,128)} %param.13) | copy-start | bytes 393220
  177.3 62.5 %copy-start.6 = (f32[32,8,128]{2,1,0:T(8,128)S(1)}, f32[32,8,128]{2,1,0:T(8,128)}, u32[]{:S(2)}) copy-start(f32[32,8,128]{2,1,0:T(8,128)} %param.12) | copy-start | bytes 393220
  185.1 0.7 copy-start.11
  185.8 53.9 %all-to-all-start.2 = ((f32[256,2,128]{2,1,0:T(2,128)}), f32[256,2,128]{2,1,0:T(2,128)S(1)}, u32[]{:S(2)}, u32[]{:S(2)}) async-start(f32[256,2,128]{2,1,0:T(2,128)} %bitcast.31), calls=%async_computation.2 | async-start | bytes 524288 | tf_op jit(solution)/shard_map/all_to_all | solution.py:284
  222.8 9.4 %collective-permute-start.1 = (f32[96,128]{1,0:T(8,128)S(1)}, f32[96,128]{1,0:T(8,128)S(1)}, u32[]{:S(2)}, u32[]{:S(2)}) collective-permute-start(f32[96,128]{1,0:T(8,128)S(1)} %get-tuple-element.12), channel_id=1, source_target_pairs={{0,1},{1,2},{2,3},{3,4},{4,5},{5,6},{6,7},{7,8},{8,9},{9,10},{10,1... | collective-permute-start | bytes 147464 | tf_op jit(solution)/shard_map/ppermute | solution.py:274
  230.9 8.8 %collective-permute-start.2 = (f32[96,128]{1,0:T(8,128)S(1)}, f32[96,128]{1,0:T(8,128)S(1)}, u32[]{:S(2)}, u32[]{:S(2)}) collective-permute-start(f32[96,128]{1,0:T(8,128)S(1)} %get-tuple-element.13), channel_id=1, source_target_pairs={{1,0},{2,1},{3,2},{4,3},{5,4},{6,5},{7,6},{8,7},{9,8},{10,9},{11,1... | collective-permute-start | bytes 147464 | tf_op jit(solution)/shard_map/ppermute | solution.py:273
  239.8 1.1 copy-start.12
  256.1 7.6 %collective-permute-start.3 = (f32[144,128]{1,0:T(8,128)S(1)}, f32[144,128]{1,0:T(8,128)S(1)}, u32[]{:S(2)}, u32[]{:S(2)}) collective-permute-start(f32[144,128]{1,0:T(8,128)S(1)} %bitcast.34), channel_id=1, source_target_pairs={{0,1},{1,2},{2,3},{3,4},{4,5},{5,6},{6,7},{7,8},{8,9},{9,10},{10,1... | collective-permute-start | bytes 221192 | tf_op jit(solution)/shard_map/ppermute | solution.py:289
  261.5 9.1 %collective-permute-start.4 = (f32[144,128]{1,0:T(8,128)S(1)}, f32[144,128]{1,0:T(8,128)S(1)}, u32[]{:S(2)}, u32[]{:S(2)}) collective-permute-start(f32[144,128]{1,0:T(8,128)S(1)} %bitcast.33), channel_id=1, source_target_pairs={{1,0},{2,1},{3,2},{4,3},{5,4},{6,5},{7,6},{8,7},{9,8},{10,9},{11,1... | collective-permute-start | bytes 221192 | tf_op jit(solution)/shard_map/ppermute | solution.py:290

commit v2 on v1

--- a/solution.py
+++ b/solution.py
@@ -88,35 +88,77 @@
     return mul(a[0], b[0]) + (mul(a[0], b[1]) + mul(a[1], b[0]))
 
 
-def enter_kernel(where, noise, table, amp, head, rech, sent, amp_sent, amp_dc, below, above):
-    ga = where[0]
+def fetch(pairs, sems):
+    copies = [pltpu.make_async_copy(src, dst, sems.at[i]) for i, (src, dst) in enumerate(pairs)]
+    for copy in copies:
+        copy.start()
+    return copies
+
+
+def enter_kernel(noise, table, sent, noise_in, table_in, rows_out, sems):
+    pairs = [(table, table_in), (noise.at[0:256, :], noise_in.at[0:256, :]),
+             (noise.at[256:512, :], noise_in.at[256:512, :])]
+    copies = fetch(pairs, sems)
+    copies[0].wait()
     for part in range(2):
-        rows = split(noise[256 * part : 256 * part + 256, :])
+        copies[1 + part].wait()
+        rows = split(noise_in[256 * part : 256 * part + 256, :])
         for c in range(2):
             own = slice(256 * c, 256 * c + 256)
-            result = dot3((table[0, own, :], table[1, own, :]), rows, 1)
+            result = dot3((table_in[0, own, :], table_in[1, own, :]), rows, 1)
             for q in range(2):
-                sent[pl.ds(4 * c + 2 * part + q, DEVS, stride=8), :] = result[:, 128 * q : 128 * q + 128]
+                at = pl.ds(4 * c + 2 * part + q, DEVS, stride=8)
+                rows_out[at, :] = result[:, 128 * q : 128 * q + 128]
+    pltpu.sync_copy(rows_out, sent)
+
+
+def edges_kernel(where, amp, head, rech, amp_sent, amp_first, below, above, amp_in, head_in, rech_in, sems):
+    ga = where[0]
+    copies = fetch([(amp.at[:, 0:40, :], amp_in), (head, head_in), (rech, rech_in)], sems)
+    for copy in copies:
+        copy.wait()
     for half in range(2):
         lanes = slice(128 * half, 128 * half + 128)
-        first = amp[:, 0, lanes]
-        amp_dc[:, lanes] = first
-        middle = amp[:, 32, lanes]
-        amp_sent[0:16, lanes] = jnp.where(ga < PACKED_GA, middle, first)
+        first = amp_in[:, 0, lanes]
+        amp_first[:, lanes] = first
+        amp_sent[0:16, lanes] = jnp.where(ga < PACKED_GA, amp_in[:, 32, lanes], first)
         for b in range(1, BA):
-            amp_sent[16 * b : 16 * b + 16, lanes] = amp[:, b, lanes]
+            amp_sent[16 * b : 16 * b + 16, lanes] = amp_in[:, b, lanes]
     for out, near in ((below, (0, 1, 0)), (above, (6, 7, 7))):
-        for i, (ref, y) in enumerate(zip((head, head, rech), near)):
+        for i, (ref, y) in enumerate(zip((head_in, head_in, rech_in), near)):
             out[32 * i : 32 * i + 32, :] = ref[pl.ds(y, 32, stride=8), :]
 
 
-def middle_kernel(where, got, amp, amp_dc, y_fwd, z_fwd, z_inv, y_inv, sent, rows, lines):
+def mirror_of(value):
+    ones = []
+    for size in value.shape:
+        i = lax.broadcasted_iota(jnp.int32, (size, size), 0)
+        j = lax.broadcasted_iota(jnp.int32, (size, size), 1)
+        ones.append((((i + j) == 0) | ((i + j) == size)).astype(bf16))
+    total = None
+    for _ in range(3):
+        part = value.astype(bf16)
+        value = value - part.astype(f32)
+        part = jnp.dot(ones[0], part, preferred_element_type=f32).astype(bf16)
+        part = jnp.dot(part, ones[1], preferred_element_type=f32)
+        total = part if total is None else total + part
+    return total
+
+
+def middle_kernel(where, got, amp, amp_row0, amp_row256, y_fwd, z_fwd, z_inv, y_inv, sent,
+                  got_in, amp_in, y_fwd_in, z_fwd_in, z_inv_in, y_inv_in, row0_in, row256_in,
+                  rows, lines, amps, sems):
+    packed = where[1] == 1
+    pairs = [(got, got_in), (y_fwd, y_fwd_in), (z_fwd, z_fwd_in), (amp, amp_in), (z_inv, z_inv_in),
+             (y_inv, y_inv_in), (amp_row0, row0_in), (amp_row256, row256_in)]
+    copies = fetch(pairs, sems)
+    copies[0].wait()
     low_half = lax.broadcasted_iota(jnp.int32, (BA, 128), 1) < 64
     for c in range(2):
         for q in range(4):
             for p in range(4):
-                even = got[pl.ds(16 * p + 4 * c + q, BA, stride=64), :]
-                odd = got[pl.ds(16 * p + 8 + 4 * c + q, BA, stride=64), :]
+                even = got_in[pl.ds(16 * p + 4 * c + q, BA, stride=64), :]
+                odd = got_in[pl.ds(16 * p + 8 + 4 * c + q, BA, stride=64), :]
                 first = jnp.where(low_half, even, pltpu.roll(odd, 64, 1))
                 second = jnp.where(low_half, pltpu.roll(even, 64, 1), odd)
                 for half, value in enumerate((first, second)):
@@ -124,37 +166,54 @@
                     high, low = split(value)
                     rows[0, at, 128 * p : 128 * p + 128] = high
                     rows[1, at, 128 * p : 128 * p + 128] = low
-
-    def spectral(amp_ref, keep):
-        for part in range(2):
-            ky = slice(256 * part, 256 * part + 256)
-            data = (rows[0], rows[1])
-            by_cos = dot3((y_fwd[0, 0, ky, :], y_fwd[1, 0, ky, :]), data, 1)
-            by_sin = dot3((y_fwd[0, 1, ky, :], y_fwd[1, 1, ky, :]), data, 1)
-            real = by_cos[:, :256] + by_sin[:, 256:]
-            imag = by_cos[:, 256:] - by_sin[:, :256]
-            forward = (z_fwd[0], z_fwd[1])
-            real, imag = dot3(split(real), forward), dot3(split(imag), forward)
+    for copy in copies[1:]:
+        copy.wait()
+
+    @pl.when(packed)
+    def _():
+        held = amp_in[...]
+        mirror = mirror_of(held)
+        ky = lax.broadcasted_iota(jnp.int32, (EY, EZ), 0)
+        amps[...] = jnp.where(ky == 0, row0_in[0:1, :], jnp.where(ky < 256, mirror, held))
+        amp_in[...] = jnp.where(ky == 256, row256_in[0:1, :], jnp.where(ky < 256, held, mirror))
+
+    for part in range(2):
+        ky = slice(256 * part, 256 * part + 256)
+        data = (rows[0], rows[1])
+        by_cos = dot3((y_fwd_in[0, 0, ky, :], y_fwd_in[1, 0, ky, :]), data, 1)
+        by_sin = dot3((y_fwd_in[0, 1, ky, :], y_fwd_in[1, 1, ky, :]), data, 1)
+        real = by_cos[:, :256] + by_sin[:, 256:]
+        imag = by_cos[:, 256:] - by_sin[:, :256]
+        forward = (z_fwd_in[0], z_fwd_in[1])
+        real, imag = dot3(split(real), forward), dot3(split(imag), forward)
+        real, imag = real[:, :256] + imag[:, 256:], imag[:, :256] - real[:, 256:]
+
+        def back(amp_ref, lanes):
+            table = (z_inv_in[0], z_inv_in[1])
             scale = amp_ref[ky, :]
-            new_real = (real[:, :256] + imag[:, 256:]) * scale
-            new_imag = (imag[:, :256] - real[:, 256:]) * scale
-            back = (z_inv[0], z_inv[1])
-            real, imag = dot3(split(new_real), back), dot3(split(new_imag), back)
-            for c, value in enumerate((real[:, :128] - imag[:, 128:], imag[:, :128] + real[:, 128:])):
+            re, im = dot3(split(real * scale), table), dot3(split(imag * scale), table)
+            for c, value in enumerate((re[:, :128] - im[:, 128:], im[:, :128] + re[:, 128:])):
                 high, low = split(value)
                 at = slice(512 * c + 256 * part, 512 * c + 256 * part + 256)
-                lines[0, at, :] = high
-                lines[1, at, :] = low
-
-    spectral(amp, None)
-    sent[...] = dot3((y_inv[0], y_inv[1]), (lines[0], lines[1]))
-
-    @pl.when(where[1] == 1)
-    def _():
-        spectral(amp_dc, None)
-        other = dot3((y_inv[0], y_inv[1]), (lines[0], lines[1]))
-        odd_row = lax.broadcasted_iota(jnp.int32, (2 * AY, AZ), 0) % 2 == 1
-        sent[...] = jnp.where(odd_row, other, sent[...])
+                lines[0, at, lanes] = high
+                lines[1, at, lanes] = low
+
+        back(amp_in, slice(0, 128))
+
+        @pl.when(packed)
+        def _():
+            back(amps, slice(128, 256))
+
+        @pl.when(jnp.logical_not(packed))
+        def _():
+            for i in range(2):
+                for c in range(2):
+                    at = slice(512 * c + 256 * part, 512 * c + 256 * part + 256)
+                    lines[i, at, 128:256] = jnp.zeros((256, 128), bf16)
+
+    result = dot3((y_inv_in[0], y_inv_in[1]), (lines[0], lines[1]))
+    odd_row = lax.broadcasted_iota(jnp.int32, (2 * AY, AZ), 0) % 2 == 1
+    sent[...] = jnp.where(odd_row & packed, result[:, 128:], result[:, :128])
 
 
 def field_kernel(where, got, table, head, rech, lo_halo, hi_halo, sent):
@@ -243,14 +302,21 @@
         press_out[pl.ds(y, 32, stride=8), :] = staged[4:36, :]
 
 
-def kernel_call(kernel, outs, inputs, scratch=()):
+def kernel_call(kernel, outs, inputs, scratch=(), held=(), outs_held=()):
     vmem = pl.BlockSpec(memory_space=pltpu.VMEM)
     smem = pl.BlockSpec(memory_space=pltpu.SMEM)
+    there = pl.BlockSpec(memory_space=pl.ANY)
+
+    def spec(i, value):
+        if value.dtype == jnp.int32:
+            return smem
+        return there if i in held else vmem
+
     return pl.pallas_call(
         kernel,
         out_shape=[jax.ShapeDtypeStruct(shape, f32) for shape in outs],
-        in_specs=[smem] + [vmem] * (len(inputs) - 1),
-        out_specs=[vmem] * len(outs),
+        in_specs=[spec(i, value) for i, value in enumerate(inputs)],
+        out_specs=[there if i in outs_held else vmem for i in range(len(outs))],
         scratch_shapes=list(scratch),
         compiler_params=pltpu.CompilerParams(vmem_limit_bytes=VMEM),
     )(*inputs)
@@ -261,25 +327,35 @@
     ga, ba = lax.axis_index("ga"), lax.axis_index("ba")
     packed = ((ga == PACKED_GA) & (ba == 0)).astype(jnp.int32)
     where = jnp.stack([ga.astype(jnp.int32), packed, ba.astype(jnp.int32)])
-    noise = noise.reshape(512, EX)
     recharge = recharge.reshape(256, AZ)
     head = head_guess.reshape(256, AZ)
-    sent, amp_sent, amp_dc, below, above = kernel_call(
-        enter_kernel, [(8 * DEVS, 128), (512, EZ), (16, EZ), (96, AZ), (96, AZ)],
-        [where, noise, x_fwd, amplitude, head, recharge],
+    memory, sems = pltpu.VMEM, pltpu.SemaphoreType.DMA
+    (sent,) = kernel_call(
+        enter_kernel, [(8 * DEVS, 128)], [noise.reshape(512, EX), x_fwd],
+        [memory((512, EX), f32), memory(x_fwd.shape, bf16), memory((8 * DEVS, 128), f32), sems((3,))],
+        held=(0, 1), outs_held=(0,),
+    )
+    got = lax.all_to_all(sent, ("ba", "ga"), 0, 0, tiled=True)
+    amp_sent, amp_first, below, above = kernel_call(
+        edges_kernel, [(512, EZ), (16, EZ), (96, AZ), (96, AZ)], [where, amplitude, head, recharge],
+        [memory((16, 40, EZ), f32), memory((256, AZ), f32), memory((256, AZ), f32), sems((3,))],
+        held=(1, 2, 3),
     )
     up = [(i, i + 1) for i in range(BA - 1)]
     down = [(j, i) for i, j in up]
     hi_halo = lax.ppermute(below, "ba", down)
     lo_halo = lax.ppermute(above, "ba", up)
-    amp_dc = lax.ppermute(amp_dc, "ga", [(0, PACKED_GA)])
-    amp_dc = lax.all_gather(amp_dc, "ba", axis=0, tiled=True)
+    amp_zero = lax.ppermute(amp_first, "ga", [(0, PACKED_GA)])
+    amp_row = lax.ppermute(amp_first, "ba", [(BA // 2, 0)])
+    swap = (ga == PACKED_GA) & (ba >= BA // 2)
+    amp_sent = amp_sent.at[:16].set(jnp.where(swap, amp_zero, amp_sent[:16]))
     amp_got = lax.all_to_all(amp_sent, "ba", 0, 0, tiled=True)
-    got = lax.all_to_all(sent, ("ba", "ga"), 0, 0, tiled=True)
+    inputs = [where, got, amp_got, amp_zero, amp_row, y_fwd, z_fwd, z_inv, y_inv]
     (sent,) = kernel_call(
-        middle_kernel, [(2 * AY, AZ)],
-        [where, got, amp_got, amp_dc, y_fwd, z_fwd, z_inv, y_inv],
-        [pltpu.VMEM((2, 512, 512), bf16), pltpu.VMEM((2, 1024, AZ), bf16)],
+        middle_kernel, [(2 * AY, AZ)], inputs,
+        [memory(value.shape, value.dtype) for value in (got, amp_got, y_fwd, z_fwd, z_inv, y_inv, amp_zero, amp_row)]
+        + [memory((2, 512, 512), bf16), memory((2, 1024, 2 * AZ), bf16), memory((EY, EZ), f32), sems((8,))],
+        held=range(1, 9),
     )
     got = lax.all_to_all(sent, ("ba", "ga"), 0, 0, tiled=True)
     (sent,) = kernel_call(

time: 276 us -> 154 us (0.56)
  the two profiles are of different devices: /device:TPU:1 before, /device:TPU:24 now
where the time goes in v2:
time: 154 us; the launch traced here: 153 us
  starting transfers between devices  56.5 us (37%)
  waiting for transfers between devices  54.7 us (36%)
  Pallas kernels  15.9 us (10%)
  blocking collectives  12.8 us (8%)
  local copies, waits for them, and re-layouts  11.1 us (7%)
    all_to_all x2, waiting for transfers between devices, body(): got = lax.all_to_all(sent, ('ba', 'ga'), 0, 0, tiled=True)  28.6 us
    all_to_all x2, starting transfers between devices, body(): got = lax.all_to_all(sent, ('ba', 'ga'), 0, 0, tiled=True)  17.2 us
    pallas_call x5, Pallas kernels, kernel_call(): pl.pallas_call(kernel, out_shape=[jax.ShapeDtypeStruct(shape, f32) for sh...  15.9 us
    all_to_all x1, blocking collectives, body(): got = lax.all_to_all(sent, 'ga', 0, 0, tiled=True)  12.8 us
    all_to_all x1, starting transfers between devices, body(): amp_got = lax.all_to_all(amp_sent, 'ba', 0, 0, tiled=True)  12.1 us
    unnamed x28, local copies, waits for them, and re-layouts  11.1 us
    all_to_all x1, waiting for transfers between devices, body(): amp_got = lax.all_to_all(amp_sent, 'ba', 0, 0, tiled=True)  9.13 us
    ppermute x1, starting transfers between devices, body(): lo_halo = lax.ppermute(above, 'ba', up)  8.36 us
  transfers between devices with their start and end apart: 9, of which 7 were waited for; matrix products, arithmetic and copies ran while one was open for 0% of the time, Pallas kernels for 2%

profile of v2, /device:TPU:24, one launch (start us, length us, event | category | flops | bytes accessed | tf_op | source)
XLA Modules:
  0.0 153.3 jit_solution(7119780111923729089)
XLA Ops:
  0.7 0.9 copy-done.3
  1.6 0.9 copy-done.5
  2.5 1.2 copy-done.10
  3.8 2.0 %shard_map.114 = (f32[512,256]{1,0:T(8,128)}, f32[16,256]{1,0:T(8,128)S(1)}, f32[96,128]{1,0:T(8,128)S(1)}, f32[96,128]{1,0:T(8,128)S(1)}) custom-call(s32[3]{0:T(128)S(1)} %pad_add_fusion.where, f32[16,64,256]{2,1,0:T(8,128)S(1)} %copy-done.10, f32[256,128]{1,0:T(8,128)S(1)} %bitcast.21, f32[256,128]{1,0:T(8,128)S(1)} %bitcast.24), custom_call_target="tpu_custom_call" | custom-call | tf_op jit(solution)/shard_map/pallas_call | solution.py:315
  5.7 5.2 %collective-permute-start = (f32[16,256]{1,0:T(8,128)S(1)}, f32[16,256]{1,0:T(8,128)S(1)}, u32[]{:S(2)}, u32[]{:S(2)}) collective-permute-start(f32[16,256]{1,0:T(8,128)S(1)} %get-tuple-element.21), channel_id=1, source_target_pairs={{0,128},{1,129},{2,130},{3,131},{4,132},{5,133},{6,134},{7,135},{8... | collective-permute-start | bytes 49160 | tf_op jit(solution)/shard_map/ppermute | solution.py:348
  10.9 1.4 collective-permute-done.amp_row0
  12.3 1.3 select_dynamic-update-slice_fusion
  13.7 12.1 %all-to-all-start.1 = ((f32[32,16,256]{2,1,0:T(8,128)}), f32[32,16,256]{2,1,0:T(8,128)S(1)}, u32[]{:S(2)}, u32[]{:S(2)}) async-start(f32[32,16,256]{2,1,0:T(8,128)} %bitcast.8), calls=%async_computation.1 | async-start | bytes 1048576 | tf_op jit(solution)/shard_map/all_to_all | solution.py:352
  25.8 1.2 copy-done.7
  27.0 1.2 copy-done.8
  28.3 2.5 %shard_map.113 = f32[2048,128]{1,0:T(8,128)} custom-call(f32[512,512]{1,0:T(8,128)S(1)} %bitcast.28, bf16[2,512,512]{2,1,0:T(8,128)(2,1)S(1)} %copy-done.8), custom_call_target="tpu_custom_call" | custom-call | tf_op jit(solution)/shard_map/pallas_call | solution.py:315
  30.7 9.1 %all-to-all-done.1 = f32[32,16,256]{2,1,0:T(8,128)S(1)} async-done(((f32[32,16,256]{2,1,0:T(8,128)}), f32[32,16,256]{2,1,0:T(8,128)S(1)}, u32[]{:S(2)}, u32[]{:S(2)}) %all-to-all-start.1) | async-done | bytes 524320 | tf_op jit(solution)/shard_map/all_to_all | solution.py:352
  39.9 0.8 copy-done.1
  40.7 9.3 %all-to-all-start = ((f32[256,8,128]{2,1,0:T(8,128)}), f32[256,8,128]{2,1,0:T(8,128)S(1)}, u32[]{:S(2)}, u32[]{:S(2)}) async-start(f32[256,8,128]{2,1,0:T(8,128)} %bitcast.4), calls=%async_computation | async-start | bytes 2097152 | tf_op jit(solution)/shard_map/all_to_all | solution.py:338
  50.7 28.6 %all-to-all-done = f32[256,8,128]{2,1,0:T(8,128)S(1)} async-done(((f32[256,8,128]{2,1,0:T(8,128)}), f32[256,8,128]{2,1,0:T(8,128)S(1)}, u32[]{:S(2)}, u32[]{:S(2)}) %all-to-all-start) | async-done | bytes 1048608 | tf_op jit(solution)/shard_map/all_to_all | solution.py:338
  79.3 1.0 copy-done.2
  80.3 1.0 copy-done.12
  81.4 0.9 copy-done.13
  82.3 8.6 %shard_map.115 = f32[512,128]{1,0:T(8,128)S(1)} custom-call(s32[3]{0:T(128)S(1)} %pad_add_fusion.where, f32[2048,128]{1,0:T(8,128)S(1)} %bitcast.18, f32[512,256]{1,0:T(8,128)S(1)} %bitcast.19, f32[16,256]{1,0:T(8,128)S(1)} %collective-permute-done.amp_row0, f32[16,256]{1,0:T(8,128)S(1)} %collective-permute-done.1.amp_row256, ...), custom_call_target="tpu_custom_call" | custom-call | tf_op jit(solution)/shard_map/pallas_call | solution.py:315
  91.7 7.9 %all-to-all-start.2 = ((f32[256,2,128]{2,1,0:T(2,128)}), f32[256,2,128]{2,1,0:T(2,128)S(1)}, u32[]{:S(2)}, u32[]{:S(2)}) async-start(f32[256,2,128]{2,1,0:T(2,128)} %bitcast.29), calls=%async_computation.2 | async-start | bytes 524288 | tf_op jit(solution)/shard_map/all_to_all | solution.py:360
  99.6 8.4 %collective-permute-start.2 = (f32[96,128]{1,0:T(8,128)S(1)}, f32[96,128]{1,0:T(8,128)S(1)}, u32[]{:S(2)}, u32[]{:S(2)}) collective-permute-start(f32[96,128]{1,0:T(8,128)S(1)} %get-tuple-element.22), channel_id=1, source_target_pairs={{0,1},{1,2},{2,3},{3,4},{4,5},{5,6},{6,7},{7,8},{8,9},{9,10},{10,1... | collective-permute-start | bytes 147464 | tf_op jit(solution)/shard_map/ppermute | solution.py:347
  107.9 2.3 %collective-permute-start.3 = (f32[96,128]{1,0:T(8,128)S(1)}, f32[96,128]{1,0:T(8,128)S(1)}, u32[]{:S(2)}, u32[]{:S(2)}) collective-permute-start(f32[96,128]{1,0:T(8,128)S(1)} %get-tuple-element.23), channel_id=1, source_target_pairs={{1,0},{2,1},{3,2},{4,3},{5,4},{6,5},{7,6},{8,7},{9,8},{10,9},{11,1... | collective-permute-start | bytes 147464 | tf_op jit(solution)/shard_map/ppermute | solution.py:346
  110.2 1.9 %collective-permute-done.2.lo_halo = f32[96,128]{1,0:T(8,128)S(1)} collective-permute-done((f32[96,128]{1,0:T(8,128)S(1)}, f32[96,128]{1,0:T(8,128)S(1)}, u32[]{:S(2)}, u32[]{:S(2)}) %collective-permute-start.2) | collective-permute-done | bytes 49184 | tf_op jit(solution)/shard_map/ppermute | solution.py:347
  112.1 6.3 %collective-permute-done.3.hi_halo = f32[96,128]{1,0:T(8,128)S(1)} collective-permute-done((f32[96,128]{1,0:T(8,128)S(1)}, f32[96,128]{1,0:T(8,128)S(1)}, u32[]{:S(2)}, u32[]{:S(2)}) %collective-permute-start.3) | collective-permute-done | bytes 49184 | tf_op jit(solution)/shard_map/ppermute | solution.py:346
  118.5 1.1 copy-done.11
  119.5 1.0 shard_map.116
  120.5 12.8 %all_to_all.44 = f32[8,72,128]{2,1,0:T(8,128)S(1)} all-to-all(f32[8,72,128]{2,1,0:T(8,128)S(1)} %bitcast.27), channel_id=1, replica_groups=mesh['ga'=8,'ba'=32] {'ga'}, dimensions={0} | all-to-all | bytes 589824 | tf_op jit(solution)/shard_map/all_to_all | solution.py:364
  133.3 7.4 %collective-permute-start.4 = (f32[144,128]{1,0:T(8,128)S(1)}, f32[144,128]{1,0:T(8,128)S(1)}, u32[]{:S(2)}, u32[]{:S(2)}) collective-permute-start(f32[144,128]{1,0:T(8,128)S(1)} %bitcast.32), channel_id=1, source_target_pairs={{0,1},{1,2},{2,3},{3,4},{4,5},{5,6},{6,7},{7,8},{8,9},{9,10},{10,1... | collective-permute-start | bytes 221192 | tf_op jit(solution)/shard_map/ppermute | solution.py:365
  140.8 3.2 %collective-permute-start.5 = (f32[144,128]{1,0:T(8,128)S(1)}, f32[144,128]{1,0:T(8,128)S(1)}, u32[]{:S(2)}, u32[]{:S(2)}) collective-permute-start(f32[144,128]{1,0:T(8,128)S(1)} %bitcast.31), channel_id=1, source_target_pairs={{1,0},{2,1},{3,2},{4,3},{5,4},{6,5},{7,6},{8,7},{9,8},{10,9},{11,1... | collective-permute-start | bytes 221192 | tf_op jit(solution)/shard_map/ppermute | solution.py:366
  144.0 1.5 collective-permute-done.4.lo_cond
  145.5 5.9 %collective-permute-done.5.hi_cond = f32[144,128]{1,0:T(8,128)S(1)} collective-permute-done((f32[144,128]{1,0:T(8,128)S(1)}, f32[144,128]{1,0:T(8,128)S(1)}, u32[]{:S(2)}, u32[]{:S(2)}) %collective-permute-start.5) | collective-permute-done | bytes 73760 | tf_op jit(solution)/shard_map/ppermute | solution.py:366
  151.4 1.9 %shard_map.117 = (f32[256,128]{1,0:T(8,128)}, f32[256,128]{1,0:T(8,128)}) custom-call(s32[3]{0:T(128)S(1)} %pad_add_fusion.where, f32[576,128]{1,0:T(8,128)S(1)} %bitcast.20, f32[144,128]{1,0:T(8,128)S(1)} %collective-permute-done.4.lo_cond, f32[144,128]{1,0:T(8,128)S(1)} %collective-permute-done.5.hi_cond, f32[256,128]{1,0:T(8,128)S(1)} %bitcast.23, ...), custom_call_target="tpu_custom_call" | custom-call | tf_op jit(solution)/shard_map/pallas_call | solution.py:315
  (23 shorter events, 1.5 us)
Async XLA Ops:
  0.7 0.9 copy-start.3
  1.6 0.9 copy-start.5
  2.5 1.2 copy-start.10
  5.7 6.6 %collective-permute-start = (f32[16,256]{1,0:T(8,128)S(1)}, f32[16,256]{1,0:T(8,128)S(1)}, u32[]{:S(2)}, u32[]{:S(2)}) collective-permute-start(f32[16,256]{1,0:T(8,128)S(1)} %get-tuple-element.21), channel_id=1, source_target_pairs={{0,128},{1,129},{2,130},{3,131},{4,132},{5,133},{6,134},{7,135},{8... | collective-permute-start | bytes 49160 | tf_op jit(solution)/shard_map/ppermute | solution.py:348
  13.7 26.2 %all-to-all-start.1 = ((f32[32,16,256]{2,1,0:T(8,128)}), f32[32,16,256]{2,1,0:T(8,128)S(1)}, u32[]{:S(2)}, u32[]{:S(2)}) async-start(f32[32,16,256]{2,1,0:T(8,128)} %bitcast.8), calls=%async_computation.1 | async-start | bytes 1048576 | tf_op jit(solution)/shard_map/all_to_all | solution.py:352
  25.8 1.2 copy-start.7
  27.0 1.2 copy-start.8
  28.3 51.0 %copy-start = (bf16[2,2,512,512]{3,2,1,0:T(8,128)(2,1)S(1)}, bf16[2,2,512,512]{3,2,1,0:T(8,128)(2,1)}, u32[]{:S(2)}) copy-start(bf16[2,2,512,512]{3,2,1,0:T(8,128)(2,1)} %constant.55.clone.y_fwd) | copy-start | bytes 6291460
  39.9 0.8 copy-start.1
  40.7 38.6 %all-to-all-start = ((f32[256,8,128]{2,1,0:T(8,128)}), f32[256,8,128]{2,1,0:T(8,128)S(1)}, u32[]{:S(2)}, u32[]{:S(2)}) async-start(f32[256,8,128]{2,1,0:T(8,128)} %bitcast.4), calls=%async_computation | async-start | bytes 2097152 | tf_op jit(solution)/shard_map/all_to_all | solution.py:338
  50.0 0.7 collective-permute-start.1
  79.3 1.0 copy-start.2
  80.3 1.0 copy-start.12
  81.4 0.9 copy-start.13
  82.3 36.1 %copy-start.4 = (f32[32,8,128]{2,1,0:T(8,128)S(1)}, f32[32,8,128]{2,1,0:T(8,128)}, u32[]{:S(2)}) copy-start(f32[32,8,128]{2,1,0:T(8,128)} %param.15) | copy-start | bytes 393220
  82.3 36.1 %copy-start.6 = (f32[32,8,128]{2,1,0:T(8,128)S(1)}, f32[32,8,128]{2,1,0:T(8,128)}, u32[]{:S(2)}) copy-start(f32[32,8,128]{2,1,0:T(8,128)} %param.14) | copy-start | bytes 393220
  91.0 0.7 copy-start.9
  91.7 26.8 %all-to-all-start.2 = ((f32[256,2,128]{2,1,0:T(2,128)}), f32[256,2,128]{2,1,0:T(2,128)S(1)}, u32[]{:S(2)}, u32[]{:S(2)}) async-start(f32[256,2,128]{2,1,0:T(2,128)} %bitcast.29), calls=%async_computation.2 | async-start | bytes 524288 | tf_op jit(solution)/shard_map/all_to_all | solution.py:360
  99.6 12.5 %collective-permute-start.2 = (f32[96,128]{1,0:T(8,128)S(1)}, f32[96,128]{1,0:T(8,128)S(1)}, u32[]{:S(2)}, u32[]{:S(2)}) collective-permute-start(f32[96,128]{1,0:T(8,128)S(1)} %get-tuple-element.22), channel_id=1, source_target_pairs={{0,1},{1,2},{2,3},{3,4},{4,5},{5,6},{6,7},{7,8},{8,9},{9,10},{10,1... | collective-permute-start | bytes 147464 | tf_op jit(solution)/shard_map/ppermute | solution.py:347
  107.9 10.5 %collective-permute-start.3 = (f32[96,128]{1,0:T(8,128)S(1)}, f32[96,128]{1,0:T(8,128)S(1)}, u32[]{:S(2)}, u32[]{:S(2)}) collective-permute-start(f32[96,128]{1,0:T(8,128)S(1)} %get-tuple-element.23), channel_id=1, source_target_pairs={{1,0},{2,1},{3,2},{4,3},{5,4},{6,5},{7,6},{8,7},{9,8},{10,9},{11,1... | collective-permute-start | bytes 147464 | tf_op jit(solution)/shard_map/ppermute | solution.py:346
  118.5 1.1 copy-start.11
  133.3 12.1 %collective-permute-start.4 = (f32[144,128]{1,0:T(8,128)S(1)}, f32[144,128]{1,0:T(8,128)S(1)}, u32[]{:S(2)}, u32[]{:S(2)}) collective-permute-start(f32[144,128]{1,0:T(8,128)S(1)} %bitcast.32), channel_id=1, source_target_pairs={{0,1},{1,2},{2,3},{3,4},{4,5},{5,6},{6,7},{7,8},{8,9},{9,10},{10,1... | collective-permute-start | bytes 221192 | tf_op jit(solution)/shard_map/ppermute | solution.py:365
  140.8 10.6 %collective-permute-start.5 = (f32[144,128]{1,0:T(8,128)S(1)}, f32[144,128]{1,0:T(8,128)S(1)}, u32[]{:S(2)}, u32[]{:S(2)}) collective-permute-start(f32[144,128]{1,0:T(8,128)S(1)} %bitcast.31), channel_id=1, source_target_pairs={{1,0},{2,1},{3,2},{4,3},{5,4},{6,5},{7,6},{8,7},{9,8},{10,9},{11,1... | collective-permute-start | bytes 221192 | tf_op jit(solution)/shard_map/ppermute | solution.py:366

commit v3 on v2

--- a/solution.py
+++ b/solution.py
@@ -16,8 +16,8 @@
 DEVS = GA * BA
 PACKED_GA = 4
 XROWS = 40
-CHUNK = XROWS + 32
-VMEM = 48 * 2**20
+CHUNK = 2 * XROWS
+VMEM = 60 * 2**20
 f32, bf16 = jnp.float32, jnp.bfloat16
 
 
@@ -65,7 +65,7 @@
 
     cos, sin = trig(np.arange(AY), np.arange(EY), EY)
     y_inv = np.concatenate(
-        [np.stack([cos, sin], 1).reshape(2 * AY, EY), np.stack([-sin, cos], 1).reshape(2 * AY, EY)], 1
+        [np.concatenate([cos, sin]), np.concatenate([-sin, cos])], 1
     )
 
     xs = np.clip((32 * np.arange(GA)[:, None] - 4 + np.arange(XROWS)).reshape(-1), 0, AX - 1)
@@ -73,7 +73,7 @@
     back_re, back_im = 2.0 * cos, -2.0 * sin
     back_re[:, packed] = alternating[xs][:, None]
     back_im[:, packed] = 1.0
-    x_inv = np.stack([back_re, back_im], 2).reshape(xs.size, 2 * DEVS) / (EX * EY * EZ)
+    x_inv = np.concatenate([back_re, back_im], 1) / (EX * EY * EZ)
     return tuple(split_np(t) for t in (x_fwd, y_fwd, z_fwd, z_inv, y_inv, x_inv))
 
 
@@ -145,7 +145,7 @@
     return total
 
 
-def middle_kernel(where, got, amp, amp_row0, amp_row256, y_fwd, z_fwd, z_inv, y_inv, sent,
+def middle_kernel(where, got, amp, amp_row0, amp_row256, y_fwd, z_fwd, z_inv, y_inv, up, down, sent,
                   got_in, amp_in, y_fwd_in, z_fwd_in, z_inv_in, y_inv_in, row0_in, row256_in,
                   rows, lines, amps, sems):
     packed = where[1] == 1
@@ -166,8 +166,9 @@
                     high, low = split(value)
                     rows[0, at, 128 * p : 128 * p + 128] = high
                     rows[1, at, 128 * p : 128 * p + 128] = low
-    for copy in copies[1:]:
-        copy.wait()
+    copies[3].wait()
+    copies[6].wait()
+    copies[7].wait()
 
     @pl.when(packed)
     def _():
@@ -180,10 +181,15 @@
     for part in range(2):
         ky = slice(256 * part, 256 * part + 256)
         data = (rows[0], rows[1])
+        if part == 0:
+            copies[1].wait()
         by_cos = dot3((y_fwd_in[0, 0, ky, :], y_fwd_in[1, 0, ky, :]), data, 1)
         by_sin = dot3((y_fwd_in[0, 1, ky, :], y_fwd_in[1, 1, ky, :]), data, 1)
         real = by_cos[:, :256] + by_sin[:, 256:]
         imag = by_cos[:, 256:] - by_sin[:, :256]
+        if part == 0:
+            copies[2].wait()
+            copies[4].wait()
         forward = (z_fwd_in[0], z_fwd_in[1])
         real, imag = dot3(split(real), forward), dot3(split(imag), forward)
         real, imag = real[:, :256] + imag[:, 256:], imag[:, :256] - real[:, 256:]
@@ -211,36 +217,46 @@
                     at = slice(512 * c + 256 * part, 512 * c + 256 * part + 256)
                     lines[i, at, 128:256] = jnp.zeros((256, 128), bf16)
 
+    copies[5].wait()
     result = dot3((y_inv_in[0], y_inv_in[1]), (lines[0], lines[1]))
-    odd_row = lax.broadcasted_iota(jnp.int32, (2 * AY, AZ), 0) % 2 == 1
-    sent[...] = jnp.where(odd_row & packed, result[:, 128:], result[:, :128])
-
-
-def field_kernel(where, got, table, head, rech, lo_halo, hi_halo, sent):
-    ga = where[0]
-    log_field = dot3((table[0], table[1]), split(got[...]))
+    forward_halo = lax.broadcasted_iota(jnp.int32, (AY, AZ), 0) % GA < GA // 2
+    for c in range(2):
+        own = result[AY * c : AY * c + AY, :AZ]
+        if c == 1:
+            own = jnp.where(packed, result[AY:, AZ:], own)
+        after = jnp.concatenate([own[GA:], own[:GA]], 0)
+        before = jnp.concatenate([own[AY - GA :], own[: AY - GA]], 0)
+        sent[pl.ds(c, AY, stride=4), :] = own
+        sent[pl.ds(2 + c, AY, stride=4), :] = jnp.where(forward_halo, after, before)
+
+
+def pack_kernel(head, rech, lo_halo, hi_halo, up, down):
+    corner = lax.broadcasted_iota(jnp.int32, (8, AZ), 0)
+    for out, far, near in ((up, 30, 31), (down, 1, 0)):
+        out[0:8, :] = head[8 * far : 8 * far + 8, :]
+        out[8:16, :] = head[8 * near : 8 * near + 8, :]
+        out[16:24, :] = rech[8 * near : 8 * near + 8, :]
+        before, after = lo_halo[32 + near : 33 + near, :], hi_halo[near : near + 1, :]
+        out[24:32, :] = jnp.where(corner == 0, before, after)
+
+
+def field_kernel(where, got, table, lo_x, hi_x, sent):
+    ga, ba = where[0], where[2]
+    own = jnp.concatenate([got[pl.ds(c, DEVS, stride=4), :] for c in range(2)], 0)
+    halo = jnp.concatenate([got[pl.ds(2 + c, DEVS, stride=4), :] for c in range(2)], 0)
+    log_field = dot3((table[0], table[1]), split(jnp.concatenate([own, halo], 1)))
     row = lax.broadcasted_iota(jnp.int32, (XROWS, AZ), 0)
-    corner = lax.broadcasted_iota(jnp.int32, (8, AZ), 0)
-
-    def pack(far, near):
-        edges = jnp.where(
-            corner == 0, lo_halo[32 + near : 33 + near, :], hi_halo[near : near + 1, :]
-        )
-        return (head[8 * far : 8 * far + 8, :], head[8 * near : 8 * near + 8, :],
-                rech[8 * near : 8 * near + 8, :], edges)
-
-    up, down = pack(30, 31), pack(1, 0)
+    halo_inside = jnp.where(ga < GA // 2, ba < BA - 1, ba > 0)
     for g in range(GA):
         x = row + (32 * g - 4)
         inside = (x >= 0) & (x < AX)
         value = jnp.exp(log_field[XROWS * g : XROWS * g + XROWS, :])
-        sent[CHUNK * g : CHUNK * g + XROWS, :] = jnp.where(inside, value, 0.0)
-        for i in range(4):
-            at = CHUNK * g + XROWS + 8 * i
-            sent[at : at + 8, :] = jnp.where(ga + 1 == g, up[i], down[i])
-
-
-def sweep_kernel(where, got, lo_cond, hi_cond, head, rech, lo_halo, hi_halo, cond_out, press_out,
+        sent[CHUNK * g : CHUNK * g + XROWS, :] = jnp.where(inside, value[:, :AZ], 0.0)
+        beside = jnp.where(inside & halo_inside, value[:, AZ:], 0.0)
+        sent[CHUNK * g + XROWS : CHUNK * g + CHUNK, :] = beside
+
+
+def sweep_kernel(where, got, head, rech, lo_halo, hi_halo, lo_x, hi_x, cond_out, press_out,
                  head_ext, rech_ext, staged):
     ga, ba = where[0], where[2]
     head_ext[...] = jnp.zeros_like(head_ext)
@@ -252,11 +268,7 @@
     for halo, (first, second, only) in ((lo_halo, (0, 1, 1)), (hi_halo, (10, 11, 10))):
         for ref, y, i in ((head_ext, first, 0), (head_ext, second, 1), (rech_ext, only, 2)):
             ref[XROWS * y + 4 : XROWS * y + 36, :] = halo[32 * i : 32 * i + 32, :]
-    for side, peer, present, far, near in (
-        (0, jnp.maximum(ga - 1, 0), ga > 0, 2, 3), (1, jnp.minimum(ga + 1, GA - 1), ga < GA - 1, 37, 36)
-    ):
-        block = got[pl.ds(pl.multiple_of(peer * CHUNK + XROWS, 8), 32), :]
-        block = jnp.where(present, block, 0.0)
+    for block, far, near in ((lo_x, 2, 3), (hi_x, 37, 36)):
         for y in range(8):
             at = XROWS * (y + 2)
             head_ext[at + far : at + far + 1, :] = block[y : y + 1, :]
@@ -275,9 +287,10 @@
         total = total + jnp.where(lane > 0, pltpu.roll(value, 1, 1), 0.0)
         return total + jnp.where(lane < AZ - 1, pltpu.roll(value, AZ - 1, 1), 0.0)
 
-    cond = [lo_cond[0:XROWS, :], lo_cond[CHUNK : CHUNK + XROWS, :]]
+    beside = {y: got[CHUNK * y + XROWS : CHUNK * y + CHUNK, :] for y in (0, 1, 6, 7)}
+    cond = [beside[6], beside[7]]
     cond += [got[CHUNK * y : CHUNK * y + XROWS, :] for y in range(8)]
-    cond += [hi_cond[0:XROWS, :], hi_cond[CHUNK : CHUNK + XROWS, :]]
+    cond += [beside[0], beside[1]]
     planes = [head_ext[XROWS * y : XROWS * y + XROWS, :] for y in range(12)]
     weight = {y: 6.0 * cond[y] + (in_plane(cond[y]) + (cond[y - 1] + cond[y + 1])) for y in range(1, 11)}
     source = {y: 2.0 * rech_ext[XROWS * y : XROWS * y + XROWS, :] for y in range(1, 11)}
@@ -350,24 +363,23 @@
     swap = (ga == PACKED_GA) & (ba >= BA // 2)
     amp_sent = amp_sent.at[:16].set(jnp.where(swap, amp_zero, amp_sent[:16]))
     amp_got = lax.all_to_all(amp_sent, "ba", 0, 0, tiled=True)
-    inputs = [where, got, amp_got, amp_zero, amp_row, y_fwd, z_fwd, z_inv, y_inv]
+    to_up, to_down = kernel_call(pack_kernel, [(32, AZ), (32, AZ)], [head, recharge, lo_halo, hi_halo])
+    inputs = [where, got, amp_got, amp_zero, amp_row, y_fwd, z_fwd, z_inv, y_inv, to_up, to_down]
     (sent,) = kernel_call(
-        middle_kernel, [(2 * AY, AZ)], inputs,
+        middle_kernel, [(4 * AY, AZ)], inputs,
         [memory(value.shape, value.dtype) for value in (got, amp_got, y_fwd, z_fwd, z_inv, y_inv, amp_zero, amp_row)]
         + [memory((2, 512, 512), bf16), memory((2, 1024, 2 * AZ), bf16), memory((EY, EZ), f32), sems((8,))],
-        held=range(1, 9),
+        held=range(1, 11),
     )
     got = lax.all_to_all(sent, ("ba", "ga"), 0, 0, tiled=True)
-    (sent,) = kernel_call(
-        field_kernel, [(CHUNK * GA, AZ)], [where, got, x_inv, head, recharge, lo_halo, hi_halo]
-    )
+    lo_x = lax.ppermute(to_up, "ga", [(i, i + 1) for i in range(GA - 1)])
+    hi_x = lax.ppermute(to_down, "ga", [(i + 1, i) for i in range(GA - 1)])
+    (sent,) = kernel_call(field_kernel, [(CHUNK * GA, AZ)], [where, got, x_inv, lo_x, hi_x], held=(3, 4))
     got = lax.all_to_all(sent, "ga", 0, 0, tiled=True)
-    lo_cond = lax.ppermute(got[6 * CHUNK :], "ba", up)
-    hi_cond = lax.ppermute(got[: 2 * CHUNK], "ba", down)
     ext = pltpu.VMEM((12 * XROWS, AZ), f32)
     conductivity, pressure = kernel_call(
         sweep_kernel, [(256, AZ), (256, AZ)],
-        [where, got, lo_cond, hi_cond, head, recharge, lo_halo, hi_halo],
+        [where, got, head, recharge, lo_halo, hi_halo, lo_x, hi_x],
         [ext, ext, pltpu.VMEM((XROWS, AZ), f32)],
     )
     return conductivity.reshape(32, 8, AZ), pressure.reshape(32, 8, AZ)

time: 154 us -> 146 us (0.948)
  the two profiles are of different devices: /device:TPU:24 before, /device:TPU:1 now
where the time goes in v3:
time: 146 us; the launch traced here: 145 us
  starting transfers between devices  55.5 us (38%)
  waiting for transfers between devices  46.3 us (32%)
  Pallas kernels  23.6 us (16%)
  blocking collectives  14.8 us (10%)
  local copies, waits for them, and re-layouts  2.46 us (2%)
  other arithmetic  1.99 us (1%)
    all_to_all x2, starting transfers between devices, body(): got = lax.all_to_all(sent, ('ba', 'ga'), 0, 0, tiled=True)  24 us
    pallas_call x6, Pallas kernels, kernel_call(): pl.pallas_call(kernel, out_shape=[jax.ShapeDtypeStruct(shape, f32) for sh...  23.6 us
    ppermute x1, waiting for transfers between devices, body(): hi_halo = lax.ppermute(below, 'ba', down)  15.7 us
    all_to_all x1, blocking collectives, body(): got = lax.all_to_all(sent, 'ga', 0, 0, tiled=True)  14.8 us
    all_to_all x1, starting transfers between devices, body(): amp_got = lax.all_to_all(amp_sent, 'ba', 0, 0, tiled=True)  14.5 us
    all_to_all x1, waiting for transfers between devices, body(): amp_got = lax.all_to_all(amp_sent, 'ba', 0, 0, tiled=True)  10.2 us
    all_to_all x2, waiting for transfers between devices, body(): got = lax.all_to_all(sent, ('ba', 'ga'), 0, 0, tiled=True)  9.02 us
    ppermute x1, starting transfers between devices, body(): lo_halo = lax.ppermute(above, 'ba', up)  8.13 us
  transfers between devices with their start and end apart: 9, of which 5 were waited for; matrix products, arithmetic and copies ran while one was open for 0% of the time, Pallas kernels for 4%

profile of v3, /device:TPU:1, one launch (start us, length us, event | category | flops | bytes accessed | tf_op | source)
XLA Modules:
  0.0 145.5 jit_solution(16632410162721435275)
XLA Ops:
  0.6 0.7 pad_add_fusion.where
  1.3 2.8 %shard_map.114 = (f32[512,256]{1,0:T(8,128)}, f32[16,256]{1,0:T(8,128)}, f32[96,128]{1,0:T(8,128)}, f32[96,128]{1,0:T(8,128)}) custom-call(s32[3]{0:T(128)} %pad_add_fusion.where, f32[16,64,256]{2,1,0:T(8,128)} %amp.1, f32[256,128]{1,0:T(8,128)} %bitcast.23, f32[256,128]{1,0:T(8,128)} %bitcast.26), custom_call_target="tpu_custom_call" | custom-call | tf_op jit(solution)/shard_map/pallas_call | solution.py:328
  4.2 0.7 collective-permute-start
  4.8 0.0 collective-permute-done.amp_row0
  4.9 1.3 select_dynamic-update-slice_fusion
  6.2 14.5 %all-to-all-start.1 = ((f32[32,16,256]{2,1,0:T(8,128)}), f32[32,16,256]{2,1,0:T(8,128)S(1)}, u32[]{:S(2)}, u32[]{:S(2)}) async-start(f32[32,16,256]{2,1,0:T(8,128)} %bitcast.30), calls=%async_computation.1 | async-start | bytes 1048576 | tf_op jit(solution)/shard_map/all_to_all | solution.py:365
  20.7 0.0 copy-start.12
  20.7 0.0 copy-start.11
  20.7 3.7 %shard_map.113 = f32[2048,128]{1,0:T(8,128)} custom-call(f32[512,512]{1,0:T(8,128)} %bitcast.29, bf16[2,512,512]{2,1,0:T(8,128)(2,1)} %constant.54.clone.table), custom_call_target="tpu_custom_call" | custom-call | tf_op jit(solution)/shard_map/pallas_call | solution.py:328
  24.5 10.2 %all-to-all-done.1 = f32[32,16,256]{2,1,0:T(8,128)S(1)} async-done(((f32[32,16,256]{2,1,0:T(8,128)}), f32[32,16,256]{2,1,0:T(8,128)S(1)}, u32[]{:S(2)}, u32[]{:S(2)}) %all-to-all-start.1) | async-done | bytes 524320 | tf_op jit(solution)/shard_map/all_to_all | solution.py:365
  34.7 14.4 %all-to-all-start = ((f32[256,8,128]{2,1,0:T(8,128)}), f32[256,8,128]{2,1,0:T(8,128)S(1)}, u32[]{:S(2)}, u32[]{:S(2)}) async-start(f32[256,8,128]{2,1,0:T(8,128)} %bitcast.17), calls=%async_computation | async-start | bytes 2097152 | tf_op jit(solution)/shard_map/all_to_all | solution.py:351
  49.1 8.1 %collective-permute-start.2 = (f32[96,128]{1,0:T(8,128)S(1)}, f32[96,128]{1,0:T(8,128)S(1)}, u32[]{:S(2)}, u32[]{:S(2)}) collective-permute-start(f32[96,128]{1,0:T(8,128)S(1)} %copy-done.12), channel_id=1, source_target_pairs={{0,1},{1,2},{2,3},{3,4},{4,5},{5,6},{6,7},{7,8},{8,9},{9,10},{10,1... | collective-permute-start | bytes 147464 | tf_op jit(solution)/shard_map/ppermute | solution.py:360
  57.3 1.3 collective-permute-start.3
  58.6 1.3 collective-permute-start.1
  59.9 4.4 %collective-permute-done.2.lo_halo = f32[96,128]{1,0:T(8,128)S(1)} collective-permute-done((f32[96,128]{1,0:T(8,128)S(1)}, f32[96,128]{1,0:T(8,128)S(1)}, u32[]{:S(2)}, u32[]{:S(2)}) %collective-permute-start.2) | collective-permute-done | bytes 49184 | tf_op jit(solution)/shard_map/ppermute | solution.py:360
  64.3 15.7 %collective-permute-done.3.hi_halo = f32[96,128]{1,0:T(8,128)S(1)} collective-permute-done((f32[96,128]{1,0:T(8,128)S(1)}, f32[96,128]{1,0:T(8,128)S(1)}, u32[]{:S(2)}, u32[]{:S(2)}) %collective-permute-start.3) | collective-permute-done | bytes 49184 | tf_op jit(solution)/shard_map/ppermute | solution.py:359
  80.0 0.6 copy-done.4
  80.6 1.6 %shard_map.115 = (f32[32,128]{1,0:T(8,128)}, f32[32,128]{1,0:T(8,128)}) custom-call(f32[256,128]{1,0:T(8,128)} %bitcast.24, f32[256,128]{1,0:T(8,128)} %bitcast.27, f32[96,128]{1,0:T(8,128)} %copy-done.3, f32[96,128]{1,0:T(8,128)} %copy-done.4), custom_call_target="tpu_custom_call" | custom-call | tf_op jit(solution)/shard_map/pallas_call | solution.py:328
  82.2 0.0 collective-permute-done.1.amp_row256
  82.3 0.6 copy-done.10
  82.8 0.4 copy-done
  83.3 10.6 %shard_map.116 = f32[1024,128]{1,0:T(8,128)} custom-call(s32[3]{0:T(128)} %pad_add_fusion.where, f32[2048,128]{1,0:T(8,128)} %bitcast.16, f32[512,256]{1,0:T(8,128)} %bitcast.18, f32[16,256]{1,0:T(8,128)} %copy-done.5, f32[16,256]{1,0:T(8,128)} %copy-done.10, bf16[2,2,512,512]{3,2,1,0:T(8,128)(2,1)} %constant.55.clone.y_fwd, ...), custom_call_target="tpu_custom_call" | custom-call | tf_op jit(solution)/shard_map/pallas_call | solution.py:328
  93.9 9.6 %all-to-all-start.2 = ((f32[256,4,128]{2,1,0:T(4,128)}), f32[256,4,128]{2,1,0:T(4,128)S(1)}, u32[]{:S(2)}, u32[]{:S(2)}) async-start(f32[256,4,128]{2,1,0:T(4,128)} %bitcast.19), calls=%async_computation.2 | async-start | bytes 1048576 | tf_op jit(solution)/shard_map/all_to_all | solution.py:374
  103.5 3.7 %collective-permute-start.4 = (f32[32,128]{1,0:T(8,128)S(1)}, f32[32,128]{1,0:T(8,128)S(1)}, u32[]{:S(2)}, u32[]{:S(2)}) collective-permute-start(f32[32,128]{1,0:T(8,128)S(1)} %copy-done.9), channel_id=1, source_target_pairs={{0,32},{32,64},{64,96},{96,128},{128,160},{160,192},{192,224},{1,3... | collective-permute-start | bytes 49160 | tf_op jit(solution)/shard_map/ppermute | solution.py:375
  107.2 1.9 %collective-permute-start.5 = (f32[32,128]{1,0:T(8,128)S(1)}, f32[32,128]{1,0:T(8,128)S(1)}, u32[]{:S(2)}, u32[]{:S(2)}) collective-permute-start(f32[32,128]{1,0:T(8,128)S(1)} %copy-done.8), channel_id=1, source_target_pairs={{32,0},{64,32},{96,64},{128,96},{160,128},{192,160},{224,192},{33,... | collective-permute-start | bytes 49160 | tf_op jit(solution)/shard_map/ppermute | solution.py:376
  109.1 0.0 collective-permute-done.4.lo_x
  109.1 6.8 %collective-permute-done.5.hi_x = f32[32,128]{1,0:T(8,128)S(1)} collective-permute-done((f32[32,128]{1,0:T(8,128)S(1)}, f32[32,128]{1,0:T(8,128)S(1)}, u32[]{:S(2)}, u32[]{:S(2)}) %collective-permute-start.5) | collective-permute-done | bytes 16416 | tf_op jit(solution)/shard_map/ppermute | solution.py:376
  116.0 9.0 %all-to-all-done.2 = f32[256,4,128]{2,1,0:T(4,128)S(1)} async-done(((f32[256,4,128]{2,1,0:T(4,128)}), f32[256,4,128]{2,1,0:T(4,128)S(1)}, u32[]{:S(2)}, u32[]{:S(2)}) %all-to-all-start.2) | async-done | bytes 524320 | tf_op jit(solution)/shard_map/all_to_all | solution.py:374
  125.0 0.8 copy-done.2
  125.8 2.4 %shard_map.117 = f32[640,128]{1,0:T(8,128)} custom-call(s32[3]{0:T(128)} %pad_add_fusion.where, f32[1024,128]{1,0:T(8,128)} %bitcast.20, bf16[2,320,512]{2,1,0:T(8,128)(2,1)} %constant.59.clone.table, f32[32,128]{1,0:T(8,128)} %copy-done.6, f32[32,128]{1,0:T(8,128)} %copy-done.7), custom_call_target="tpu_custom_call" | custom-call | tf_op jit(solution)/shard_map/pallas_call | solution.py:328
  128.2 14.8 %all_to_all.44 = f32[8,80,128]{2,1,0:T(8,128)} all-to-all(f32[8,80,128]{2,1,0:T(8,128)} %bitcast.22), channel_id=1, replica_groups=mesh['ga'=8,'ba'=32] {'ga'}, dimensions={0} | all-to-all | bytes 655360 | tf_op jit(solution)/shard_map/all_to_all | solution.py:378
  143.0 2.5 %shard_map.118 = (f32[256,128]{1,0:T(8,128)}, f32[256,128]{1,0:T(8,128)}) custom-call(s32[3]{0:T(128)} %pad_add_fusion.where, f32[640,128]{1,0:T(8,128)} %bitcast.21, f32[256,128]{1,0:T(8,128)} %bitcast.25, f32[256,128]{1,0:T(8,128)} %bitcast.28, f32[96,128]{1,0:T(8,128)} %copy-done.3, f32[96,128]{1,0:T(8,128)} %copy-done.4, f32[32,128]{1,0:T(8,128)} %copy-done.6, ...), custom_call_target="tpu_custom_call" | custom-call | tf_op jit(solution)/shard_map/pallas_call | solution.py:328
  (23 shorter events, 0.0 us)
Async XLA Ops:
  4.2 0.7 collective-permute-start
  4.9 19.6 %copy-start.5 = (f32[16,256]{1,0:T(8,128)}, f32[16,256]{1,0:T(8,128)S(1)}, u32[]{:S(2)}) copy-start(f32[16,256]{1,0:T(8,128)S(1)} %collective-permute-done.amp_row0) | copy-start | bytes 49156
  6.2 28.5 %all-to-all-start.1 = ((f32[32,16,256]{2,1,0:T(8,128)}), f32[32,16,256]{2,1,0:T(8,128)S(1)}, u32[]{:S(2)}, u32[]{:S(2)}) async-start(f32[32,16,256]{2,1,0:T(8,128)} %bitcast.30), calls=%async_computation.1 | async-start | bytes 1048576 | tf_op jit(solution)/shard_map/all_to_all | solution.py:365
  20.7 28.4 %copy-start.12 = (f32[96,128]{1,0:T(8,128)S(1)}, f32[96,128]{1,0:T(8,128)}, u32[]{:S(2)}) copy-start(f32[96,128]{1,0:T(8,128)} %get-tuple-element.24) | copy-start | bytes 147460
  20.7 36.5 %copy-start.11 = (f32[96,128]{1,0:T(8,128)S(1)}, f32[96,128]{1,0:T(8,128)}, u32[]{:S(2)}) copy-start(f32[96,128]{1,0:T(8,128)} %get-tuple-element.25) | copy-start | bytes 147460
  20.7 37.8 %copy-start.13 = (f32[16,256]{1,0:T(8,128)S(1)}, f32[16,256]{1,0:T(8,128)}, u32[]{:S(2)}) copy-start(f32[16,256]{1,0:T(8,128)} %get-tuple-element.23) | copy-start | bytes 49156
  34.7 47.6 %copy-start.1 = (f32[32,16,256]{2,1,0:T(8,128)}, f32[32,16,256]{2,1,0:T(8,128)S(1)}, u32[]{:S(2)}) copy-start(f32[32,16,256]{2,1,0:T(8,128)S(1)} %all-to-all-done.1) | copy-start | bytes 1572868
  34.7 47.6 %all-to-all-start = ((f32[256,8,128]{2,1,0:T(8,128)}), f32[256,8,128]{2,1,0:T(8,128)S(1)}, u32[]{:S(2)}, u32[]{:S(2)}) async-start(f32[256,8,128]{2,1,0:T(8,128)} %bitcast.17), calls=%async_computation | async-start | bytes 2097152 | tf_op jit(solution)/shard_map/all_to_all | solution.py:351
  49.1 15.2 %collective-permute-start.2 = (f32[96,128]{1,0:T(8,128)S(1)}, f32[96,128]{1,0:T(8,128)S(1)}, u32[]{:S(2)}, u32[]{:S(2)}) collective-permute-start(f32[96,128]{1,0:T(8,128)S(1)} %copy-done.12), channel_id=1, source_target_pairs={{0,1},{1,2},{2,3},{3,4},{4,5},{5,6},{6,7},{7,8},{8,9},{9,10},{10,1... | collective-permute-start | bytes 147464 | tf_op jit(solution)/shard_map/ppermute | solution.py:360
  57.3 22.8 %collective-permute-start.3 = (f32[96,128]{1,0:T(8,128)S(1)}, f32[96,128]{1,0:T(8,128)S(1)}, u32[]{:S(2)}, u32[]{:S(2)}) collective-permute-start(f32[96,128]{1,0:T(8,128)S(1)} %copy-done.11), channel_id=1, source_target_pairs={{1,0},{2,1},{3,2},{4,3},{5,4},{6,5},{7,6},{8,7},{9,8},{10,9},{11,1... | collective-permute-start | bytes 147464 | tf_op jit(solution)/shard_map/ppermute | solution.py:359
  58.6 23.7 %collective-permute-start.1 = (f32[16,256]{1,0:T(8,128)S(1)}, f32[16,256]{1,0:T(8,128)S(1)}, u32[]{:S(2)}, u32[]{:S(2)}) collective-permute-start(f32[16,256]{1,0:T(8,128)S(1)} %copy-done.13), channel_id=1, source_target_pairs={{16,0},{48,32},{80,64},{112,96},{144,128},{176,160},{208,192},{240... | collective-permute-start | bytes 49160 | tf_op jit(solution)/shard_map/ppermute | solution.py:362
  64.3 15.7 %copy-start.3 = (f32[96,128]{1,0:T(8,128)}, f32[96,128]{1,0:T(8,128)S(1)}, u32[]{:S(2)}) copy-start(f32[96,128]{1,0:T(8,128)S(1)} %collective-permute-done.2.lo_halo) | copy-start | bytes 147460
  80.0 0.6 copy-start.4
  82.2 0.6 copy-start.10
  82.2 1.0 copy-start
  83.3 20.3 %copy-start.9 = (f32[32,128]{1,0:T(8,128)S(1)}, f32[32,128]{1,0:T(8,128)}, u32[]{:S(2)}) copy-start(f32[32,128]{1,0:T(8,128)} %get-tuple-element.26.up) | copy-start | bytes 49156
  83.3 23.9 %copy-start.8 = (f32[32,128]{1,0:T(8,128)S(1)}, f32[32,128]{1,0:T(8,128)}, u32[]{:S(2)}) copy-start(f32[32,128]{1,0:T(8,128)} %get-tuple-element.27.down) | copy-start | bytes 49156
  93.9 31.1 %all-to-all-start.2 = ((f32[256,4,128]{2,1,0:T(4,128)}), f32[256,4,128]{2,1,0:T(4,128)S(1)}, u32[]{:S(2)}, u32[]{:S(2)}) async-start(f32[256,4,128]{2,1,0:T(4,128)} %bitcast.19), calls=%async_computation.2 | async-start | bytes 1048576 | tf_op jit(solution)/shard_map/all_to_all | solution.py:374
  103.5 5.6 %collective-permute-start.4 = (f32[32,128]{1,0:T(8,128)S(1)}, f32[32,128]{1,0:T(8,128)S(1)}, u32[]{:S(2)}, u32[]{:S(2)}) collective-permute-start(f32[32,128]{1,0:T(8,128)S(1)} %copy-done.9), channel_id=1, source_target_pairs={{0,32},{32,64},{64,96},{96,128},{128,160},{160,192},{192,224},{1,3... | collective-permute-start | bytes 49160 | tf_op jit(solution)/shard_map/ppermute | solution.py:375
  107.2 8.8 %collective-permute-start.5 = (f32[32,128]{1,0:T(8,128)S(1)}, f32[32,128]{1,0:T(8,128)S(1)}, u32[]{:S(2)}, u32[]{:S(2)}) collective-permute-start(f32[32,128]{1,0:T(8,128)S(1)} %copy-done.8), channel_id=1, source_target_pairs={{32,0},{64,32},{96,64},{128,96},{160,128},{192,160},{224,192},{33,... | collective-permute-start | bytes 49160 | tf_op jit(solution)/shard_map/ppermute | solution.py:376
  109.1 15.9 %copy-start.6 = (f32[32,128]{1,0:T(8,128)}, f32[32,128]{1,0:T(8,128)S(1)}, u32[]{:S(2)}) copy-start(f32[32,128]{1,0:T(8,128)S(1)} %collective-permute-done.4.lo_x) | copy-start | bytes 49156
  116.0 9.0 %copy-start.7 = (f32[32,128]{1,0:T(8,128)}, f32[32,128]{1,0:T(8,128)S(1)}, u32[]{:S(2)}) copy-start(f32[32,128]{1,0:T(8,128)S(1)} %collective-permute-done.5.hi_x) | copy-start | bytes 49156
  125.0 0.8 copy-start.2

commit v4 on v3

--- a/solution.py
+++ b/solution.py
@@ -63,18 +63,13 @@
     z_fwd = np.concatenate(trig(z_order, np.arange(EZ), EZ), 1)
     z_inv = np.concatenate(trig(np.arange(EZ), np.arange(AZ), EZ), 1)
 
-    cos, sin = trig(np.arange(AY), np.arange(EY), EY)
-    y_inv = np.concatenate(
-        [np.concatenate([cos, sin]), np.concatenate([-sin, cos])], 1
-    )
-
     xs = np.clip((32 * np.arange(GA)[:, None] - 4 + np.arange(XROWS)).reshape(-1), 0, AX - 1)
     cos, sin = trig(xs, np.maximum(kx, 0), EX)
     back_re, back_im = 2.0 * cos, -2.0 * sin
     back_re[:, packed] = alternating[xs][:, None]
     back_im[:, packed] = 1.0
     x_inv = np.concatenate([back_re, back_im], 1) / (EX * EY * EZ)
-    return tuple(split_np(t) for t in (x_fwd, y_fwd, z_fwd, z_inv, y_inv, x_inv))
+    return tuple(split_np(t) for t in (x_fwd, y_fwd, z_fwd, z_inv, x_inv))
 
 
 def split(value):
@@ -112,21 +107,21 @@
     pltpu.sync_copy(rows_out, sent)
 
 
-def edges_kernel(where, amp, head, rech, amp_sent, amp_first, below, above, amp_in, head_in, rech_in, sems):
-    ga = where[0]
-    copies = fetch([(amp.at[:, 0:40, :], amp_in), (head, head_in), (rech, rech_in)], sems)
-    for copy in copies:
-        copy.wait()
+def edges_kernel(amp, amp_first, amp_zero, head, rech, amp_sent, up, down, amp_in, sems):
+    ga, ba = lax.axis_index("ga"), lax.axis_index("ba")
+    (copy,) = fetch([(amp.at[:, 0:40, :], amp_in)], sems)
+    for out, far, near in ((up, 30, 31), (down, 1, 0)):
+        out[0:8, :] = head[8 * far : 8 * far + 8, :]
+        out[8:16, :] = head[8 * near : 8 * near + 8, :]
+        out[16:24, :] = rech[8 * near : 8 * near + 8, :]
+    copy.wait()
+    zero = (ga == PACKED_GA) & (ba >= BA // 2)
     for half in range(2):
         lanes = slice(128 * half, 128 * half + 128)
-        first = amp_in[:, 0, lanes]
-        amp_first[:, lanes] = first
+        first = jnp.where(zero, amp_zero[:, lanes], amp_first[:, lanes])
         amp_sent[0:16, lanes] = jnp.where(ga < PACKED_GA, amp_in[:, 32, lanes], first)
         for b in range(1, BA):
             amp_sent[16 * b : 16 * b + 16, lanes] = amp_in[:, b, lanes]
-    for out, near in ((below, (0, 1, 0)), (above, (6, 7, 7))):
-        for i, (ref, y) in enumerate(zip((head_in, head_in, rech_in), near)):
-            out[32 * i : 32 * i + 32, :] = ref[pl.ds(y, 32, stride=8), :]
 
 
 def mirror_of(value):
@@ -145,12 +140,14 @@
     return total
 
 
-def middle_kernel(where, got, amp, amp_row0, amp_row256, y_fwd, z_fwd, z_inv, y_inv, up, down, sent,
-                  got_in, amp_in, y_fwd_in, z_fwd_in, z_inv_in, y_inv_in, row0_in, row256_in,
+def middle_kernel(got, amp_near, amp_far, amp_row0, amp_row256, y_fwd, z_fwd, z_inv, below, above, sent,
+                  got_in, amp_in, y_fwd_in, z_fwd_in, z_inv_in, row0_in, row256_in,
                   rows, lines, amps, sems):
-    packed = where[1] == 1
-    pairs = [(got, got_in), (y_fwd, y_fwd_in), (z_fwd, z_fwd_in), (amp, amp_in), (z_inv, z_inv_in),
-             (y_inv, y_inv_in), (amp_row0, row0_in), (amp_row256, row256_in)]
+    ga, ba = lax.axis_index("ga"), lax.axis_index("ba")
+    packed = (ga == PACKED_GA) & (ba == 0)
+    side = lax.rem(ba, 2)
+    pairs = [(got, got_in), (y_fwd, y_fwd_in), (z_fwd, z_fwd_in), (amp_near.at[:, side], amp_in.at[:, side]),
+             (amp_far, amp_in.at[:, 1 - side]), (z_inv, z_inv_in), (amp_row0, row0_in), (amp_row256, row256_in)]
     copies = fetch(pairs, sems)
     copies[0].wait()
     low_half = lax.broadcasted_iota(jnp.int32, (BA, 128), 1) < 64
@@ -166,17 +163,17 @@
                     high, low = split(value)
                     rows[0, at, 128 * p : 128 * p + 128] = high
                     rows[1, at, 128 * p : 128 * p + 128] = low
-    copies[3].wait()
-    copies[6].wait()
-    copies[7].wait()
+    for i in (3, 4, 6, 7):
+        copies[i].wait()
 
     @pl.when(packed)
     def _():
-        held = amp_in[...]
+        held = amp_in[...].reshape(EY, EZ)
         mirror = mirror_of(held)
         ky = lax.broadcasted_iota(jnp.int32, (EY, EZ), 0)
         amps[...] = jnp.where(ky == 0, row0_in[0:1, :], jnp.where(ky < 256, mirror, held))
-        amp_in[...] = jnp.where(ky == 256, row256_in[0:1, :], jnp.where(ky < 256, held, mirror))
+        new = jnp.where(ky == 256, row256_in[0:1, :], jnp.where(ky < 256, held, mirror))
+        amp_in[...] = new.reshape(amp_in.shape)
 
     for part in range(2):
         ky = slice(256 * part, 256 * part + 256)
@@ -189,59 +186,57 @@
         imag = by_cos[:, 256:] - by_sin[:, :256]
         if part == 0:
             copies[2].wait()
-            copies[4].wait()
+            copies[5].wait()
         forward = (z_fwd_in[0], z_fwd_in[1])
         real, imag = dot3(split(real), forward), dot3(split(imag), forward)
         real, imag = real[:, :256] + imag[:, 256:], imag[:, :256] - real[:, 256:]
 
-        def back(amp_ref, lanes):
+        def back(scale, at):
             table = (z_inv_in[0], z_inv_in[1])
-            scale = amp_ref[ky, :]
             re, im = dot3(split(real * scale), table), dot3(split(imag * scale), table)
             for c, value in enumerate((re[:, :128] - im[:, 128:], im[:, :128] + re[:, 128:])):
-                high, low = split(value)
-                at = slice(512 * c + 256 * part, 512 * c + 256 * part + 256)
-                lines[0, at, lanes] = high
-                lines[1, at, lanes] = low
-
-        back(amp_in, slice(0, 128))
+                lanes = slice(128 * c, 128 * c + 128)
+                lines[at, 0, ky, lanes], lines[at, 1, ky, lanes] = split(value)
+
+        back(amp_in[8 * part : 8 * part + 8].reshape(256, EZ), 0)
 
         @pl.when(packed)
         def _():
-            back(amps, slice(128, 256))
-
-        @pl.when(jnp.logical_not(packed))
-        def _():
-            for i in range(2):
-                for c in range(2):
-                    at = slice(512 * c + 256 * part, 512 * c + 256 * part + 256)
-                    lines[i, at, 128:256] = jnp.zeros((256, 128), bf16)
-
-    copies[5].wait()
-    result = dot3((y_inv_in[0], y_inv_in[1]), (lines[0], lines[1]))
-    forward_halo = lax.broadcasted_iota(jnp.int32, (AY, AZ), 0) % GA < GA // 2
-    for c in range(2):
-        own = result[AY * c : AY * c + AY, :AZ]
-        if c == 1:
-            own = jnp.where(packed, result[AY:, AZ:], own)
+            back(amps[ky, :], 1)
+
+    def inverse(at):
+        data = (lines[at, 0], lines[at, 1])
+        near = slice(0, AY)
+        by_cos = dot3((y_fwd_in[0, 0, near, :], y_fwd_in[1, 0, near, :]), data)
+        by_sin = dot3((y_fwd_in[0, 1, near, :], y_fwd_in[1, 1, near, :]), data)
+        return by_cos[:, :AZ] - by_sin[:, AZ:], by_cos[:, AZ:] + by_sin[:, :AZ]
+
+    def store(c, own):
+        forward_halo = lax.broadcasted_iota(jnp.int32, (AY, AZ), 0) % GA < GA // 2
         after = jnp.concatenate([own[GA:], own[:GA]], 0)
         before = jnp.concatenate([own[AY - GA :], own[: AY - GA]], 0)
         sent[pl.ds(c, AY, stride=4), :] = own
         sent[pl.ds(2 + c, AY, stride=4), :] = jnp.where(forward_halo, after, before)
 
-
-def pack_kernel(head, rech, lo_halo, hi_halo, up, down):
+    real, imag = inverse(0)
+    store(0, real)
+    store(1, imag)
+
+    @pl.when(packed)
+    def _():
+        store(1, inverse(1)[1])
+
+
+def pack_kernel(head, rech, lo_x, hi_x, below, above):
     corner = lax.broadcasted_iota(jnp.int32, (8, AZ), 0)
-    for out, far, near in ((up, 30, 31), (down, 1, 0)):
-        out[0:8, :] = head[8 * far : 8 * far + 8, :]
-        out[8:16, :] = head[8 * near : 8 * near + 8, :]
-        out[16:24, :] = rech[8 * near : 8 * near + 8, :]
-        before, after = lo_halo[32 + near : 33 + near, :], hi_halo[near : near + 1, :]
-        out[24:32, :] = jnp.where(corner == 0, before, after)
-
-
-def field_kernel(where, got, table, lo_x, hi_x, sent):
-    ga, ba = where[0], where[2]
+    for out, near, far in ((below, 0, 1), (above, 7, 6)):
+        for i, (ref, y) in enumerate(((head, near), (head, far), (rech, near))):
+            out[32 * i : 32 * i + 32, :] = ref[pl.ds(y, 32, stride=8), :]
+        out[96:104, :] = jnp.where(corner == 0, lo_x[8 + near : 9 + near, :], hi_x[8 + near : 9 + near, :])
+
+
+def field_kernel(got, table, lo_halo, hi_halo, sent):
+    ga, ba = lax.axis_index("ga"), lax.axis_index("ba")
     own = jnp.concatenate([got[pl.ds(c, DEVS, stride=4), :] for c in range(2)], 0)
     halo = jnp.concatenate([got[pl.ds(2 + c, DEVS, stride=4), :] for c in range(2)], 0)
     log_field = dot3((table[0], table[1]), split(jnp.concatenate([own, halo], 1)))
@@ -256,16 +251,16 @@
         sent[CHUNK * g + XROWS : CHUNK * g + CHUNK, :] = beside
 
 
-def sweep_kernel(where, got, head, rech, lo_halo, hi_halo, lo_x, hi_x, cond_out, press_out,
+def sweep_kernel(got, head, rech, lo_halo, hi_halo, lo_x, hi_x, cond_out, press_out,
                  head_ext, rech_ext, staged):
-    ga, ba = where[0], where[2]
+    ga, ba = lax.axis_index("ga"), lax.axis_index("ba")
     head_ext[...] = jnp.zeros_like(head_ext)
     rech_ext[...] = jnp.zeros_like(rech_ext)
     for y in range(8):
         at = XROWS * (y + 2)
         head_ext[at + 4 : at + 36, :] = head[pl.ds(y, 32, stride=8), :]
         rech_ext[at + 4 : at + 36, :] = rech[pl.ds(y, 32, stride=8), :]
-    for halo, (first, second, only) in ((lo_halo, (0, 1, 1)), (hi_halo, (10, 11, 10))):
+    for halo, (first, second, only) in ((lo_halo, (1, 0, 1)), (hi_halo, (10, 11, 10))):
         for ref, y, i in ((head_ext, first, 0), (head_ext, second, 1), (rech_ext, only, 2)):
             ref[XROWS * y + 4 : XROWS * y + 36, :] = halo[32 * i : 32 * i + 32, :]
     for block, far, near in ((lo_x, 2, 3), (hi_x, 37, 36)):
@@ -274,8 +269,9 @@
             head_ext[at + far : at + far + 1, :] = block[y : y + 1, :]
             head_ext[at + near : at + near + 1, :] = block[8 + y : 9 + y, :]
             rech_ext[at + near : at + near + 1, :] = block[16 + y : 17 + y, :]
-        head_ext[XROWS + near : XROWS + near + 1, :] = block[24:25, :]
-        head_ext[10 * XROWS + near : 10 * XROWS + near + 1, :] = block[25:26, :]
+    for halo, y in ((lo_halo, 1), (hi_halo, 10)):
+        for i, near in enumerate((3, 36)):
+            head_ext[XROWS * y + near : XROWS * y + near + 1, :] = halo[96 + i : 97 + i, :]
 
     lane = lax.broadcasted_iota(jnp.int32, (XROWS, AZ), 1)
     row = lax.broadcasted_iota(jnp.int32, (XROWS, AZ), 0)
@@ -317,29 +313,24 @@
 
 def kernel_call(kernel, outs, inputs, scratch=(), held=(), outs_held=()):
     vmem = pl.BlockSpec(memory_space=pltpu.VMEM)
-    smem = pl.BlockSpec(memory_space=pltpu.SMEM)
     there = pl.BlockSpec(memory_space=pl.ANY)
-
-    def spec(i, value):
-        if value.dtype == jnp.int32:
-            return smem
-        return there if i in held else vmem
-
     return pl.pallas_call(
         kernel,
         out_shape=[jax.ShapeDtypeStruct(shape, f32) for shape in outs],
-        in_specs=[spec(i, value) for i, value in enumerate(inputs)],
+        in_specs=[there if i in held else vmem for i in range(len(inputs))],
         out_specs=[there if i in outs_held else vmem for i in range(len(outs))],
         scratch_shapes=list(scratch),
         compiler_params=pltpu.CompilerParams(vmem_limit_bytes=VMEM),
     )(*inputs)
 
 
+def steps(axis):
+    up = [(i, i + 1) for i in range(lax.axis_size(axis) - 1)]
+    return up, [(j, i) for i, j in up]
+
+
 def body(noise, amplitude, recharge, head_guess):
-    x_fwd, y_fwd, z_fwd, z_inv, y_inv, x_inv = (jnp.asarray(t) for t in tables())
-    ga, ba = lax.axis_index("ga"), lax.axis_index("ba")
-    packed = ((ga == PACKED_GA) & (ba == 0)).astype(jnp.int32)
-    where = jnp.stack([ga.astype(jnp.int32), packed, ba.astype(jnp.int32)])
+    x_fwd, y_fwd, z_fwd, z_inv, x_inv = (jnp.asarray(t) for t in tables())
     recharge = recharge.reshape(256, AZ)
     head = head_guess.reshape(256, AZ)
     memory, sems = pltpu.VMEM, pltpu.SemaphoreType.DMA
@@ -349,37 +340,39 @@
         held=(0, 1), outs_held=(0,),
     )
     got = lax.all_to_all(sent, ("ba", "ga"), 0, 0, tiled=True)
-    amp_sent, amp_first, below, above = kernel_call(
-        edges_kernel, [(512, EZ), (16, EZ), (96, AZ), (96, AZ)], [where, amplitude, head, recharge],
-        [memory((16, 40, EZ), f32), memory((256, AZ), f32), memory((256, AZ), f32), sems((3,))],
-        held=(1, 2, 3),
-    )
-    up = [(i, i + 1) for i in range(BA - 1)]
-    down = [(j, i) for i, j in up]
+    amp_first = amplitude[:, 0, :]
+    amp_zero = lax.ppermute(amp_first, "ga", [(0, PACKED_GA)])
+    amp_row = lax.ppermute(amp_first, "ba", [(BA // 2, 0)])
+    amp_sent, to_up, to_down = kernel_call(
+        edges_kernel, [(512, EZ), (24, AZ), (24, AZ)], [amplitude, amp_first, amp_zero, head, recharge],
+        [memory((16, 40, EZ), f32), sems((1,))], held=(0,),
+    )
+    halves = [list(range(side, BA, 2)) for side in range(2)]
+    amp_near = lax.all_to_all(amp_sent, "ba", 0, 0, tiled=True, axis_index_groups=halves)
+    amp_near = amp_near.reshape(BA // 2, 2, 16, EZ)
+    give = jnp.where(lax.axis_index("ba") % 2 == 0, amp_near[:, 1], amp_near[:, 0])
+    amp_far = lax.ppermute(give, "ba", [(i, i ^ 1) for i in range(BA)])
+    up, down = steps("ga")
+    lo_x = lax.ppermute(to_up, "ga", up)
+    hi_x = lax.ppermute(to_down, "ga", down)
+    below, above = kernel_call(pack_kernel, [(104, AZ), (104, AZ)], [head, recharge, lo_x, hi_x])
+    inputs = [got, amp_near, amp_far, amp_zero, amp_row, y_fwd, z_fwd, z_inv, below, above]
+    (sent,) = kernel_call(
+        middle_kernel, [(4 * AY, AZ)], inputs,
+        [memory(value.shape, value.dtype) for value in (got, amp_near, y_fwd, z_fwd, z_inv, amp_zero, amp_row)]
+        + [memory((2, 512, 512), bf16), memory((2, 2, EY, 2 * AZ), bf16), memory((EY, EZ), f32), sems((8,))],
+        held=range(10),
+    )
+    got = lax.all_to_all(sent, ("ba", "ga"), 0, 0, tiled=True)
+    up, down = steps("ba")
     hi_halo = lax.ppermute(below, "ba", down)
     lo_halo = lax.ppermute(above, "ba", up)
-    amp_zero = lax.ppermute(amp_first, "ga", [(0, PACKED_GA)])
-    amp_row = lax.ppermute(amp_first, "ba", [(BA // 2, 0)])
-    swap = (ga == PACKED_GA) & (ba >= BA // 2)
-    amp_sent = amp_sent.at[:16].set(jnp.where(swap, amp_zero, amp_sent[:16]))
-    amp_got = lax.all_to_all(amp_sent, "ba", 0, 0, tiled=True)
-    to_up, to_down = kernel_call(pack_kernel, [(32, AZ), (32, AZ)], [head, recharge, lo_halo, hi_halo])
-    inputs = [where, got, amp_got, amp_zero, amp_row, y_fwd, z_fwd, z_inv, y_inv, to_up, to_down]
-    (sent,) = kernel_call(
-        middle_kernel, [(4 * AY, AZ)], inputs,
-        [memory(value.shape, value.dtype) for value in (got, amp_got, y_fwd, z_fwd, z_inv, y_inv, amp_zero, amp_row)]
-        + [memory((2, 512, 512), bf16), memory((2, 1024, 2 * AZ), bf16), memory((EY, EZ), f32), sems((8,))],
-        held=range(1, 11),
-    )
-    got = lax.all_to_all(sent, ("ba", "ga"), 0, 0, tiled=True)
-    lo_x = lax.ppermute(to_up, "ga", [(i, i + 1) for i in range(GA - 1)])
-    hi_x = lax.ppermute(to_down, "ga", [(i + 1, i) for i in range(GA - 1)])
-    (sent,) = kernel_call(field_kernel, [(CHUNK * GA, AZ)], [where, got, x_inv, lo_x, hi_x], held=(3, 4))
+    (sent,) = kernel_call(field_kernel, [(CHUNK * GA, AZ)], [got, x_inv, lo_halo, hi_halo], held=(2, 3))
     got = lax.all_to_all(sent, "ga", 0, 0, tiled=True)
     ext = pltpu.VMEM((12 * XROWS, AZ), f32)
     conductivity, pressure = kernel_call(
         sweep_kernel, [(256, AZ), (256, AZ)],
-        [where, got, head, recharge, lo_halo, hi_halo, lo_x, hi_x],
+        [got, head, recharge, lo_halo, hi_halo, lo_x, hi_x],
         [ext, ext, pltpu.VMEM((XROWS, AZ), f32)],
     )
     return conductivity.reshape(32, 8, AZ), pressure.reshape(32, 8, AZ)

time: 146 us -> 145 us (level)
  waiting for transfers between devices: 46.3 us -> 40.9 us
  starting transfers between devices: 55.5 us -> 58.7 us
  blocking collectives: 14.8 us -> 17.8 us
  other arithmetic: 1.99 us -> 0.04 us
  local copies, waits for them, and re-layouts: 2.46 us -> 4.02 us
  Pallas kernels: 23.6 us -> 22.1 us
    ppermute x2 -> x3, waiting for transfers between devices: 6.85 us -> 24.2 us  [the longest x1 11.6 us: body(): lo_x = lax.ppermute(to_up, 'ga', up)]
    all_to_all x2, waiting for transfers between devices: 9.02 us -> 0.91 us  [body(): got = lax.all_to_all(sent, ('ba', 'ga'), 0, 0, tiled=True)]
    all_to_all x1, starting transfers between devices: 14.5 us -> 7.6 us  [body(): lax.all_to_all(amp_sent, 'ba', 0, 0, tiled=True, axis_index_groups=halves)]
    ppermute x2 -> x3, starting transfers between devices: 5.58 us -> 11.2 us  [the longest x1 6.31 us: body(): amp_far = lax.ppermute(give, 'ba', [(i, i ^ 1) for i in range(BA)])]
    ppermute x1, waiting for transfers between devices: 15.7 us -> 10.4 us  [body(): hi_halo = lax.ppermute(below, 'ba', down)]
    all_to_all x1, waiting for transfers between devices: 10.2 us -> 5.25 us  [body(): lax.all_to_all(amp_sent, 'ba', 0, 0, tiled=True, axis_index_groups=halves)]
    all_to_all x2, starting transfers between devices: 24 us -> 28.5 us  [body(): got = lax.all_to_all(sent, ('ba', 'ga'), 0, 0, tiled=True)]
    ppermute x1, waiting for transfers between devices: 4.42 us -> 0.14 us  [body(): lo_halo = lax.ppermute(above, 'ba', up)]
  transfers between devices with their start and end apart: 9 -> 10, of which waited for: 5 -> 7; matrix products, arithmetic and copies ran while one was open for 0% -> 0% of each run, Pallas kernels for 4% -> 4%
where the time goes in v4:
time: 145 us; the launch traced here: 144 us
  starting transfers between devices  58.7 us (40%)
  waiting for transfers between devices  40.9 us (28%)
  Pallas kernels  22.1 us (15%)
  blocking collectives  17.8 us (12%)
  local copies, waits for them, and re-layouts  4.02 us (3%)
    all_to_all x2, starting transfers between devices, body(): got = lax.all_to_all(sent, ('ba', 'ga'), 0, 0, tiled=True)  28.5 us
    pallas_call x6, Pallas kernels, kernel_call(): pl.pallas_call(kernel, out_shape=[jax.ShapeDtypeStruct(shape, f32) for sh...  22.1 us
    all_to_all x1, blocking collectives, body(): got = lax.all_to_all(sent, 'ga', 0, 0, tiled=True)  17.8 us
    ppermute x1, waiting for transfers between devices, body(): lo_x = lax.ppermute(to_up, 'ga', up)  11.6 us
    ppermute x1, waiting for transfers between devices, body(): hi_x = lax.ppermute(to_down, 'ga', down)  10.8 us
    ppermute x1, waiting for transfers between devices, body(): hi_halo = lax.ppermute(below, 'ba', down)  10.4 us
    ppermute x1, starting transfers between devices, body(): lo_halo = lax.ppermute(above, 'ba', up)  8.13 us
    all_to_all x1, starting transfers between devices, body(): lax.all_to_all(amp_sent, 'ba', 0, 0, tiled=True, axis_index_groups=halves)  7.6 us
  transfers between devices with their start and end apart: 10, of which 7 were waited for; matrix products, arithmetic and copies ran while one was open for 0% of the time, Pallas kernels for 4%

profile of v4, /device:TPU:1, one launch (start us, length us, event | category | flops | bytes accessed | tf_op | source)
XLA Modules:
  0.0 144.4 jit_solution(5773628381245504700)
XLA Ops:
  0.6 0.9 slice.9
  1.6 0.0 copy-start.7
  1.6 0.7 collective-permute-start
  2.3 0.6 copy-done.6
  2.9 3.1 %shard_map.105 = (f32[512,256]{1,0:T(8,128)}, f32[24,128]{1,0:T(8,128)}, f32[24,128]{1,0:T(8,128)}) custom-call(f32[16,64,256]{2,1,0:T(8,128)} %amp.1, f32[16,256]{1,0:T(8,128)} %bitcast.45, f32[16,256]{1,0:T(8,128)} %copy-done.6, f32[256,128]{1,0:T(8,128)} %bitcast.36, f32[256,128]{1,0:T(8,128)} %bitcast.39), custom_call_target="tpu_custom_call" | custom-call | tf_op jit(solution)/shard_map/pallas_call | solution.py:317
  6.0 7.6 %all-to-all-start.1 = ((f32[16,32,256]{2,1,0:T(8,128)}), f32[16,32,256]{2,1,0:T(8,128)S(1)}, u32[]{:S(2)}, u32[]{:S(2)}) async-start(f32[16,32,256]{2,1,0:T(8,128)} %bitcast.43), calls=%async_computation.1 | async-start | bytes 1048576 | tf_op jit(solution)/shard_map/all_to_all | solution.py:351
  13.6 3.7 %shard_map.104 = f32[2048,128]{1,0:T(8,128)} custom-call(f32[512,512]{1,0:T(8,128)} %bitcast.42, bf16[2,512,512]{2,1,0:T(8,128)(2,1)} %constant.28.clone.table), custom_call_target="tpu_custom_call" | custom-call | tf_op jit(solution)/shard_map/pallas_call | solution.py:317
  17.2 0.0 copy-start.8
  17.3 5.2 %all-to-all-done.1 = f32[16,32,256]{2,1,0:T(8,128)S(1)} async-done(((f32[16,32,256]{2,1,0:T(8,128)}), f32[16,32,256]{2,1,0:T(8,128)S(1)}, u32[]{:S(2)}, u32[]{:S(2)}) %all-to-all-start.1) | async-done | bytes 524320 | tf_op jit(solution)/shard_map/all_to_all | solution.py:351
  22.5 17.6 %all-to-all-start = ((f32[256,8,128]{2,1,0:T(8,128)}), f32[256,8,128]{2,1,0:T(8,128)S(1)}, u32[]{:S(2)}, u32[]{:S(2)}) async-start(f32[256,8,128]{2,1,0:T(8,128)} %bitcast.30), calls=%async_computation | async-start | bytes 2097152 | tf_op jit(solution)/shard_map/all_to_all | solution.py:342
  40.2 6.3 %collective-permute-start.1 = (f32[16,16,256]{2,1,0:T(8,128)S(1)}, f32[16,16,256]{2,1,0:T(8,128)S(1)}, u32[]{:S(2)}, u32[]{:S(2)}) collective-permute-start(f32[16,16,256]{2,1,0:T(8,128)S(1)} %fusion.1), channel_id=1, source_target_pairs={{0,1},{1,0},{2,3},{3,2},{4,5},{5,4},{6,7},{7,6},{8,9},{9,8},{10,11... | collective-permute-start | bytes 786440 | tf_op jit(solution)/shard_map/ppermute | solution.py:354
  46.5 1.3 collective-permute-start.2
  47.8 3.0 %collective-permute-start.3 = (f32[24,128]{1,0:T(8,128)S(1)}, f32[24,128]{1,0:T(8,128)S(1)}, u32[]{:S(2)}, u32[]{:S(2)}) collective-permute-start(f32[24,128]{1,0:T(8,128)S(1)} %copy-done.15), channel_id=1, source_target_pairs={{0,32},{32,64},{64,96},{96,128},{128,160},{160,192},{192,224},{1,3... | collective-permute-start | bytes 36872 | tf_op jit(solution)/shard_map/ppermute | solution.py:356
  50.8 1.9 %collective-permute-start.4 = (f32[24,128]{1,0:T(8,128)S(1)}, f32[24,128]{1,0:T(8,128)S(1)}, u32[]{:S(2)}, u32[]{:S(2)}) collective-permute-start(f32[24,128]{1,0:T(8,128)S(1)} %copy-done.14), channel_id=1, source_target_pairs={{32,0},{64,32},{96,64},{128,96},{160,128},{192,160},{224,192},{33,... | collective-permute-start | bytes 36872 | tf_op jit(solution)/shard_map/ppermute | solution.py:357
  52.8 11.6 %collective-permute-done.3.lo_x = f32[24,128]{1,0:T(8,128)S(1)} collective-permute-done((f32[24,128]{1,0:T(8,128)S(1)}, f32[24,128]{1,0:T(8,128)S(1)}, u32[]{:S(2)}, u32[]{:S(2)}) %collective-permute-start.3) | collective-permute-done | bytes 12320 | tf_op jit(solution)/shard_map/ppermute | solution.py:356
  64.3 10.8 %collective-permute-done.4.hi_x = f32[24,128]{1,0:T(8,128)S(1)} collective-permute-done((f32[24,128]{1,0:T(8,128)S(1)}, f32[24,128]{1,0:T(8,128)S(1)}, u32[]{:S(2)}, u32[]{:S(2)}) %collective-permute-start.4) | collective-permute-done | bytes 12320 | tf_op jit(solution)/shard_map/ppermute | solution.py:357
  75.1 0.6 copy-done.12
  75.7 1.6 %shard_map.106 = (f32[104,128]{1,0:T(8,128)}, f32[104,128]{1,0:T(8,128)}) custom-call(f32[256,128]{1,0:T(8,128)} %bitcast.37, f32[256,128]{1,0:T(8,128)} %bitcast.40, f32[24,128]{1,0:T(8,128)} %copy-done.11, f32[24,128]{1,0:T(8,128)} %copy-done.12), custom_call_target="tpu_custom_call" | custom-call | tf_op jit(solution)/shard_map/pallas_call | solution.py:317
  77.3 1.9 %collective-permute-done.1.amp_far = f32[16,16,256]{2,1,0:T(8,128)S(1)} collective-permute-done((f32[16,16,256]{2,1,0:T(8,128)S(1)}, f32[16,16,256]{2,1,0:T(8,128)S(1)}, u32[]{:S(2)}, u32[]{:S(2)}) %collective-permute-start.1) | collective-permute-done | bytes 262176 | tf_op jit(solution)/shard_map/ppermute | solution.py:354
  79.2 0.7 copy-done.3
  79.9 0.4 copy-done.1
  80.3 8.8 %shard_map.107 = f32[1024,128]{1,0:T(8,128)} custom-call(f32[2048,128]{1,0:T(8,128)} %bitcast.31, f32[16,2,16,256]{3,2,1,0:T(8,128)} %bitcast.29, f32[16,16,256]{2,1,0:T(8,128)} %copy-done.3, f32[16,256]{1,0:T(8,128)} %copy-done.6, f32[16,256]{1,0:T(8,128)} %copy-done.13, bf16[2,2,512,512]{3,2,1,0:T(8,128)(2,1)} %constant.29.clone.y_fwd, ...), custom_call_target="tpu_custom_call" | custom-call | tf_op jit(solution)/shard_map/pallas_call | solution.py:317
  89.1 10.9 %all-to-all-start.2 = ((f32[256,4,128]{2,1,0:T(4,128)}), f32[256,4,128]{2,1,0:T(4,128)S(1)}, u32[]{:S(2)}, u32[]{:S(2)}) async-start(f32[256,4,128]{2,1,0:T(4,128)} %bitcast.33), calls=%async_computation.2 | async-start | bytes 1048576 | tf_op jit(solution)/shard_map/all_to_all | solution.py:366
  100.0 8.1 %collective-permute-start.5 = (f32[104,128]{1,0:T(8,128)S(1)}, f32[104,128]{1,0:T(8,128)S(1)}, u32[]{:S(2)}, u32[]{:S(2)}) collective-permute-start(f32[104,128]{1,0:T(8,128)S(1)} %copy-done.10), channel_id=1, source_target_pairs={{0,1},{1,2},{2,3},{3,4},{4,5},{5,6},{6,7},{7,8},{8,9},{9,10},{10,1... | collective-permute-start | bytes 159752 | tf_op jit(solution)/shard_map/ppermute | solution.py:369
  108.2 1.3 collective-permute-start.6
  109.5 0.1 collective-permute-done.5.lo_halo
  109.6 10.4 %collective-permute-done.6.hi_halo = f32[104,128]{1,0:T(8,128)S(1)} collective-permute-done((f32[104,128]{1,0:T(8,128)S(1)}, f32[104,128]{1,0:T(8,128)S(1)}, u32[]{:S(2)}, u32[]{:S(2)}) %collective-permute-start.6) | collective-permute-done | bytes 53280 | tf_op jit(solution)/shard_map/ppermute | solution.py:368
  120.0 0.9 all-to-all-done.2
  120.9 0.8 copy-done.2
  121.7 2.4 %shard_map.108 = f32[640,128]{1,0:T(8,128)} custom-call(f32[1024,128]{1,0:T(8,128)} %bitcast.32, bf16[2,320,512]{2,1,0:T(8,128)(2,1)} %constant.32.clone.table, f32[104,128]{1,0:T(8,128)} %copy-done.4, f32[104,128]{1,0:T(8,128)} %copy-done.5), custom_call_target="tpu_custom_call" | custom-call | tf_op jit(solution)/shard_map/pallas_call | solution.py:317
  124.1 17.8 %all_to_all.42 = f32[8,80,128]{2,1,0:T(8,128)} all-to-all(f32[8,80,128]{2,1,0:T(8,128)} %bitcast.35), channel_id=1, replica_groups=mesh['ga'=8,'ba'=32] {'ga'}, dimensions={0} | all-to-all | bytes 655360 | tf_op jit(solution)/shard_map/all_to_all | solution.py:371
  142.0 2.5 %shard_map.109 = (f32[256,128]{1,0:T(8,128)}, f32[256,128]{1,0:T(8,128)}) custom-call(f32[640,128]{1,0:T(8,128)} %bitcast.34, f32[256,128]{1,0:T(8,128)} %bitcast.38, f32[256,128]{1,0:T(8,128)} %bitcast.41, f32[104,128]{1,0:T(8,128)} %copy-done.4, f32[104,128]{1,0:T(8,128)} %copy-done.5, f32[24,128]{1,0:T(8,128)} %copy-done.11, f32[24,128]{1,0:T(8,128)} %copy-done.12), custom_call_target="tpu_custom_call" | custom-call | tf_op jit(solution)/shard_map/pallas_call | solution.py:317
  (30 shorter events, 0.1 us)
Async XLA Ops:
  1.6 0.7 copy-start.7
  1.6 0.7 collective-permute-start
  2.3 0.6 copy-start.6
  6.0 16.6 %all-to-all-start.1 = ((f32[16,32,256]{2,1,0:T(8,128)}), f32[16,32,256]{2,1,0:T(8,128)S(1)}, u32[]{:S(2)}, u32[]{:S(2)}) async-start(f32[16,32,256]{2,1,0:T(8,128)} %bitcast.43), calls=%async_computation.1 | async-start | bytes 1048576 | tf_op jit(solution)/shard_map/all_to_all | solution.py:351
  17.2 29.3 %copy-start.8 = (f32[16,1,256]{2,0,1:T(8,128)S(1)}, f32[16,1,256]{2,0,1:T(8,128)}, u32[]{:S(2)}) copy-start(f32[16,1,256]{2,0,1:T(8,128)} %copy-done.7) | copy-start | bytes 49156
  17.3 30.6 %copy-start.15 = (f32[24,128]{1,0:T(8,128)S(1)}, f32[24,128]{1,0:T(8,128)}, u32[]{:S(2)}) copy-start(f32[24,128]{1,0:T(8,128)} %get-tuple-element.10) | copy-start | bytes 36868
  17.3 33.6 %copy-start.14 = (f32[24,128]{1,0:T(8,128)S(1)}, f32[24,128]{1,0:T(8,128)}, u32[]{:S(2)}) copy-start(f32[24,128]{1,0:T(8,128)} %get-tuple-element.11) | copy-start | bytes 36868
  22.5 56.7 %copy-start = (f32[16,32,256]{2,1,0:T(8,128)}, f32[16,32,256]{2,1,0:T(8,128)S(1)}, u32[]{:S(2)}) copy-start(f32[16,32,256]{2,1,0:T(8,128)S(1)} %all-to-all-done.1) | copy-start | bytes 1572868
  22.5 56.6 %all-to-all-start = ((f32[256,8,128]{2,1,0:T(8,128)}), f32[256,8,128]{2,1,0:T(8,128)S(1)}, u32[]{:S(2)}, u32[]{:S(2)}) async-start(f32[256,8,128]{2,1,0:T(8,128)} %bitcast.30), calls=%async_computation | async-start | bytes 2097152 | tf_op jit(solution)/shard_map/all_to_all | solution.py:342
  40.2 38.9 %collective-permute-start.1 = (f32[16,16,256]{2,1,0:T(8,128)S(1)}, f32[16,16,256]{2,1,0:T(8,128)S(1)}, u32[]{:S(2)}, u32[]{:S(2)}) collective-permute-start(f32[16,16,256]{2,1,0:T(8,128)S(1)} %fusion.1), channel_id=1, source_target_pairs={{0,1},{1,0},{2,3},{3,2},{4,5},{5,4},{6,7},{7,6},{8,9},{9,8},{10,11... | collective-permute-start | bytes 786440 | tf_op jit(solution)/shard_map/ppermute | solution.py:354
  46.5 30.8 %collective-permute-start.2 = (f32[16,256]{1,0:T(8,128)S(1)}, f32[16,256]{1,0:T(8,128)S(1)}, u32[]{:S(2)}, u32[]{:S(2)}) collective-permute-start(f32[16,256]{1,0:T(8,128)S(1)} %bitcast.46), channel_id=1, source_target_pairs={{16,0},{48,32},{80,64},{112,96},{144,128},{176,160},{208,192},{240... | collective-permute-start | bytes 49160 | tf_op jit(solution)/shard_map/ppermute | solution.py:345
  47.8 16.5 %collective-permute-start.3 = (f32[24,128]{1,0:T(8,128)S(1)}, f32[24,128]{1,0:T(8,128)S(1)}, u32[]{:S(2)}, u32[]{:S(2)}) collective-permute-start(f32[24,128]{1,0:T(8,128)S(1)} %copy-done.15), channel_id=1, source_target_pairs={{0,32},{32,64},{64,96},{96,128},{128,160},{160,192},{192,224},{1,3... | collective-permute-start | bytes 36872 | tf_op jit(solution)/shard_map/ppermute | solution.py:356
  50.8 24.2 %collective-permute-start.4 = (f32[24,128]{1,0:T(8,128)S(1)}, f32[24,128]{1,0:T(8,128)S(1)}, u32[]{:S(2)}, u32[]{:S(2)}) collective-permute-start(f32[24,128]{1,0:T(8,128)S(1)} %copy-done.14), channel_id=1, source_target_pairs={{32,0},{64,32},{96,64},{128,96},{160,128},{192,160},{224,192},{33,... | collective-permute-start | bytes 36872 | tf_op jit(solution)/shard_map/ppermute | solution.py:357
  64.3 10.8 %copy-start.11 = (f32[24,128]{1,0:T(8,128)}, f32[24,128]{1,0:T(8,128)S(1)}, u32[]{:S(2)}) copy-start(f32[24,128]{1,0:T(8,128)S(1)} %collective-permute-done.3.lo_x) | copy-start | bytes 36868
  75.1 0.6 copy-start.12
  77.3 1.9 %copy-start.13 = (f32[16,256]{1,0:T(8,128)}, f32[16,256]{1,0:T(8,128)S(1)}, u32[]{:S(2)}) copy-start(f32[16,256]{1,0:T(8,128)S(1)} %collective-permute-done.2.amp_row256) | copy-start | bytes 49156
  79.2 0.7 copy-start.3
  79.2 1.1 copy-start.1
  80.3 19.7 %copy-start.10 = (f32[104,128]{1,0:T(8,128)S(1)}, f32[104,128]{1,0:T(8,128)}, u32[]{:S(2)}) copy-start(f32[104,128]{1,0:T(8,128)} %get-tuple-element.13.above) | copy-start | bytes 159748
  80.3 27.9 %copy-start.9 = (f32[104,128]{1,0:T(8,128)S(1)}, f32[104,128]{1,0:T(8,128)}, u32[]{:S(2)}) copy-start(f32[104,128]{1,0:T(8,128)} %get-tuple-element.12.below) | copy-start | bytes 159748
  89.1 31.8 %all-to-all-start.2 = ((f32[256,4,128]{2,1,0:T(4,128)}), f32[256,4,128]{2,1,0:T(4,128)S(1)}, u32[]{:S(2)}, u32[]{:S(2)}) async-start(f32[256,4,128]{2,1,0:T(4,128)} %bitcast.33), calls=%async_computation.2 | async-start | bytes 1048576 | tf_op jit(solution)/shard_map/all_to_all | solution.py:366
  100.0 9.6 %collective-permute-start.5 = (f32[104,128]{1,0:T(8,128)S(1)}, f32[104,128]{1,0:T(8,128)S(1)}, u32[]{:S(2)}, u32[]{:S(2)}) collective-permute-start(f32[104,128]{1,0:T(8,128)S(1)} %copy-done.10), channel_id=1, source_target_pairs={{0,1},{1,2},{2,3},{3,4},{4,5},{5,6},{6,7},{7,8},{8,9},{9,10},{10,1... | collective-permute-start | bytes 159752 | tf_op jit(solution)/shard_map/ppermute | solution.py:369
  108.2 11.8 %collective-permute-start.6 = (f32[104,128]{1,0:T(8,128)S(1)}, f32[104,128]{1,0:T(8,128)S(1)}, u32[]{:S(2)}, u32[]{:S(2)}) collective-permute-start(f32[104,128]{1,0:T(8,128)S(1)} %copy-done.9), channel_id=1, source_target_pairs={{1,0},{2,1},{3,2},{4,3},{5,4},{6,5},{7,6},{8,7},{9,8},{10,9},{11,1... | collective-permute-start | bytes 159752 | tf_op jit(solution)/shard_map/ppermute | solution.py:368
  109.6 11.3 %copy-start.4 = (f32[104,128]{1,0:T(8,128)}, f32[104,128]{1,0:T(8,128)S(1)}, u32[]{:S(2)}) copy-start(f32[104,128]{1,0:T(8,128)S(1)} %collective-permute-done.5.lo_halo) | copy-start | bytes 159748
  120.0 0.9 copy-start.5
  120.9 0.8 copy-start.2

commit v5 on v4

--- a/solution.py
+++ b/solution.py
@@ -18,6 +18,7 @@
 XROWS = 40
 CHUNK = 2 * XROWS
 VMEM = 60 * 2**20
+VMEM_END = 16 * 2**20
 f32, bf16 = jnp.float32, jnp.bfloat16
 
 
@@ -90,7 +91,7 @@
     return copies
 
 
-def enter_kernel(noise, table, sent, noise_in, table_in, rows_out, sems):
+def enter_kernel(noise, table, after, sent, noise_in, table_in, rows_out, sems):
     pairs = [(table, table_in), (noise.at[0:256, :], noise_in.at[0:256, :]),
              (noise.at[256:512, :], noise_in.at[256:512, :])]
     copies = fetch(pairs, sems)
@@ -107,13 +108,12 @@
     pltpu.sync_copy(rows_out, sent)
 
 
-def edges_kernel(amp, amp_first, amp_zero, head, rech, amp_sent, up, down, amp_in, sems):
+def edges_kernel(amp, amp_first, amp_zero, head, rech, amp_sent, below, above, amp_in, sems):
     ga, ba = lax.axis_index("ga"), lax.axis_index("ba")
     (copy,) = fetch([(amp.at[:, 0:40, :], amp_in)], sems)
-    for out, far, near in ((up, 30, 31), (down, 1, 0)):
-        out[0:8, :] = head[8 * far : 8 * far + 8, :]
-        out[8:16, :] = head[8 * near : 8 * near + 8, :]
-        out[16:24, :] = rech[8 * near : 8 * near + 8, :]
+    for out, near, far in ((below, 0, 1), (above, 7, 6)):
+        for i, (ref, y) in enumerate(((head, near), (head, far), (rech, near))):
+            out[32 * i : 32 * i + 32, :] = ref[pl.ds(y, 32, stride=8), :]
     copy.wait()
     zero = (ga == PACKED_GA) & (ba >= BA // 2)
     for half in range(2):
@@ -122,6 +122,10 @@
         amp_sent[0:16, lanes] = jnp.where(ga < PACKED_GA, amp_in[:, 32, lanes], first)
         for b in range(1, BA):
             amp_sent[16 * b : 16 * b + 16, lanes] = amp_in[:, b, lanes]
+
+
+def gate_kernel(amp_sent, got, lo_halo, hi_halo, same):
+    pass
 
 
 def mirror_of(value):
@@ -140,15 +144,8 @@
     return total
 
 
-def middle_kernel(got, amp_near, amp_far, amp_row0, amp_row256, y_fwd, z_fwd, z_inv, below, above, sent,
-                  got_in, amp_in, y_fwd_in, z_fwd_in, z_inv_in, row0_in, row256_in,
-                  rows, lines, amps, sems):
-    ga, ba = lax.axis_index("ga"), lax.axis_index("ba")
-    packed = (ga == PACKED_GA) & (ba == 0)
-    side = lax.rem(ba, 2)
-    pairs = [(got, got_in), (y_fwd, y_fwd_in), (z_fwd, z_fwd_in), (amp_near.at[:, side], amp_in.at[:, side]),
-             (amp_far, amp_in.at[:, 1 - side]), (z_inv, z_inv_in), (amp_row0, row0_in), (amp_row256, row256_in)]
-    copies = fetch(pairs, sems)
+def forward_kernel(got, y_fwd, z_fwd, spectrum, got_in, y_fwd_in, z_fwd_in, rows, held, sems):
+    copies = fetch([(got, got_in), (y_fwd, y_fwd_in), (z_fwd, z_fwd_in)], sems)
     copies[0].wait()
     low_half = lax.broadcasted_iota(jnp.int32, (BA, 128), 1) < 64
     for c in range(2):
@@ -163,18 +160,7 @@
                     high, low = split(value)
                     rows[0, at, 128 * p : 128 * p + 128] = high
                     rows[1, at, 128 * p : 128 * p + 128] = low
-    for i in (3, 4, 6, 7):
-        copies[i].wait()
-
-    @pl.when(packed)
-    def _():
-        held = amp_in[...].reshape(EY, EZ)
-        mirror = mirror_of(held)
-        ky = lax.broadcasted_iota(jnp.int32, (EY, EZ), 0)
-        amps[...] = jnp.where(ky == 0, row0_in[0:1, :], jnp.where(ky < 256, mirror, held))
-        new = jnp.where(ky == 256, row256_in[0:1, :], jnp.where(ky < 256, held, mirror))
-        amp_in[...] = new.reshape(amp_in.shape)
-
+    leaving = []
     for part in range(2):
         ky = slice(256 * part, 256 * part + 256)
         data = (rows[0], rows[1])
@@ -186,10 +172,40 @@
         imag = by_cos[:, 256:] - by_sin[:, :256]
         if part == 0:
             copies[2].wait()
-            copies[5].wait()
         forward = (z_fwd_in[0], z_fwd_in[1])
         real, imag = dot3(split(real), forward), dot3(split(imag), forward)
         real, imag = real[:, :256] + imag[:, 256:], imag[:, :256] - real[:, 256:]
+
+        held[0, ky, :] = real
+        held[1, ky, :] = imag
+        leaving += fetch([(held.at[:, ky, :], spectrum.at[:, ky, :])], sems.at[pl.ds(3 + part, 1)])
+    for copy in leaving:
+        copy.wait()
+
+
+def inverse_kernel(spectrum, amp, amp_row0, amp_row256, z_inv, y_fwd, up, down, sent,
+                   spectrum_in, amp_in, y_fwd_in, z_inv_in, row0_in, row256_in, lines, amps, sems):
+    ga, ba = lax.axis_index("ga"), lax.axis_index("ba")
+    packed = (ga == PACKED_GA) & (ba == 0)
+    pairs = [(amp, amp_in), (amp_row0, row0_in), (amp_row256, row256_in), (spectrum, spectrum_in), (z_inv, z_inv_in),
+             (y_fwd.at[:, :, 0:256, :], y_fwd_in)]
+    copies = fetch(pairs, sems)
+    for i in range(3):
+        copies[i].wait()
+
+    @pl.when(packed)
+    def _():
+        held = amp_in[...]
+        mirror = mirror_of(held)
+        ky = lax.broadcasted_iota(jnp.int32, (EY, EZ), 0)
+        amps[...] = jnp.where(ky == 0, row0_in[0:1, :], jnp.where(ky < 256, mirror, held))
+        amp_in[...] = jnp.where(ky == 256, row256_in[0:1, :], jnp.where(ky < 256, held, mirror))
+
+    copies[3].wait()
+    copies[4].wait()
+    for part in range(2):
+        ky = slice(256 * part, 256 * part + 256)
+        real, imag = spectrum_in[0, ky, :], spectrum_in[1, ky, :]
 
         def back(scale, at):
             table = (z_inv_in[0], z_inv_in[1])
@@ -198,7 +214,7 @@
                 lanes = slice(128 * c, 128 * c + 128)
                 lines[at, 0, ky, lanes], lines[at, 1, ky, lanes] = split(value)
 
-        back(amp_in[8 * part : 8 * part + 8].reshape(256, EZ), 0)
+        back(amp_in[ky, :], 0)
 
         @pl.when(packed)
         def _():
@@ -206,9 +222,8 @@
 
     def inverse(at):
         data = (lines[at, 0], lines[at, 1])
-        near = slice(0, AY)
-        by_cos = dot3((y_fwd_in[0, 0, near, :], y_fwd_in[1, 0, near, :]), data)
-        by_sin = dot3((y_fwd_in[0, 1, near, :], y_fwd_in[1, 1, near, :]), data)
+        by_cos = dot3((y_fwd_in[0, 0], y_fwd_in[1, 0]), data)
+        by_sin = dot3((y_fwd_in[0, 1], y_fwd_in[1, 1]), data)
         return by_cos[:, :AZ] - by_sin[:, AZ:], by_cos[:, AZ:] + by_sin[:, :AZ]
 
     def store(c, own):
@@ -218,6 +233,7 @@
         sent[pl.ds(c, AY, stride=4), :] = own
         sent[pl.ds(2 + c, AY, stride=4), :] = jnp.where(forward_halo, after, before)
 
+    copies[5].wait()
     real, imag = inverse(0)
     store(0, real)
     store(1, imag)
@@ -227,19 +243,22 @@
         store(1, inverse(1)[1])
 
 
-def pack_kernel(head, rech, lo_x, hi_x, below, above):
+def pack_kernel(head, rech, lo_halo, hi_halo, up, down):
     corner = lax.broadcasted_iota(jnp.int32, (8, AZ), 0)
-    for out, near, far in ((below, 0, 1), (above, 7, 6)):
-        for i, (ref, y) in enumerate(((head, near), (head, far), (rech, near))):
-            out[32 * i : 32 * i + 32, :] = ref[pl.ds(y, 32, stride=8), :]
-        out[96:104, :] = jnp.where(corner == 0, lo_x[8 + near : 9 + near, :], hi_x[8 + near : 9 + near, :])
-
-
-def field_kernel(got, table, lo_halo, hi_halo, sent):
+    for out, far, near in ((up, 30, 31), (down, 1, 0)):
+        out[0:8, :] = head[8 * far : 8 * far + 8, :]
+        out[8:16, :] = head[8 * near : 8 * near + 8, :]
+        out[16:24, :] = rech[8 * near : 8 * near + 8, :]
+        out[24:32, :] = jnp.where(corner == 0, lo_halo[near : near + 1, :], hi_halo[near : near + 1, :])
+
+
+def field_kernel(got, table, lo_x, hi_x, sent, table_in, sems):
+    (copy,) = fetch([(table, table_in)], sems)
     ga, ba = lax.axis_index("ga"), lax.axis_index("ba")
     own = jnp.concatenate([got[pl.ds(c, DEVS, stride=4), :] for c in range(2)], 0)
     halo = jnp.concatenate([got[pl.ds(2 + c, DEVS, stride=4), :] for c in range(2)], 0)
-    log_field = dot3((table[0], table[1]), split(jnp.concatenate([own, halo], 1)))
+    copy.wait()
+    log_field = dot3((table_in[0], table_in[1]), split(jnp.concatenate([own, halo], 1)))
     row = lax.broadcasted_iota(jnp.int32, (XROWS, AZ), 0)
     halo_inside = jnp.where(ga < GA // 2, ba < BA - 1, ba > 0)
     for g in range(GA):
@@ -269,9 +288,8 @@
             head_ext[at + far : at + far + 1, :] = block[y : y + 1, :]
             head_ext[at + near : at + near + 1, :] = block[8 + y : 9 + y, :]
             rech_ext[at + near : at + near + 1, :] = block[16 + y : 17 + y, :]
-    for halo, y in ((lo_halo, 1), (hi_halo, 10)):
-        for i, near in enumerate((3, 36)):
-            head_ext[XROWS * y + near : XROWS * y + near + 1, :] = halo[96 + i : 97 + i, :]
+        head_ext[XROWS + near : XROWS + near + 1, :] = block[24:25, :]
+        head_ext[10 * XROWS + near : 10 * XROWS + near + 1, :] = block[25:26, :]
 
     lane = lax.broadcasted_iota(jnp.int32, (XROWS, AZ), 1)
     row = lax.broadcasted_iota(jnp.int32, (XROWS, AZ), 0)
@@ -311,16 +329,18 @@
         press_out[pl.ds(y, 32, stride=8), :] = staged[4:36, :]
 
 
-def kernel_call(kernel, outs, inputs, scratch=(), held=(), outs_held=()):
-    vmem = pl.BlockSpec(memory_space=pltpu.VMEM)
+def kernel_call(kernel, outs, inputs, scratch=(), held=(), outs_held=(), vmem=VMEM, flops=0, aliases=None):
+    whole = pl.BlockSpec(memory_space=pltpu.VMEM)
     there = pl.BlockSpec(memory_space=pl.ANY)
     return pl.pallas_call(
         kernel,
         out_shape=[jax.ShapeDtypeStruct(shape, f32) for shape in outs],
-        in_specs=[there if i in held else vmem for i in range(len(inputs))],
-        out_specs=[there if i in outs_held else vmem for i in range(len(outs))],
+        in_specs=[there if i in held else whole for i in range(len(inputs))],
+        out_specs=[there if i in outs_held else whole for i in range(len(outs))],
         scratch_shapes=list(scratch),
-        compiler_params=pltpu.CompilerParams(vmem_limit_bytes=VMEM),
+        input_output_aliases=aliases or {},
+        compiler_params=pltpu.CompilerParams(vmem_limit_bytes=vmem),
+        cost_estimate=pl.CostEstimate(flops=flops, bytes_accessed=6 * 2**20, transcendentals=0) if flops else None,
     )(*inputs)
 
 
@@ -334,46 +354,55 @@
     recharge = recharge.reshape(256, AZ)
     head = head_guess.reshape(256, AZ)
     memory, sems = pltpu.VMEM, pltpu.SemaphoreType.DMA
-    (sent,) = kernel_call(
-        enter_kernel, [(8 * DEVS, 128)], [noise.reshape(512, EX), x_fwd],
-        [memory((512, EX), f32), memory(x_fwd.shape, bf16), memory((8 * DEVS, 128), f32), sems((3,))],
-        held=(0, 1), outs_held=(0,),
-    )
-    got = lax.all_to_all(sent, ("ba", "ga"), 0, 0, tiled=True)
     amp_first = amplitude[:, 0, :]
     amp_zero = lax.ppermute(amp_first, "ga", [(0, PACKED_GA)])
     amp_row = lax.ppermute(amp_first, "ba", [(BA // 2, 0)])
-    amp_sent, to_up, to_down = kernel_call(
-        edges_kernel, [(512, EZ), (24, AZ), (24, AZ)], [amplitude, amp_first, amp_zero, head, recharge],
+    (sent,) = kernel_call(
+        enter_kernel, [(8 * DEVS, 128)], [noise.reshape(512, EX), x_fwd, amp_zero],
+        [memory((512, EX), f32), memory(x_fwd.shape, bf16), memory((8 * DEVS, 128), f32), sems((3,))],
+        held=(0, 1, 2), outs_held=(0,), flops=10**9,
+    )
+    got = lax.all_to_all(sent, ("ba", "ga"), 0, 0, tiled=True)
+    amp_sent, below, above = kernel_call(
+        edges_kernel, [(512, EZ), (96, AZ), (96, AZ)], [amplitude, amp_first, amp_zero, head, recharge],
         [memory((16, 40, EZ), f32), sems((1,))], held=(0,),
     )
-    halves = [list(range(side, BA, 2)) for side in range(2)]
-    amp_near = lax.all_to_all(amp_sent, "ba", 0, 0, tiled=True, axis_index_groups=halves)
-    amp_near = amp_near.reshape(BA // 2, 2, 16, EZ)
-    give = jnp.where(lax.axis_index("ba") % 2 == 0, amp_near[:, 1], amp_near[:, 0])
-    amp_far = lax.ppermute(give, "ba", [(i, i ^ 1) for i in range(BA)])
+    up, down = steps("ba")
+    hi_halo = lax.ppermute(below, "ba", down)
+    lo_halo = lax.ppermute(above, "ba", up)
+    (amp_sent,) = kernel_call(
+        gate_kernel, [(512, EZ)], [amp_sent, got, lo_halo, hi_halo], held=range(4), outs_held=(0,), aliases={0: 0}
+    )
+    amp = lax.all_to_all(amp_sent, "ba", 0, 0, tiled=True)
+    (spectrum,) = kernel_call(
+        forward_kernel, [(2, EY, EZ)], [got, y_fwd, z_fwd],
+        [memory(value.shape, value.dtype) for value in (got, y_fwd, z_fwd)]
+        + [memory((2, 512, 512), bf16), memory((2, EY, EZ), f32), sems((5,))],
+        held=range(3), outs_held=(0,), flops=3 * 10**9,
+    )
+    to_up, to_down = kernel_call(pack_kernel, [(32, AZ), (32, AZ)], [head, recharge, lo_halo, hi_halo])
+    plane = (EY, EZ)
+    (sent,) = kernel_call(
+        inverse_kernel, [(4 * AY, AZ)],
+        [spectrum, amp, amp_zero, amp_row, z_inv, y_fwd, to_up, to_down],
+        [memory((2, EY, EZ), f32), memory(plane, f32), memory((2, 2, AY, EY), bf16), memory(z_inv.shape, bf16)]
+        + [memory((16, EZ), f32)] * 2 + [memory((2, 2, EY, 2 * AZ), bf16), memory(plane, f32), sems((6,))],
+        held=range(8),
+    )
+    got = lax.all_to_all(sent, ("ba", "ga"), 0, 0, tiled=True)
     up, down = steps("ga")
     lo_x = lax.ppermute(to_up, "ga", up)
     hi_x = lax.ppermute(to_down, "ga", down)
-    below, above = kernel_call(pack_kernel, [(104, AZ), (104, AZ)], [head, recharge, lo_x, hi_x])
-    inputs = [got, amp_near, amp_far, amp_zero, amp_row, y_fwd, z_fwd, z_inv, below, above]
     (sent,) = kernel_call(
-        middle_kernel, [(4 * AY, AZ)], inputs,
-        [memory(value.shape, value.dtype) for value in (got, amp_near, y_fwd, z_fwd, z_inv, amp_zero, amp_row)]
-        + [memory((2, 512, 512), bf16), memory((2, 2, EY, 2 * AZ), bf16), memory((EY, EZ), f32), sems((8,))],
-        held=range(10),
-    )
-    got = lax.all_to_all(sent, ("ba", "ga"), 0, 0, tiled=True)
-    up, down = steps("ba")
-    hi_halo = lax.ppermute(below, "ba", down)
-    lo_halo = lax.ppermute(above, "ba", up)
-    (sent,) = kernel_call(field_kernel, [(CHUNK * GA, AZ)], [got, x_inv, lo_halo, hi_halo], held=(2, 3))
+        field_kernel, [(CHUNK * GA, AZ)], [got, x_inv, lo_x, hi_x],
+        [memory(x_inv.shape, bf16), sems((1,))], held=(1, 2, 3), vmem=VMEM_END,
+    )
     got = lax.all_to_all(sent, "ga", 0, 0, tiled=True)
     ext = pltpu.VMEM((12 * XROWS, AZ), f32)
     conductivity, pressure = kernel_call(
         sweep_kernel, [(256, AZ), (256, AZ)],
         [got, head, recharge, lo_halo, hi_halo, lo_x, hi_x],
-        [ext, ext, pltpu.VMEM((XROWS, AZ), f32)],
+        [ext, ext, pltpu.VMEM((XROWS, AZ), f32)], vmem=VMEM_END,
     )
     return conductivity.reshape(32, 8, AZ), pressure.reshape(32, 8, AZ)
 

time: 145 us -> 138 us (0.952)
  blocking collectives: 17.8 us -> 13.1 us
    ppermute x1, waiting for transfers between devices: 11.6 us -> 0.01 us  [body(): lo_x = lax.ppermute(to_up, 'ga', up)]
    all_to_all x2, waiting for transfers between devices: 0.91 us -> 9.4 us  [body(): got = lax.all_to_all(sent, ('ba', 'ga'), 0, 0, tiled=True)]
    ppermute x1 -> x0, starting transfers between devices: 6.31 us -> none  [body(): amp_far = lax.ppermute(give, 'ba', [(i, i ^ 1) for i in range(BA)])]
    all_to_all x2, starting transfers between devices: 28.5 us -> 34.5 us  [body(): got = lax.all_to_all(sent, ('ba', 'ga'), 0, 0, tiled=True)]
    ppermute x1, waiting for transfers between devices: 10.4 us -> 15.6 us  [body(): hi_halo = lax.ppermute(below, 'ba', down)]
    all_to_all x1, blocking collectives: 17.8 us -> 13.1 us  [body(): got = lax.all_to_all(sent, 'ga', 0, 0, tiled=True)]
    ppermute x1, waiting for transfers between devices: 10.8 us -> 6.86 us  [body(): hi_x = lax.ppermute(to_down, 'ga', down)]
    ppermute x1, waiting for transfers between devices: 0.14 us -> 2.74 us  [body(): lo_halo = lax.ppermute(above, 'ba', up)]
  transfers between devices with their start and end apart: 10 -> 9, of which waited for: 7 -> 6; matrix products, arithmetic and copies ran while one was open for 0% -> 0% of each run, Pallas kernels for 4% -> 8%
where the time goes in v5:
time: 138 us
  starting transfers between devices  59.6 us (43%)
  waiting for transfers between devices  40 us (29%)
  Pallas kernels  20.8 us (15%)
  blocking collectives  13.1 us (9%)
  local copies, waits for them, and re-layouts  3.39 us (2%)
    all_to_all x2, starting transfers between devices, body(): got = lax.all_to_all(sent, ('ba', 'ga'), 0, 0, tiled=True)  34.5 us
    pallas_call x8, Pallas kernels, kernel_call(): pl.pallas_call(kernel, out_shape=[jax.ShapeDtypeStruct(shape, f32) for sh...  20.8 us
    ppermute x1, waiting for transfers between devices, body(): hi_halo = lax.ppermute(below, 'ba', down)  15.6 us
    all_to_all x1, blocking collectives, body(): got = lax.all_to_all(sent, 'ga', 0, 0, tiled=True)  13.1 us
    all_to_all x2, waiting for transfers between devices, body(): got = lax.all_to_all(sent, ('ba', 'ga'), 0, 0, tiled=True)  9.4 us
    ppermute x1, starting transfers between devices, body(): lo_halo = lax.ppermute(above, 'ba', up)  8.13 us
    all_to_all x1, starting transfers between devices, body(): amp = lax.all_to_all(amp_sent, 'ba', 0, 0, tiled=True)  8.11 us
    ppermute x1, waiting for transfers between devices, body(): hi_x = lax.ppermute(to_down, 'ga', down)  6.86 us
  transfers between devices with their start and end apart: 9, of which 6 were waited for; matrix products, arithmetic and copies ran while one was open for 0% of the time, Pallas kernels for 8%

profile of v5, /device:TPU:1, one launch (start us, length us, event | category | flops | bytes accessed | tf_op | source)
XLA Modules:
  0.0 137.7 jit_solution(17785034324869410740)
XLA Ops:
  0.6 0.9 slice.3
  1.6 0.7 collective-permute-start
  2.3 0.6 copy-done.9
  2.8 3.7 %shard_map.104 = f32[2048,128]{1,0:T(8,128)} custom-call(f32[512,512]{1,0:T(8,128)} %bitcast.34, bf16[2,512,512]{2,1,0:T(8,128)(2,1)} %constant.10.clone.table, f32[16,256]{1,0:T(8,128)} %copy-done.9), custom_call_target="tpu_custom_call" | custom-call | flops 1000000000 | bytes 6291456 | tf_op jit(solution)/shard_map/pallas_call | solution.py:335
  6.6 20.6 %all-to-all-start = ((f32[256,8,128]{2,1,0:T(8,128)}), f32[256,8,128]{2,1,0:T(8,128)S(1)}, u32[]{:S(2)}, u32[]{:S(2)}) async-start(f32[256,8,128]{2,1,0:T(8,128)} %bitcast.30), calls=%async_computation | async-start | bytes 2097152 | tf_op jit(solution)/shard_map/all_to_all | solution.py:365
  27.2 3.1 %shard_map.106 = (f32[512,256]{1,0:T(8,128)}, f32[96,128]{1,0:T(8,128)}, f32[96,128]{1,0:T(8,128)}) custom-call(f32[16,64,256]{2,1,0:T(8,128)} %amp.1, f32[16,256]{1,0:T(8,128)} %bitcast.32, f32[16,256]{1,0:T(8,128)} %copy-done.9, f32[256,128]{1,0:T(8,128)} %bitcast.19, f32[256,128]{1,0:T(8,128)} %bitcast.22), custom_call_target="tpu_custom_call" | custom-call | tf_op jit(solution)/shard_map/pallas_call | solution.py:335
  30.4 8.1 %collective-permute-start.1 = (f32[96,128]{1,0:T(8,128)}, f32[96,128]{1,0:T(8,128)S(1)}, u32[]{:S(2)}, u32[]{:S(2)}) collective-permute-start(f32[96,128]{1,0:T(8,128)} %get-tuple-element.10), channel_id=1, source_target_pairs={{0,1},{1,2},{2,3},{3,4},{4,5},{5,6},{6,7},{7,8},{8,9},{9,10},{10,1... | collective-permute-start | bytes 147464 | tf_op jit(solution)/shard_map/ppermute | solution.py:372
  38.5 1.3 collective-permute-start.2
  39.8 2.7 %collective-permute-done.1.lo_halo = f32[96,128]{1,0:T(8,128)S(1)} collective-permute-done((f32[96,128]{1,0:T(8,128)}, f32[96,128]{1,0:T(8,128)S(1)}, u32[]{:S(2)}, u32[]{:S(2)}) %collective-permute-start.1) | collective-permute-done | bytes 49184 | tf_op jit(solution)/shard_map/ppermute | solution.py:372
  42.6 15.6 %collective-permute-done.2.hi_halo = f32[96,128]{1,0:T(8,128)S(1)} collective-permute-done((f32[96,128]{1,0:T(8,128)}, f32[96,128]{1,0:T(8,128)S(1)}, u32[]{:S(2)}, u32[]{:S(2)}) %collective-permute-start.2) | collective-permute-done | bytes 49184 | tf_op jit(solution)/shard_map/ppermute | solution.py:371
  58.1 0.4 all-to-all-done
  58.5 0.2 copy-done.5
  58.8 0.8 copy-done.7
  59.6 8.1 %all-to-all-start.1 = ((f32[32,16,256]{2,1,0:T(8,128)}), f32[32,16,256]{2,1,0:T(8,128)S(1)}, u32[]{:S(2)}, u32[]{:S(2)}) async-start(f32[32,16,256]{2,1,0:T(8,128)} %bitcast.29), calls=%async_computation.1 | async-start | bytes 1048576 | tf_op jit(solution)/shard_map/all_to_all | solution.py:376
  67.7 1.3 collective-permute-start.3
  69.0 1.6 %shard_map.108 = (f32[32,128]{1,0:T(8,128)}, f32[32,128]{1,0:T(8,128)}) custom-call(f32[256,128]{1,0:T(8,128)} %bitcast.20, f32[256,128]{1,0:T(8,128)} %bitcast.23, f32[96,128]{1,0:T(8,128)} %copy-done.3, f32[96,128]{1,0:T(8,128)} %copy-done.5), custom_call_target="tpu_custom_call" | custom-call | tf_op jit(solution)/shard_map/pallas_call | solution.py:335
  70.6 6.6 %shard_map.105.spectrum = f32[2,512,256]{2,1,0:T(8,128)} custom-call(f32[2048,128]{1,0:T(8,128)} %bitcast.26, bf16[2,2,512,512]{3,2,1,0:T(8,128)(2,1)} %constant.11.clone.y_fwd, bf16[2,256,512]{2,1,0:T(8,128)(2,1)} %constant.12.clone.z_fwd), custom_call_target="tpu_custom_call" | custom-call | flops 3000000000 | bytes 6291456 | tf_op jit(solution)/shard_map/pallas_call | solution.py:335
  77.2 5.4 %all-to-all-done.1 = f32[32,16,256]{2,1,0:T(8,128)S(1)} async-done(((f32[32,16,256]{2,1,0:T(8,128)}), f32[32,16,256]{2,1,0:T(8,128)S(1)}, u32[]{:S(2)}, u32[]{:S(2)}) %all-to-all-start.1) | async-done | bytes 524320 | tf_op jit(solution)/shard_map/all_to_all | solution.py:376
  82.6 0.8 copy-done.8
  83.4 3.7 %shard_map.109 = f32[1024,128]{1,0:T(8,128)} custom-call(f32[2,512,256]{2,1,0:T(8,128)} %shard_map.105.spectrum, f32[512,256]{1,0:T(8,128)} %bitcast.27, f32[16,256]{1,0:T(8,128)} %copy-done.9, f32[16,256]{1,0:T(8,128)} %copy-done.14, bf16[2,256,256]{2,1,0:T(8,128)(2,1)} %constant.13.clone.z_inv, bf16[2,2,512,512]{3,2,1,0:T(8,128)(2,1)} %constant.11.clone.y_fwd, ...), custom_call_target="tpu_custom_call" | custom-call | tf_op jit(solution)/shard_map/pallas_call | solution.py:335
  87.2 0.0 copy-start
  87.2 0.0 copy-start.1
  87.2 0.0 copy-start.4
  87.2 0.0 copy-start.6
  87.2 13.8 %all-to-all-start.2 = ((f32[256,4,128]{2,1,0:T(4,128)}), f32[256,4,128]{2,1,0:T(4,128)S(1)}, u32[]{:S(2)}, u32[]{:S(2)}) async-start(f32[256,4,128]{2,1,0:T(4,128)} %bitcast.28), calls=%async_computation.2 | async-start | bytes 1048576 | tf_op jit(solution)/shard_map/all_to_all | solution.py:392
  101.1 3.7 %collective-permute-start.4 = (f32[32,128]{1,0:T(8,128)S(1)}, f32[32,128]{1,0:T(8,128)S(1)}, u32[]{:S(2)}, u32[]{:S(2)}) collective-permute-start(f32[32,128]{1,0:T(8,128)S(1)} %copy-done.13), channel_id=1, source_target_pairs={{0,32},{32,64},{64,96},{96,128},{128,160},{160,192},{192,224},{1,3... | collective-permute-start | bytes 49160 | tf_op jit(solution)/shard_map/ppermute | solution.py:394
  104.7 1.9 %collective-permute-start.5 = (f32[32,128]{1,0:T(8,128)S(1)}, f32[32,128]{1,0:T(8,128)S(1)}, u32[]{:S(2)}, u32[]{:S(2)}) collective-permute-start(f32[32,128]{1,0:T(8,128)S(1)} %copy-done.12), channel_id=1, source_target_pairs={{32,0},{64,32},{96,64},{128,96},{160,128},{192,160},{224,192},{33,... | collective-permute-start | bytes 49160 | tf_op jit(solution)/shard_map/ppermute | solution.py:395
  106.7 6.9 %collective-permute-done.5.hi_x = f32[32,128]{1,0:T(8,128)S(1)} collective-permute-done((f32[32,128]{1,0:T(8,128)S(1)}, f32[32,128]{1,0:T(8,128)S(1)}, u32[]{:S(2)}, u32[]{:S(2)}) %collective-permute-start.5) | collective-permute-done | bytes 16416 | tf_op jit(solution)/shard_map/ppermute | solution.py:395
  113.5 9.0 %all-to-all-done.2 = f32[256,4,128]{2,1,0:T(4,128)S(1)} async-done(((f32[256,4,128]{2,1,0:T(4,128)}), f32[256,4,128]{2,1,0:T(4,128)S(1)}, u32[]{:S(2)}, u32[]{:S(2)}) %all-to-all-start.2) | async-done | bytes 524320 | tf_op jit(solution)/shard_map/all_to_all | solution.py:392
  122.6 0.7 shard_map.110
  123.2 13.1 %all_to_all.44 = f32[8,80,128]{2,1,0:T(8,128)S(1)} all-to-all(f32[8,80,128]{2,1,0:T(8,128)S(1)} %bitcast.18), channel_id=1, replica_groups=mesh['ga'=8,'ba'=32] {'ga'}, dimensions={0} | all-to-all | bytes 655360 | tf_op jit(solution)/shard_map/all_to_all | solution.py:400
  136.4 1.3 shard_map.111
  (27 shorter events, 0.1 us)
Async XLA Ops:
  1.6 25.7 %copy-start.10 = (f32[16,1,256]{2,0,1:T(8,128)}, f32[16,1,256]{2,0,1:T(8,128)S(1)}, u32[]{:S(2)}) copy-start(f32[16,1,256]{2,0,1:T(8,128)S(1)} %copy.15) | copy-start | bytes 49156
  1.6 0.7 collective-permute-start
  2.2 0.6 copy-start.9
  6.6 52.0 %all-to-all-start = ((f32[256,8,128]{2,1,0:T(8,128)}), f32[256,8,128]{2,1,0:T(8,128)S(1)}, u32[]{:S(2)}, u32[]{:S(2)}) async-start(f32[256,8,128]{2,1,0:T(8,128)} %bitcast.30), calls=%async_computation | async-start | bytes 2097152 | tf_op jit(solution)/shard_map/all_to_all | solution.py:365
  30.4 37.3 %copy-start.11 = (f32[16,1,256]{2,0,1:T(8,128)S(1)}, f32[16,1,256]{2,0,1:T(8,128)}, u32[]{:S(2)}) copy-start(f32[16,1,256]{2,0,1:T(8,128)} %copy-done.10) | copy-start | bytes 49156
  30.4 12.2 %collective-permute-start.1 = (f32[96,128]{1,0:T(8,128)}, f32[96,128]{1,0:T(8,128)S(1)}, u32[]{:S(2)}, u32[]{:S(2)}) collective-permute-start(f32[96,128]{1,0:T(8,128)} %get-tuple-element.10), channel_id=1, source_target_pairs={{0,1},{1,2},{2,3},{3,4},{4,5},{5,6},{6,7},{7,8},{8,9},{9,10},{10,1... | collective-permute-start | bytes 147464 | tf_op jit(solution)/shard_map/ppermute | solution.py:372
  38.5 19.6 %collective-permute-start.2 = (f32[96,128]{1,0:T(8,128)}, f32[96,128]{1,0:T(8,128)S(1)}, u32[]{:S(2)}, u32[]{:S(2)}) collective-permute-start(f32[96,128]{1,0:T(8,128)} %get-tuple-element.11), channel_id=1, source_target_pairs={{1,0},{2,1},{3,2},{4,3},{5,4},{6,5},{7,6},{8,7},{9,8},{10,9},{11,1... | collective-permute-start | bytes 147464 | tf_op jit(solution)/shard_map/ppermute | solution.py:371
  42.6 16.0 %copy-start.3 = (f32[96,128]{1,0:T(8,128)}, f32[96,128]{1,0:T(8,128)S(1)}, u32[]{:S(2)}) copy-start(f32[96,128]{1,0:T(8,128)S(1)} %collective-permute-done.1.lo_halo) | copy-start | bytes 147460
  58.1 0.6 copy-start.5
  58.5 1.0 copy-start.7
  59.6 23.1 %all-to-all-start.1 = ((f32[32,16,256]{2,1,0:T(8,128)}), f32[32,16,256]{2,1,0:T(8,128)S(1)}, u32[]{:S(2)}, u32[]{:S(2)}) async-start(f32[32,16,256]{2,1,0:T(8,128)} %bitcast.29), calls=%async_computation.1 | async-start | bytes 1048576 | tf_op jit(solution)/shard_map/all_to_all | solution.py:376
  67.7 9.5 %collective-permute-start.3 = (f32[16,256]{1,0:T(8,128)S(1)}, f32[16,256]{1,0:T(8,128)S(1)}, u32[]{:S(2)}, u32[]{:S(2)}) collective-permute-start(f32[16,256]{1,0:T(8,128)S(1)} %bitcast.33), channel_id=1, source_target_pairs={{16,0},{48,32},{80,64},{112,96},{144,128},{176,160},{208,192},{240... | collective-permute-start | bytes 49160 | tf_op jit(solution)/shard_map/ppermute | solution.py:359
  77.2 5.4 %copy-start.14 = (f32[16,256]{1,0:T(8,128)}, f32[16,256]{1,0:T(8,128)S(1)}, u32[]{:S(2)}) copy-start(f32[16,256]{1,0:T(8,128)S(1)} %collective-permute-done.3.amp_row256) | copy-start | bytes 49156
  82.6 0.8 copy-start.8
  83.4 17.6 %copy-start.13 = (f32[32,128]{1,0:T(8,128)S(1)}, f32[32,128]{1,0:T(8,128)}, u32[]{:S(2)}) copy-start(f32[32,128]{1,0:T(8,128)} %get-tuple-element.12.up) | copy-start | bytes 49156
  83.4 21.3 %copy-start.12 = (f32[32,128]{1,0:T(8,128)S(1)}, f32[32,128]{1,0:T(8,128)}, u32[]{:S(2)}) copy-start(f32[32,128]{1,0:T(8,128)} %get-tuple-element.13.down) | copy-start | bytes 49156
  83.4 39.1 %copy-start.2 = (bf16[2,320,512]{2,1,0:T(8,128)(2,1)S(1)}, bf16[2,320,512]{2,1,0:T(8,128)(2,1)}, u32[]{:S(2)}) copy-start(bf16[2,320,512]{2,1,0:T(8,128)(2,1)} %constant.14.clone.table) | copy-start | bytes 1966084
  87.2 49.2 %copy-start = (f32[32,8,128]{2,1,0:T(8,128)S(1)}, f32[32,8,128]{2,1,0:T(8,128)}, u32[]{:S(2)}) copy-start(f32[32,8,128]{2,1,0:T(8,128)} %param.12) | copy-start | bytes 393220
  87.2 49.2 %copy-start.1 = (f32[32,8,128]{2,1,0:T(8,128)S(1)}, f32[32,8,128]{2,1,0:T(8,128)}, u32[]{:S(2)}) copy-start(f32[32,8,128]{2,1,0:T(8,128)} %param.11) | copy-start | bytes 393220
  87.2 49.2 %copy-start.4 = (f32[96,128]{1,0:T(8,128)S(1)}, f32[96,128]{1,0:T(8,128)}, u32[]{:S(2)}) copy-start(f32[96,128]{1,0:T(8,128)} %copy-done.3) | copy-start | bytes 147460
  87.2 49.2 %copy-start.6 = (f32[96,128]{1,0:T(8,128)S(1)}, f32[96,128]{1,0:T(8,128)}, u32[]{:S(2)}) copy-start(f32[96,128]{1,0:T(8,128)} %copy-done.5) | copy-start | bytes 147460
  87.2 35.3 %all-to-all-start.2 = ((f32[256,4,128]{2,1,0:T(4,128)}), f32[256,4,128]{2,1,0:T(4,128)S(1)}, u32[]{:S(2)}, u32[]{:S(2)}) async-start(f32[256,4,128]{2,1,0:T(4,128)} %bitcast.28), calls=%async_computation.2 | async-start | bytes 1048576 | tf_op jit(solution)/shard_map/all_to_all | solution.py:392
  101.1 5.6 %collective-permute-start.4 = (f32[32,128]{1,0:T(8,128)S(1)}, f32[32,128]{1,0:T(8,128)S(1)}, u32[]{:S(2)}, u32[]{:S(2)}) collective-permute-start(f32[32,128]{1,0:T(8,128)S(1)} %copy-done.13), channel_id=1, source_target_pairs={{0,32},{32,64},{64,96},{96,128},{128,160},{160,192},{192,224},{1,3... | collective-permute-start | bytes 49160 | tf_op jit(solution)/shard_map/ppermute | solution.py:394
  104.7 8.8 %collective-permute-start.5 = (f32[32,128]{1,0:T(8,128)S(1)}, f32[32,128]{1,0:T(8,128)S(1)}, u32[]{:S(2)}, u32[]{:S(2)}) collective-permute-start(f32[32,128]{1,0:T(8,128)S(1)} %copy-done.12), channel_id=1, source_target_pairs={{32,0},{64,32},{96,64},{128,96},{160,128},{192,160},{224,192},{33,... | collective-permute-start | bytes 49160 | tf_op jit(solution)/shard_map/ppermute | solution.py:395

commit v6 on v5

--- a/solution.py
+++ b/solution.py
@@ -91,7 +91,7 @@
     return copies
 
 
-def enter_kernel(noise, table, after, sent, noise_in, table_in, rows_out, sems):
+def enter_kernel(noise, table, sent, noise_in, table_in, out, sems):
     pairs = [(table, table_in), (noise.at[0:256, :], noise_in.at[0:256, :]),
              (noise.at[256:512, :], noise_in.at[256:512, :])]
     copies = fetch(pairs, sems)
@@ -104,28 +104,38 @@
             result = dot3((table_in[0, own, :], table_in[1, own, :]), rows, 1)
             for q in range(2):
                 at = pl.ds(4 * c + 2 * part + q, DEVS, stride=8)
-                rows_out[at, :] = result[:, 128 * q : 128 * q + 128]
-    pltpu.sync_copy(rows_out, sent)
-
-
-def edges_kernel(amp, amp_first, amp_zero, head, rech, amp_sent, below, above, amp_in, sems):
+                out[at, :] = result[:, 128 * q : 128 * q + 128]
+    pltpu.sync_copy(out, sent)
+
+
+def edges_kernel(amp, head, rech, keep, give, first, below, above, amp_in, sems):
     ga, ba = lax.axis_index("ga"), lax.axis_index("ba")
     (copy,) = fetch([(amp.at[:, 0:40, :], amp_in)], sems)
     for out, near, far in ((below, 0, 1), (above, 7, 6)):
         for i, (ref, y) in enumerate(((head, near), (head, far), (rech, near))):
             out[32 * i : 32 * i + 32, :] = ref[pl.ds(y, 32, stride=8), :]
     copy.wait()
-    zero = (ga == PACKED_GA) & (ba >= BA // 2)
+    even = lax.rem(ba, 2) == 0
     for half in range(2):
         lanes = slice(128 * half, 128 * half + 128)
-        first = jnp.where(zero, amp_zero[:, lanes], amp_first[:, lanes])
-        amp_sent[0:16, lanes] = jnp.where(ga < PACKED_GA, amp_in[:, 32, lanes], first)
-        for b in range(1, BA):
-            amp_sent[16 * b : 16 * b + 16, lanes] = amp_in[:, b, lanes]
-
-
-def gate_kernel(amp_sent, got, lo_halo, hi_halo, same):
-    pass
+        for b in range(0, BA, 2):
+            near, far = amp_in[:, b, lanes], amp_in[:, b + 1, lanes]
+            if b == 0:
+                first[:, lanes] = near
+                near = jnp.where(ga < PACKED_GA, amp_in[:, 32, lanes], near)
+            keep[b // 2, 0, :, lanes] = jnp.where(even, near, far)
+            give[b // 2, :, lanes] = jnp.where(even, far, near)
+
+
+def join_kernel(keep, other, zero_near, zero_far, got, lo_halo, hi_halo, sent, sems):
+    ga, ba = lax.axis_index("ga"), lax.axis_index("ba")
+    (copy,) = fetch([(other, sent.at[:, 1])], sems)
+    copy.wait()
+
+    @pl.when((ga == PACKED_GA) & (ba >= BA // 2) & (lax.rem(ba, 2) == 0))
+    def _():
+        for copy in fetch([(zero_near, sent.at[0, 0]), (zero_far, sent.at[0, 1])], sems):
+            copy.wait()
 
 
 def mirror_of(value):
@@ -144,8 +154,14 @@
     return total
 
 
-def forward_kernel(got, y_fwd, z_fwd, spectrum, got_in, y_fwd_in, z_fwd_in, rows, held, sems):
-    copies = fetch([(got, got_in), (y_fwd, y_fwd_in), (z_fwd, z_fwd_in)], sems)
+def forward_kernel(got, y_fwd, z_fwd, head, rech, lo_halo, hi_halo, spectrum, up, down,
+                   got_in, y_fwd_in, z_fwd_in, rows, held, edge, sems):
+    pairs = [(got, got_in), (y_fwd, y_fwd_in), (z_fwd, z_fwd_in), (head.at[0:16, :], edge.at[0:16, :]),
+             (head.at[240:256, :], edge.at[16:32, :]), (rech.at[0:8, :], edge.at[32:40, :]),
+             (rech.at[248:256, :], edge.at[40:48, :])]
+    pairs += [(halo.at[x : x + 8, :], edge.at[48 + 16 * i + x // 3 : 56 + 16 * i + x // 3, :])
+              for i, halo in enumerate((lo_halo, hi_halo)) for x in (0, 24)]
+    copies = fetch(pairs, sems)
     copies[0].wait()
     low_half = lax.broadcasted_iota(jnp.int32, (BA, 128), 1) < 64
     for c in range(2):
@@ -178,31 +194,42 @@
 
         held[0, ky, :] = real
         held[1, ky, :] = imag
-        leaving += fetch([(held.at[:, ky, :], spectrum.at[:, ky, :])], sems.at[pl.ds(3 + part, 1)])
+        leaving += fetch([(held.at[:, ky, :], spectrum.at[:, ky, :])], sems.at[pl.ds(11 + part, 1)])
+    for copy in copies[3:]:
+        copy.wait()
+    corner = lax.broadcasted_iota(jnp.int32, (8, AZ), 0)
+    for out, far, near, rech_at, x in ((up, 16, 24, 40, 15), (down, 8, 0, 32, 0)):
+        out[0:8, :] = edge[far : far + 8, :]
+        out[8:16, :] = edge[near : near + 8, :]
+        out[16:24, :] = edge[rech_at : rech_at + 8, :]
+        out[24:32, :] = jnp.where(corner == 0, edge[48 + x : 49 + x, :], edge[64 + x : 65 + x, :])
     for copy in leaving:
         copy.wait()
 
 
-def inverse_kernel(spectrum, amp, amp_row0, amp_row256, z_inv, y_fwd, up, down, sent,
+def inverse_kernel(spectrum, amp, amp_row0, amp_row256, z_inv, y_fwd, sent,
                    spectrum_in, amp_in, y_fwd_in, z_inv_in, row0_in, row256_in, lines, amps, sems):
     ga, ba = lax.axis_index("ga"), lax.axis_index("ba")
     packed = (ga == PACKED_GA) & (ba == 0)
-    pairs = [(amp, amp_in), (amp_row0, row0_in), (amp_row256, row256_in), (spectrum, spectrum_in), (z_inv, z_inv_in),
+    side = lax.rem(ba, 2)
+    pairs = [(amp.at[:, 0], amp_in.at[:, side]), (amp.at[:, 1], amp_in.at[:, 1 - side]),
+             (amp_row0, row0_in), (amp_row256, row256_in), (spectrum, spectrum_in), (z_inv, z_inv_in),
              (y_fwd.at[:, :, 0:256, :], y_fwd_in)]
     copies = fetch(pairs, sems)
-    for i in range(3):
+    for i in range(4):
         copies[i].wait()
 
     @pl.when(packed)
     def _():
-        held = amp_in[...]
+        held = amp_in[...].reshape(EY, EZ)
         mirror = mirror_of(held)
         ky = lax.broadcasted_iota(jnp.int32, (EY, EZ), 0)
         amps[...] = jnp.where(ky == 0, row0_in[0:1, :], jnp.where(ky < 256, mirror, held))
-        amp_in[...] = jnp.where(ky == 256, row256_in[0:1, :], jnp.where(ky < 256, held, mirror))
-
-    copies[3].wait()
+        new = jnp.where(ky == 256, row256_in[0:1, :], jnp.where(ky < 256, held, mirror))
+        amp_in[...] = new.reshape(amp_in.shape)
+
     copies[4].wait()
+    copies[5].wait()
     for part in range(2):
         ky = slice(256 * part, 256 * part + 256)
         real, imag = spectrum_in[0, ky, :], spectrum_in[1, ky, :]
@@ -214,7 +241,7 @@
                 lanes = slice(128 * c, 128 * c + 128)
                 lines[at, 0, ky, lanes], lines[at, 1, ky, lanes] = split(value)
 
-        back(amp_in[ky, :], 0)
+        back(amp_in[8 * part : 8 * part + 8].reshape(256, EZ), 0)
 
         @pl.when(packed)
         def _():
@@ -233,7 +260,7 @@
         sent[pl.ds(c, AY, stride=4), :] = own
         sent[pl.ds(2 + c, AY, stride=4), :] = jnp.where(forward_halo, after, before)
 
-    copies[5].wait()
+    copies[6].wait()
     real, imag = inverse(0)
     store(0, real)
     store(1, imag)
@@ -241,15 +268,6 @@
     @pl.when(packed)
     def _():
         store(1, inverse(1)[1])
-
-
-def pack_kernel(head, rech, lo_halo, hi_halo, up, down):
-    corner = lax.broadcasted_iota(jnp.int32, (8, AZ), 0)
-    for out, far, near in ((up, 30, 31), (down, 1, 0)):
-        out[0:8, :] = head[8 * far : 8 * far + 8, :]
-        out[8:16, :] = head[8 * near : 8 * near + 8, :]
-        out[16:24, :] = rech[8 * near : 8 * near + 8, :]
-        out[24:32, :] = jnp.where(corner == 0, lo_halo[near : near + 1, :], hi_halo[near : near + 1, :])
 
 
 def field_kernel(got, table, lo_x, hi_x, sent, table_in, sems):
@@ -354,40 +372,43 @@
     recharge = recharge.reshape(256, AZ)
     head = head_guess.reshape(256, AZ)
     memory, sems = pltpu.VMEM, pltpu.SemaphoreType.DMA
-    amp_first = amplitude[:, 0, :]
-    amp_zero = lax.ppermute(amp_first, "ga", [(0, PACKED_GA)])
+    (sent,) = kernel_call(
+        enter_kernel, [(8 * DEVS, 128)], [noise.reshape(512, EX), x_fwd],
+        [memory((512, EX), f32), memory(x_fwd.shape, bf16), memory((8 * DEVS, 128), f32), sems((3,))],
+        held=(0, 1), outs_held=(0,), flops=10**9,
+    )
+    got = lax.all_to_all(sent, ("ba", "ga"), 0, 0, tiled=True)
+    half, plane = (BA // 2, 16, EZ), (BA // 2, 2, 16, EZ)
+    keep, give, amp_first, below, above = kernel_call(
+        edges_kernel, [plane, half, (16, EZ), (96, AZ), (96, AZ)], [amplitude, head, recharge],
+        [memory((16, 40, EZ), f32), sems((1,))], held=(0,),
+    )
+    other = lax.ppermute(give, "ba", [(i, i ^ 1) for i in range(BA)])
+    zero_near = lax.ppermute(amp_first, "ga", [(0, PACKED_GA)])
+    pairs = [(b + 1, PACKED_GA * BA + b) for b in range(BA // 2, BA, 2)]
+    zero_far = lax.ppermute(amp_first, ("ga", "ba"), pairs)
     amp_row = lax.ppermute(amp_first, "ba", [(BA // 2, 0)])
-    (sent,) = kernel_call(
-        enter_kernel, [(8 * DEVS, 128)], [noise.reshape(512, EX), x_fwd, amp_zero],
-        [memory((512, EX), f32), memory(x_fwd.shape, bf16), memory((8 * DEVS, 128), f32), sems((3,))],
-        held=(0, 1, 2), outs_held=(0,), flops=10**9,
-    )
-    got = lax.all_to_all(sent, ("ba", "ga"), 0, 0, tiled=True)
-    amp_sent, below, above = kernel_call(
-        edges_kernel, [(512, EZ), (96, AZ), (96, AZ)], [amplitude, amp_first, amp_zero, head, recharge],
-        [memory((16, 40, EZ), f32), sems((1,))], held=(0,),
-    )
     up, down = steps("ba")
     hi_halo = lax.ppermute(below, "ba", down)
     lo_halo = lax.ppermute(above, "ba", up)
     (amp_sent,) = kernel_call(
-        gate_kernel, [(512, EZ)], [amp_sent, got, lo_halo, hi_halo], held=range(4), outs_held=(0,), aliases={0: 0}
-    )
-    amp = lax.all_to_all(amp_sent, "ba", 0, 0, tiled=True)
-    (spectrum,) = kernel_call(
-        forward_kernel, [(2, EY, EZ)], [got, y_fwd, z_fwd],
+        join_kernel, [plane], [keep, other, zero_near, zero_far, got, lo_halo, hi_halo],
+        [sems((2,))], held=(0, 4, 5, 6), outs_held=(0,), vmem=4 * 2**20, aliases={0: 0},
+    )
+    halves = [list(range(side, BA, 2)) for side in range(2)]
+    amp = lax.all_to_all(amp_sent.reshape(EY, EZ), "ba", 0, 0, tiled=True, axis_index_groups=halves)
+    spectrum, to_up, to_down = kernel_call(
+        forward_kernel, [(2, EY, EZ), (32, AZ), (32, AZ)], [got, y_fwd, z_fwd, head, recharge, lo_halo, hi_halo],
         [memory(value.shape, value.dtype) for value in (got, y_fwd, z_fwd)]
-        + [memory((2, 512, 512), bf16), memory((2, EY, EZ), f32), sems((5,))],
-        held=range(3), outs_held=(0,), flops=3 * 10**9,
-    )
-    to_up, to_down = kernel_call(pack_kernel, [(32, AZ), (32, AZ)], [head, recharge, lo_halo, hi_halo])
-    plane = (EY, EZ)
+        + [memory((2, 512, 512), bf16), memory((2, EY, EZ), f32), memory((80, AZ), f32), sems((13,))],
+        held=range(7), outs_held=(0,), flops=3 * 10**9,
+    )
     (sent,) = kernel_call(
         inverse_kernel, [(4 * AY, AZ)],
-        [spectrum, amp, amp_zero, amp_row, z_inv, y_fwd, to_up, to_down],
+        [spectrum, amp.reshape(plane), zero_near, amp_row, z_inv, y_fwd],
         [memory((2, EY, EZ), f32), memory(plane, f32), memory((2, 2, AY, EY), bf16), memory(z_inv.shape, bf16)]
-        + [memory((16, EZ), f32)] * 2 + [memory((2, 2, EY, 2 * AZ), bf16), memory(plane, f32), sems((6,))],
-        held=range(8),
+        + [memory((16, EZ), f32)] * 2 + [memory((2, 2, EY, 2 * AZ), bf16), memory((EY, EZ), f32), sems((7,))],
+        held=range(6),
     )
     got = lax.all_to_all(sent, ("ba", "ga"), 0, 0, tiled=True)
     up, down = steps("ga")

time: 138 us -> 132 us (0.957)
  starting transfers between devices: 59.6 us -> 48.5 us
  waiting for transfers between devices: 40 us -> 45.5 us
    all_to_all x2, starting transfers between devices: 34.5 us -> 23 us  [body(): got = lax.all_to_all(sent, ('ba', 'ga'), 0, 0, tiled=True)]
    ppermute x1, waiting for transfers between devices: 2.74 us -> 11.2 us  [body(): lo_halo = lax.ppermute(above, 'ba', up)]
    ppermute x1 -> x3, starting transfers between devices: 0.66 us -> 7.63 us  [the longest x1 6.31 us: body(): other = lax.ppermute(give, 'ba', [(i, i ^ 1) for i in range(BA)])]
    ppermute x1, starting transfers between devices: 8.13 us -> 1.92 us  [body(): lo_halo = lax.ppermute(above, 'ba', up)]
    all_to_all x1, waiting for transfers between devices: 5.41 us -> 1.48 us  [body(): lax.all_to_all(amp_sent.reshape(EY, EZ), 'ba', 0, 0, tiled=True, axis_ind...]
    pallas_call x8 -> x7, Pallas kernels: 20.8 us -> 20 us  [kernel_call(): pl.pallas_call(kernel, out_shape=[jax.ShapeDtypeStruct(shape, f32) for sh...]
    unnamed x31 -> x32, local copies, waits for them, and re-layouts: 2.48 us -> 3.07 us
  transfers between devices with their start and end apart: 9 -> 11, of which waited for: 6 -> 6; matrix products, arithmetic and copies ran while one was open for 0% -> 0% of each run, Pallas kernels for 8% -> 8%
where the time goes in v6:
time: 132 us; the launch traced here: 131 us
  starting transfers between devices  48.5 us (37%)
  waiting for transfers between devices  45.5 us (34%)
  Pallas kernels  20 us (15%)
  blocking collectives  13.1 us (10%)
  local copies, waits for them, and re-layouts  3.07 us (2%)
    all_to_all x2, starting transfers between devices, body(): got = lax.all_to_all(sent, ('ba', 'ga'), 0, 0, tiled=True)  23 us
    pallas_call x7, Pallas kernels, kernel_call(): pl.pallas_call(kernel, out_shape=[jax.ShapeDtypeStruct(shape, f32) for sh...  20 us
    ppermute x1, waiting for transfers between devices, body(): hi_halo = lax.ppermute(below, 'ba', down)  16.7 us
    all_to_all x1, blocking collectives, body(): got = lax.all_to_all(sent, 'ga', 0, 0, tiled=True)  13.1 us
    ppermute x1, waiting for transfers between devices, body(): lo_halo = lax.ppermute(above, 'ba', up)  11.2 us
    all_to_all x2, waiting for transfers between devices, body(): got = lax.all_to_all(sent, ('ba', 'ga'), 0, 0, tiled=True)  9.02 us
    all_to_all x1, starting transfers between devices, body(): lax.all_to_all(amp_sent.reshape(EY, EZ), 'ba', 0, 0, tiled=True, axis_ind...  7.7 us
    ppermute x1, waiting for transfers between devices, body(): hi_x = lax.ppermute(to_down, 'ga', down)  6.86 us
  transfers between devices with their start and end apart: 11, of which 6 were waited for; matrix products, arithmetic and copies ran while one was open for 0% of the time, Pallas kernels for 8%

profile of v6, /device:TPU:1, one launch (start us, length us, event | category | flops | bytes accessed | tf_op | source)
XLA Modules:
  0.0 131.1 jit_solution(3058990110353502474)
XLA Ops:
  0.6 3.7 %shard_map.104 = f32[2048,128]{1,0:T(8,128)} custom-call(f32[512,512]{1,0:T(8,128)} %bitcast.28, bf16[2,512,512]{2,1,0:T(8,128)(2,1)} %constant.10.clone.table), custom_call_target="tpu_custom_call" | custom-call | flops 1000000000 | bytes 6291456 | tf_op jit(solution)/shard_map/pallas_call | solution.py:353
  4.3 15.7 %all-to-all-start = ((f32[256,8,128]{2,1,0:T(8,128)}), f32[256,8,128]{2,1,0:T(8,128)S(1)}, u32[]{:S(2)}, u32[]{:S(2)}) async-start(f32[256,8,128]{2,1,0:T(8,128)} %bitcast.27), calls=%async_computation | async-start | bytes 2097152 | tf_op jit(solution)/shard_map/all_to_all | solution.py:380
  20.0 3.3 %shard_map.105 = (f32[16,2,16,256]{3,2,1,0:T(8,128)}, f32[16,16,256]{2,1,0:T(8,128)}, f32[16,256]{1,0:T(8,128)}, f32[96,128]{1,0:T(8,128)}, f32[96,128]{1,0:T(8,128)}) custom-call(f32[16,64,256]{2,1,0:T(8,128)} %amp.1, f32[256,128]{1,0:T(8,128)} %bitcast.19, f32[256,128]{1,0:T(8,128)} %bitcast.22), custom_call_target="tpu_custom_call" | custom-call | tf_op jit(solution)/shard_map/pallas_call | solution.py:353
  23.3 6.3 %collective-permute-start.2 = (f32[16,16,256]{2,1,0:T(8,128)}, f32[16,16,256]{2,1,0:T(8,128)S(1)}, u32[]{:S(2)}, u32[]{:S(2)}) collective-permute-start(f32[16,16,256]{2,1,0:T(8,128)} %get-tuple-element.16), channel_id=1, source_target_pairs={{0,1},{1,0},{2,3},{3,2},{4,5},{5,4},{6,7},{7,6},{8,9},{9,8},{10,11... | collective-permute-start | bytes 786440 | tf_op jit(solution)/shard_map/ppermute | solution.py:386
  29.6 1.9 %collective-permute-start = (f32[96,128]{1,0:T(8,128)}, f32[96,128]{1,0:T(8,128)S(1)}, u32[]{:S(2)}, u32[]{:S(2)}) collective-permute-start(f32[96,128]{1,0:T(8,128)} %get-tuple-element.12), channel_id=1, source_target_pairs={{0,1},{1,2},{2,3},{3,4},{4,5},{5,6},{6,7},{7,8},{8,9},{9,10},{10,1... | collective-permute-start | bytes 147464 | tf_op jit(solution)/shard_map/ppermute | solution.py:393
  31.5 1.3 collective-permute-start.1
  32.8 0.7 collective-permute-start.4
  33.5 0.7 collective-permute-start.3
  34.2 0.0 collective-permute-done.3.zero_near.amp_row0
  34.2 11.2 %collective-permute-done.lo_halo = f32[96,128]{1,0:T(8,128)S(1)} collective-permute-done((f32[96,128]{1,0:T(8,128)}, f32[96,128]{1,0:T(8,128)S(1)}, u32[]{:S(2)}, u32[]{:S(2)}) %collective-permute-start) | collective-permute-done | bytes 49184 | tf_op jit(solution)/shard_map/ppermute | solution.py:393
  45.4 16.7 %collective-permute-done.1.hi_halo = f32[96,128]{1,0:T(8,128)S(1)} collective-permute-done((f32[96,128]{1,0:T(8,128)}, f32[96,128]{1,0:T(8,128)S(1)}, u32[]{:S(2)}, u32[]{:S(2)}) %collective-permute-start.1) | collective-permute-done | bytes 49184 | tf_op jit(solution)/shard_map/ppermute | solution.py:392
  62.2 1.4 %copy-done.1 = f32[16,2,16,256]{3,2,1,0:T(8,128)S(1)} copy-done((f32[16,2,16,256]{3,2,1,0:T(8,128)S(1)}, f32[16,2,16,256]{3,2,1,0:T(8,128)}, u32[]{:S(2)}) %copy-start.1) | copy-done | bytes 524312
  63.6 0.8 copy-done.2
  64.4 7.7 %all-to-all-start.1 = ((f32[16,32,256]{2,1,0:T(8,128)}), f32[16,32,256]{2,1,0:T(8,128)S(1)}, u32[]{:S(2)}, u32[]{:S(2)}) async-start(f32[16,32,256]{2,1,0:T(8,128)} %bitcast.15), calls=%async_computation.1 | async-start | bytes 1048576 | tf_op jit(solution)/shard_map/all_to_all | solution.py:399
  72.2 1.3 collective-permute-start.5
  73.5 7.3 %shard_map.106 = (f32[2,512,256]{2,1,0:T(8,128)}, f32[32,128]{1,0:T(8,128)}, f32[32,128]{1,0:T(8,128)}) custom-call(f32[2048,128]{1,0:T(8,128)} %bitcast.14, bf16[2,2,512,512]{3,2,1,0:T(8,128)(2,1)} %constant.11.clone.y_fwd, bf16[2,256,512]{2,1,0:T(8,128)(2,1)} %constant.12.clone.z_fwd, f32[256,128]{1,0:T(8,128)} %bitcast.20, f32[256,128]{1,0:T(8,128)} %bitcast.23, ...), custom_call_target="tpu_custom_call" | custom-call | flops 3000000000 | bytes 6291456 | tf_op jit(solution)/shard_map/pallas_call | solution.py:353
  80.8 0.2 collective-permute-done.5.amp_row256
  81.0 1.5 %all-to-all-done.1 = f32[16,32,256]{2,1,0:T(8,128)S(1)} async-done(((f32[16,32,256]{2,1,0:T(8,128)}), f32[16,32,256]{2,1,0:T(8,128)S(1)}, u32[]{:S(2)}, u32[]{:S(2)}) %all-to-all-start.1) | async-done | bytes 524320 | tf_op jit(solution)/shard_map/all_to_all | solution.py:399
  82.5 0.8 copy-done.11
  83.3 3.7 %shard_map.108 = f32[1024,128]{1,0:T(8,128)} custom-call(f32[2,512,256]{2,1,0:T(8,128)} %get-tuple-element.14.spectrum, f32[16,2,16,256]{3,2,1,0:T(8,128)} %bitcast.26, f32[16,256]{1,0:T(8,128)} %copy-done.10, f32[16,256]{1,0:T(8,128)} %copy-done.12, bf16[2,256,256]{2,1,0:T(8,128)(2,1)} %constant.13.clone.z_inv, bf16[2,2,512,512]{3,2,1,0:T(8,128)(2,1)} %constant.11.clone.y_fwd), custom_call_target="tpu_custom_call" | custom-call | tf_op jit(solution)/shard_map/pallas_call | solution.py:353
  87.0 0.0 copy-start.4
  87.0 0.0 copy-start.5
  87.0 0.0 copy-start.7
  87.0 0.0 copy-start.9
  87.0 7.3 %all-to-all-start.2 = ((f32[256,4,128]{2,1,0:T(4,128)}), f32[256,4,128]{2,1,0:T(4,128)S(1)}, u32[]{:S(2)}, u32[]{:S(2)}) async-start(f32[256,4,128]{2,1,0:T(4,128)} %bitcast.25), calls=%async_computation.2 | async-start | bytes 1048576 | tf_op jit(solution)/shard_map/all_to_all | solution.py:413
  94.4 3.8 %collective-permute-start.6 = (f32[32,128]{1,0:T(8,128)S(1)}, f32[32,128]{1,0:T(8,128)S(1)}, u32[]{:S(2)}, u32[]{:S(2)}) collective-permute-start(f32[32,128]{1,0:T(8,128)S(1)} %copy-done.15), channel_id=1, source_target_pairs={{0,32},{32,64},{64,96},{96,128},{128,160},{160,192},{192,224},{1,3... | collective-permute-start | bytes 49160 | tf_op jit(solution)/shard_map/ppermute | solution.py:415
  98.2 1.9 %collective-permute-start.7 = (f32[32,128]{1,0:T(8,128)S(1)}, f32[32,128]{1,0:T(8,128)S(1)}, u32[]{:S(2)}, u32[]{:S(2)}) collective-permute-start(f32[32,128]{1,0:T(8,128)S(1)} %copy-done.14), channel_id=1, source_target_pairs={{32,0},{64,32},{96,64},{128,96},{160,128},{192,160},{224,192},{33,... | collective-permute-start | bytes 49160 | tf_op jit(solution)/shard_map/ppermute | solution.py:416
  100.1 6.9 %collective-permute-done.7.hi_x = f32[32,128]{1,0:T(8,128)S(1)} collective-permute-done((f32[32,128]{1,0:T(8,128)S(1)}, f32[32,128]{1,0:T(8,128)S(1)}, u32[]{:S(2)}, u32[]{:S(2)}) %collective-permute-start.7) | collective-permute-done | bytes 16416 | tf_op jit(solution)/shard_map/ppermute | solution.py:416
  107.0 9.0 %all-to-all-done.2 = f32[256,4,128]{2,1,0:T(4,128)S(1)} async-done(((f32[256,4,128]{2,1,0:T(4,128)}), f32[256,4,128]{2,1,0:T(4,128)S(1)}, u32[]{:S(2)}, u32[]{:S(2)}) %all-to-all-start.2) | async-done | bytes 524320 | tf_op jit(solution)/shard_map/all_to_all | solution.py:413
  116.0 0.7 shard_map.109
  116.7 13.1 %all_to_all.42 = f32[8,80,128]{2,1,0:T(8,128)S(1)} all-to-all(f32[8,80,128]{2,1,0:T(8,128)S(1)} %bitcast.18), channel_id=1, replica_groups=mesh['ga'=8,'ba'=32] {'ga'}, dimensions={0} | all-to-all | bytes 655360 | tf_op jit(solution)/shard_map/all_to_all | solution.py:421
  129.8 1.3 %shard_map.110 = (f32[256,128]{1,0:T(8,128)}, f32[256,128]{1,0:T(8,128)}) custom-call(f32[640,128]{1,0:T(8,128)S(1)} %bitcast.17, f32[256,128]{1,0:T(8,128)S(1)} %bitcast.21, f32[256,128]{1,0:T(8,128)S(1)} %bitcast.24, f32[96,128]{1,0:T(8,128)S(1)} %copy-done.7, f32[96,128]{1,0:T(8,128)S(1)} %copy-done.9, f32[32,128]{1,0:T(8,128)S(1)} %collective-permute-done.6.lo_x, ...), custom_call_target="tpu_custom_call" | custom-call | tf_op jit(solution)/shard_map/pallas_call | solution.py:353
  (30 shorter events, 0.1 us)
Async XLA Ops:
  4.3 57.8 %all-to-all-start = ((f32[256,8,128]{2,1,0:T(8,128)}), f32[256,8,128]{2,1,0:T(8,128)S(1)}, u32[]{:S(2)}, u32[]{:S(2)}) async-start(f32[256,8,128]{2,1,0:T(8,128)} %bitcast.27), calls=%async_computation | async-start | bytes 2097152 | tf_op jit(solution)/shard_map/all_to_all | solution.py:380
  23.3 38.9 %collective-permute-start.2 = (f32[16,16,256]{2,1,0:T(8,128)}, f32[16,16,256]{2,1,0:T(8,128)S(1)}, u32[]{:S(2)}, u32[]{:S(2)}) collective-permute-start(f32[16,16,256]{2,1,0:T(8,128)} %get-tuple-element.16), channel_id=1, source_target_pairs={{0,1},{1,0},{2,3},{3,2},{4,5},{5,4},{6,7},{7,6},{8,9},{9,8},{10,11... | collective-permute-start | bytes 786440 | tf_op jit(solution)/shard_map/ppermute | solution.py:386
  29.6 15.8 %collective-permute-start = (f32[96,128]{1,0:T(8,128)}, f32[96,128]{1,0:T(8,128)S(1)}, u32[]{:S(2)}, u32[]{:S(2)}) collective-permute-start(f32[96,128]{1,0:T(8,128)} %get-tuple-element.12), channel_id=1, source_target_pairs={{0,1},{1,2},{2,3},{3,4},{4,5},{5,6},{6,7},{7,8},{8,9},{9,10},{10,1... | collective-permute-start | bytes 147464 | tf_op jit(solution)/shard_map/ppermute | solution.py:393
  31.5 30.6 %collective-permute-start.1 = (f32[96,128]{1,0:T(8,128)}, f32[96,128]{1,0:T(8,128)S(1)}, u32[]{:S(2)}, u32[]{:S(2)}) collective-permute-start(f32[96,128]{1,0:T(8,128)} %get-tuple-element.13), channel_id=1, source_target_pairs={{1,0},{2,1},{3,2},{4,3},{5,4},{6,5},{7,6},{8,7},{9,8},{10,9},{11,1... | collective-permute-start | bytes 147464 | tf_op jit(solution)/shard_map/ppermute | solution.py:392
  32.8 1.3 %collective-permute-start.4 = (f32[16,256]{1,0:T(8,128)}, f32[16,256]{1,0:T(8,128)S(1)}, u32[]{:S(2)}, u32[]{:S(2)}) collective-permute-start(f32[16,256]{1,0:T(8,128)} %get-tuple-element.17), channel_id=1, source_target_pairs={{17,144},{19,146},{21,148},{23,150},{25,152},{27,154},{29,156},{31... | collective-permute-start | bytes 49160 | tf_op jit(solution)/shard_map/ppermute | solution.py:389
  33.5 0.7 collective-permute-start.3
  34.2 46.6 %copy-start.10 = (f32[16,256]{1,0:T(8,128)}, f32[16,256]{1,0:T(8,128)S(1)}, u32[]{:S(2)}) copy-start(f32[16,256]{1,0:T(8,128)S(1)} %collective-permute-done.3.zero_near.amp_row0) | copy-start | bytes 49156
  45.4 28.0 %copy-start.6 = (f32[96,128]{1,0:T(8,128)}, f32[96,128]{1,0:T(8,128)S(1)}, u32[]{:S(2)}) copy-start(f32[96,128]{1,0:T(8,128)S(1)} %collective-permute-done.lo_halo) | copy-start | bytes 147460
  62.1 11.3 %copy-start.8 = (f32[96,128]{1,0:T(8,128)}, f32[96,128]{1,0:T(8,128)S(1)}, u32[]{:S(2)}) copy-start(f32[96,128]{1,0:T(8,128)S(1)} %collective-permute-done.1.hi_halo) | copy-start | bytes 147460
  62.1 11.3 %copy-start = (f32[256,8,128]{2,1,0:T(8,128)}, f32[256,8,128]{2,1,0:T(8,128)S(1)}, u32[]{:S(2)}) copy-start(f32[256,8,128]{2,1,0:T(8,128)S(1)} %all-to-all-done) | copy-start | bytes 3145732
  62.2 1.4 %copy-start.1 = (f32[16,2,16,256]{3,2,1,0:T(8,128)S(1)}, f32[16,2,16,256]{3,2,1,0:T(8,128)}, u32[]{:S(2)}) copy-start(f32[16,2,16,256]{3,2,1,0:T(8,128)} %get-tuple-element.15.keep) | copy-start | bytes 1572868
  63.6 8.6 %copy-start.13 = (f32[16,256]{1,0:T(8,128)S(1)}, f32[16,256]{1,0:T(8,128)}, u32[]{:S(2)}) copy-start(f32[16,256]{1,0:T(8,128)} %get-tuple-element.17) | copy-start | bytes 49156
  63.6 0.8 copy-start.2
  64.4 18.0 %all-to-all-start.1 = ((f32[16,32,256]{2,1,0:T(8,128)}), f32[16,32,256]{2,1,0:T(8,128)S(1)}, u32[]{:S(2)}, u32[]{:S(2)}) async-start(f32[16,32,256]{2,1,0:T(8,128)} %bitcast.15), calls=%async_computation.1 | async-start | bytes 1048576 | tf_op jit(solution)/shard_map/all_to_all | solution.py:399
  72.2 8.8 %collective-permute-start.5 = (f32[16,256]{1,0:T(8,128)S(1)}, f32[16,256]{1,0:T(8,128)S(1)}, u32[]{:S(2)}, u32[]{:S(2)}) collective-permute-start(f32[16,256]{1,0:T(8,128)S(1)} %copy-done.13), channel_id=1, source_target_pairs={{16,0},{48,32},{80,64},{112,96},{144,128},{176,160},{208,192},{240... | collective-permute-start | bytes 49160 | tf_op jit(solution)/shard_map/ppermute | solution.py:390
  81.0 1.5 %copy-start.12 = (f32[16,256]{1,0:T(8,128)}, f32[16,256]{1,0:T(8,128)S(1)}, u32[]{:S(2)}) copy-start(f32[16,256]{1,0:T(8,128)S(1)} %collective-permute-done.5.amp_row256) | copy-start | bytes 49156
  82.5 0.8 copy-start.11
  83.2 11.1 %copy-start.15 = (f32[32,128]{1,0:T(8,128)S(1)}, f32[32,128]{1,0:T(8,128)}, u32[]{:S(2)}) copy-start(f32[32,128]{1,0:T(8,128)} %get-tuple-element.18) | copy-start | bytes 49156
  83.2 14.9 %copy-start.14 = (f32[32,128]{1,0:T(8,128)S(1)}, f32[32,128]{1,0:T(8,128)}, u32[]{:S(2)}) copy-start(f32[32,128]{1,0:T(8,128)} %get-tuple-element.19) | copy-start | bytes 49156
  83.3 32.7 %copy-start.3 = (bf16[2,320,512]{2,1,0:T(8,128)(2,1)S(1)}, bf16[2,320,512]{2,1,0:T(8,128)(2,1)}, u32[]{:S(2)}) copy-start(bf16[2,320,512]{2,1,0:T(8,128)(2,1)} %constant.14.clone.table) | copy-start | bytes 1966084
  87.0 42.8 %copy-start.4 = (f32[32,8,128]{2,1,0:T(8,128)S(1)}, f32[32,8,128]{2,1,0:T(8,128)}, u32[]{:S(2)}) copy-start(f32[32,8,128]{2,1,0:T(8,128)} %param.12) | copy-start | bytes 393220
  87.0 42.8 %copy-start.5 = (f32[32,8,128]{2,1,0:T(8,128)S(1)}, f32[32,8,128]{2,1,0:T(8,128)}, u32[]{:S(2)}) copy-start(f32[32,8,128]{2,1,0:T(8,128)} %param.11) | copy-start | bytes 393220
  87.0 42.8 %copy-start.7 = (f32[96,128]{1,0:T(8,128)S(1)}, f32[96,128]{1,0:T(8,128)}, u32[]{:S(2)}) copy-start(f32[96,128]{1,0:T(8,128)} %copy-done.6) | copy-start | bytes 147460
  87.0 42.8 %copy-start.9 = (f32[96,128]{1,0:T(8,128)S(1)}, f32[96,128]{1,0:T(8,128)}, u32[]{:S(2)}) copy-start(f32[96,128]{1,0:T(8,128)} %copy-done.8) | copy-start | bytes 147460
  87.0 29.0 %all-to-all-start.2 = ((f32[256,4,128]{2,1,0:T(4,128)}), f32[256,4,128]{2,1,0:T(4,128)S(1)}, u32[]{:S(2)}, u32[]{:S(2)}) async-start(f32[256,4,128]{2,1,0:T(4,128)} %bitcast.25), calls=%async_computation.2 | async-start | bytes 1048576 | tf_op jit(solution)/shard_map/all_to_all | solution.py:413
  94.4 5.7 %collective-permute-start.6 = (f32[32,128]{1,0:T(8,128)S(1)}, f32[32,128]{1,0:T(8,128)S(1)}, u32[]{:S(2)}, u32[]{:S(2)}) collective-permute-start(f32[32,128]{1,0:T(8,128)S(1)} %copy-done.15), channel_id=1, source_target_pairs={{0,32},{32,64},{64,96},{96,128},{128,160},{160,192},{192,224},{1,3... | collective-permute-start | bytes 49160 | tf_op jit(solution)/shard_map/ppermute | solution.py:415
  98.2 8.8 %collective-permute-start.7 = (f32[32,128]{1,0:T(8,128)S(1)}, f32[32,128]{1,0:T(8,128)S(1)}, u32[]{:S(2)}, u32[]{:S(2)}) collective-permute-start(f32[32,128]{1,0:T(8,128)S(1)} %copy-done.14), channel_id=1, source_target_pairs={{32,0},{64,32},{96,64},{128,96},{160,128},{192,160},{224,192},{33,... | collective-permute-start | bytes 49160 | tf_op jit(solution)/shard_map/ppermute | solution.py:416

commit v7 on v6

--- a/solution.py
+++ b/solution.py
@@ -16,7 +16,7 @@
 DEVS = GA * BA
 PACKED_GA = 4
 XROWS = 40
-CHUNK = 2 * XROWS
+CHUNK = XROWS + 24
 VMEM = 60 * 2**20
 VMEM_END = 16 * 2**20
 f32, bf16 = jnp.float32, jnp.bfloat16
@@ -253,39 +253,48 @@
         by_sin = dot3((y_fwd_in[0, 1], y_fwd_in[1, 1]), data)
         return by_cos[:, :AZ] - by_sin[:, AZ:], by_cos[:, AZ:] + by_sin[:, :AZ]
 
-    def store(c, own):
-        forward_halo = lax.broadcasted_iota(jnp.int32, (AY, AZ), 0) % GA < GA // 2
-        after = jnp.concatenate([own[GA:], own[:GA]], 0)
-        before = jnp.concatenate([own[AY - GA :], own[: AY - GA]], 0)
-        sent[pl.ds(c, AY, stride=4), :] = own
-        sent[pl.ds(2 + c, AY, stride=4), :] = jnp.where(forward_halo, after, before)
-
     copies[6].wait()
     real, imag = inverse(0)
-    store(0, real)
-    store(1, imag)
+
+    def store(real, imag):
+        lane = lax.broadcasted_iota(jnp.int32, (AY, AZ), 1)
+        peer = lax.broadcasted_iota(jnp.int32, (AY, AZ), 0) % GA
+        first = jnp.where(lane < 64, real, pltpu.roll(imag, 64, 1))
+        second = jnp.where(lane < 64, pltpu.roll(real, 64, 1), imag)
+        halo = pltpu.roll(first, AY - 8, 0)
+        for g, shift in ((1, 7), (2, 7), (3, 6), (4, -6), (5, -7), (6, -7), (7, -8)):
+            moved = pltpu.roll(second if g % 2 else first, (AY - shift) % AY, 0)
+            halo = jnp.where(peer == g, moved, halo)
+        for i, rows in enumerate((real, imag, halo)):
+            sent[pl.ds(i, AY, stride=3), :] = rows
+
+    store(real, imag)
 
     @pl.when(packed)
     def _():
-        store(1, inverse(1)[1])
+        store(real, inverse(1)[1])
 
 
 def field_kernel(got, table, lo_x, hi_x, sent, table_in, sems):
     (copy,) = fetch([(table, table_in)], sems)
     ga, ba = lax.axis_index("ga"), lax.axis_index("ba")
-    own = jnp.concatenate([got[pl.ds(c, DEVS, stride=4), :] for c in range(2)], 0)
-    halo = jnp.concatenate([got[pl.ds(2 + c, DEVS, stride=4), :] for c in range(2)], 0)
+    own = jnp.concatenate([got[pl.ds(c, DEVS, stride=3), :] for c in range(2)], 0)
+    halo = got[pl.ds(2, DEVS, stride=3), :]
+    halo = jnp.concatenate([halo, pltpu.roll(halo, 64, 1)], 0)
     copy.wait()
     log_field = dot3((table_in[0], table_in[1]), split(jnp.concatenate([own, halo], 1)))
     row = lax.broadcasted_iota(jnp.int32, (XROWS, AZ), 0)
+    low_half = lax.broadcasted_iota(jnp.int32, (24, AZ), 1) < 64
+    in_half = lax.broadcasted_iota(jnp.int32, (XROWS, AZ), 1) < 64
     halo_inside = jnp.where(ga < GA // 2, ba < BA - 1, ba > 0)
     for g in range(GA):
         x = row + (32 * g - 4)
         inside = (x >= 0) & (x < AX)
-        value = jnp.exp(log_field[XROWS * g : XROWS * g + XROWS, :])
-        sent[CHUNK * g : CHUNK * g + XROWS, :] = jnp.where(inside, value[:, :AZ], 0.0)
-        beside = jnp.where(inside & halo_inside, value[:, AZ:], 0.0)
-        sent[CHUNK * g + XROWS : CHUNK * g + CHUNK, :] = beside
+        value = log_field[XROWS * g : XROWS * g + XROWS, :]
+        sent[CHUNK * g : CHUNK * g + XROWS, :] = jnp.where(inside, jnp.exp(value[:, :AZ]), 0.0)
+        beside = jnp.where(inside & halo_inside & in_half, jnp.exp(value[:, AZ:]), 0.0)
+        late = jnp.concatenate([beside[24:], beside[32:]], 0)
+        sent[CHUNK * g + XROWS : CHUNK * g + CHUNK, :] = jnp.where(low_half, beside[:24], pltpu.roll(late, 64, 1))
 
 
 def sweep_kernel(got, head, rech, lo_halo, hi_halo, lo_x, hi_x, cond_out, press_out,
@@ -319,10 +328,17 @@
         total = total + jnp.where(lane > 0, pltpu.roll(value, 1, 1), 0.0)
         return total + jnp.where(lane < AZ - 1, pltpu.roll(value, AZ - 1, 1), 0.0)
 
-    beside = {y: got[CHUNK * y + XROWS : CHUNK * y + CHUNK, :] for y in (0, 1, 6, 7)}
-    cond = [beside[6], beside[7]]
+    low_half = lax.broadcasted_iota(jnp.int32, (24, AZ), 1) < 64
+
+    def beside(i):
+        first, second = (got[CHUNK * g + XROWS : CHUNK * g + CHUNK, :] for g in (2 * i, 2 * i + 1))
+        early = jnp.where(low_half, first, pltpu.roll(second, 64, 1))
+        late = jnp.where(low_half, pltpu.roll(first, 64, 1), second)
+        return jnp.concatenate([early, late[:16]], 0)
+
+    cond = [beside(2), beside(3)]
     cond += [got[CHUNK * y : CHUNK * y + XROWS, :] for y in range(8)]
-    cond += [beside[0], beside[1]]
+    cond += [beside(0), beside(1)]
     planes = [head_ext[XROWS * y : XROWS * y + XROWS, :] for y in range(12)]
     weight = {y: 6.0 * cond[y] + (in_plane(cond[y]) + (cond[y - 1] + cond[y + 1])) for y in range(1, 11)}
     source = {y: 2.0 * rech_ext[XROWS * y : XROWS * y + XROWS, :] for y in range(1, 11)}
@@ -404,13 +420,14 @@
         held=range(7), outs_held=(0,), flops=3 * 10**9,
     )
     (sent,) = kernel_call(
-        inverse_kernel, [(4 * AY, AZ)],
+        inverse_kernel, [(3 * AY, AZ)],
         [spectrum, amp.reshape(plane), zero_near, amp_row, z_inv, y_fwd],
         [memory((2, EY, EZ), f32), memory(plane, f32), memory((2, 2, AY, EY), bf16), memory(z_inv.shape, bf16)]
         + [memory((16, EZ), f32)] * 2 + [memory((2, 2, EY, 2 * AZ), bf16), memory((EY, EZ), f32), sems((7,))],
         held=range(6),
     )
-    got = lax.all_to_all(sent, ("ba", "ga"), 0, 0, tiled=True)
+    sent = sent.reshape(DEVS, 1, 3 * AZ)
+    got = lax.all_to_all(sent, ("ba", "ga"), 0, 0, tiled=True).reshape(3 * DEVS, AZ)
     up, down = steps("ga")
     lo_x = lax.ppermute(to_up, "ga", up)
     hi_x = lax.ppermute(to_down, "ga", down)

time: 132 us -> 128 us (0.970)
  waiting for transfers between devices: 45.5 us -> 42.8 us
  blocking collectives: 13.1 us -> 11.5 us
    all_to_all x0 -> x1, waiting for transfers between devices: none -> 9.1 us  [body(): lax.all_to_all(sent, ('ba', 'ga'), 0, 0, tiled=True).reshape(3 * DEVS, AZ)]
    all_to_all x2 -> x1, waiting for transfers between devices: 9.02 us -> 0.01 us  [body(): got = lax.all_to_all(sent, ('ba', 'ga'), 0, 0, tiled=True)]
    all_to_all x2 -> x1, starting transfers between devices: 23 us -> 15.7 us  [body(): got = lax.all_to_all(sent, ('ba', 'ga'), 0, 0, tiled=True)]
    all_to_all x0 -> x1, starting transfers between devices: none -> 7.3 us  [body(): lax.all_to_all(sent, ('ba', 'ga'), 0, 0, tiled=True).reshape(3 * DEVS, AZ)]
    ppermute x1, waiting for transfers between devices: 6.86 us -> 4.05 us  [body(): hi_x = lax.ppermute(to_down, 'ga', down)]
    all_to_all x1, blocking collectives: 13.1 us -> 11.5 us  [body(): got = lax.all_to_all(sent, 'ga', 0, 0, tiled=True)]
where the time goes in v7:
time: 128 us; the launch traced here: 127 us
  starting transfers between devices  48.5 us (38%)
  waiting for transfers between devices  42.8 us (33%)
  Pallas kernels  20.3 us (16%)
  blocking collectives  11.5 us (9%)
  local copies, waits for them, and re-layouts  3.08 us (2%)
    pallas_call x7, Pallas kernels, kernel_call(): pl.pallas_call(kernel, out_shape=[jax.ShapeDtypeStruct(shape, f32) for sh...  20.3 us
    ppermute x1, waiting for transfers between devices, body(): hi_halo = lax.ppermute(below, 'ba', down)  16.7 us
    all_to_all x1, starting transfers between devices, body(): got = lax.all_to_all(sent, ('ba', 'ga'), 0, 0, tiled=True)  15.7 us
    all_to_all x1, blocking collectives, body(): got = lax.all_to_all(sent, 'ga', 0, 0, tiled=True)  11.5 us
    ppermute x1, waiting for transfers between devices, body(): lo_halo = lax.ppermute(above, 'ba', up)  11.2 us
    all_to_all x1, waiting for transfers between devices, body(): lax.all_to_all(sent, ('ba', 'ga'), 0, 0, tiled=True).reshape(3 * DEVS, AZ)  9.1 us
    all_to_all x1, starting transfers between devices, body(): lax.all_to_all(amp_sent.reshape(EY, EZ), 'ba', 0, 0, tiled=True, axis_ind...  7.7 us
    all_to_all x1, starting transfers between devices, body(): lax.all_to_all(sent, ('ba', 'ga'), 0, 0, tiled=True).reshape(3 * DEVS, AZ)  7.3 us
  transfers between devices with their start and end apart: 11, of which 6 were waited for; matrix products, arithmetic and copies ran while one was open for 0% of the time, Pallas kernels for 8%

profile of v7, /device:TPU:1, one launch (start us, length us, event | category | flops | bytes accessed | tf_op | source)
XLA Modules:
  0.0 127.1 jit_solution(15869298846907963663)
XLA Ops:
  0.6 3.7 %shard_map.104 = f32[2048,128]{1,0:T(8,128)} custom-call(f32[512,512]{1,0:T(8,128)} %bitcast.28, bf16[2,512,512]{2,1,0:T(8,128)(2,1)} %constant.10.clone.table), custom_call_target="tpu_custom_call" | custom-call | flops 1000000000 | bytes 6291456 | tf_op jit(solution)/shard_map/pallas_call | solution.py:369
  4.3 15.7 %all-to-all-start = ((f32[256,8,128]{2,1,0:T(8,128)}), f32[256,8,128]{2,1,0:T(8,128)S(1)}, u32[]{:S(2)}, u32[]{:S(2)}) async-start(f32[256,8,128]{2,1,0:T(8,128)} %bitcast.27), calls=%async_computation | async-start | bytes 2097152 | tf_op jit(solution)/shard_map/all_to_all | solution.py:396
  20.0 3.3 %shard_map.105 = (f32[16,2,16,256]{3,2,1,0:T(8,128)}, f32[16,16,256]{2,1,0:T(8,128)}, f32[16,256]{1,0:T(8,128)}, f32[96,128]{1,0:T(8,128)}, f32[96,128]{1,0:T(8,128)}) custom-call(f32[16,64,256]{2,1,0:T(8,128)} %amp.1, f32[256,128]{1,0:T(8,128)} %bitcast.19, f32[256,128]{1,0:T(8,128)} %bitcast.22), custom_call_target="tpu_custom_call" | custom-call | tf_op jit(solution)/shard_map/pallas_call | solution.py:369
  23.3 6.3 %collective-permute-start.2 = (f32[16,16,256]{2,1,0:T(8,128)}, f32[16,16,256]{2,1,0:T(8,128)S(1)}, u32[]{:S(2)}, u32[]{:S(2)}) collective-permute-start(f32[16,16,256]{2,1,0:T(8,128)} %get-tuple-element.16), channel_id=1, source_target_pairs={{0,1},{1,0},{2,3},{3,2},{4,5},{5,4},{6,7},{7,6},{8,9},{9,8},{10,11... | collective-permute-start | bytes 786440 | tf_op jit(solution)/shard_map/ppermute | solution.py:402
  29.6 1.9 %collective-permute-start = (f32[96,128]{1,0:T(8,128)}, f32[96,128]{1,0:T(8,128)S(1)}, u32[]{:S(2)}, u32[]{:S(2)}) collective-permute-start(f32[96,128]{1,0:T(8,128)} %get-tuple-element.12), channel_id=1, source_target_pairs={{0,1},{1,2},{2,3},{3,4},{4,5},{5,6},{6,7},{7,8},{8,9},{9,10},{10,1... | collective-permute-start | bytes 147464 | tf_op jit(solution)/shard_map/ppermute | solution.py:409
  31.5 1.3 %collective-permute-start.1 = (f32[96,128]{1,0:T(8,128)}, f32[96,128]{1,0:T(8,128)S(1)}, u32[]{:S(2)}, u32[]{:S(2)}) collective-permute-start(f32[96,128]{1,0:T(8,128)} %get-tuple-element.13), channel_id=1, source_target_pairs={{1,0},{2,1},{3,2},{4,3},{5,4},{6,5},{7,6},{8,7},{9,8},{10,9},{11,1... | collective-permute-start | bytes 147464 | tf_op jit(solution)/shard_map/ppermute | solution.py:408
  32.8 0.7 collective-permute-start.4
  33.5 0.7 collective-permute-start.3
  34.1 0.0 collective-permute-done.4.zero_far
  34.2 11.2 %collective-permute-done.lo_halo = f32[96,128]{1,0:T(8,128)S(1)} collective-permute-done((f32[96,128]{1,0:T(8,128)}, f32[96,128]{1,0:T(8,128)S(1)}, u32[]{:S(2)}, u32[]{:S(2)}) %collective-permute-start) | collective-permute-done | bytes 49184 | tf_op jit(solution)/shard_map/ppermute | solution.py:409
  45.4 16.7 %collective-permute-done.1.hi_halo = f32[96,128]{1,0:T(8,128)S(1)} collective-permute-done((f32[96,128]{1,0:T(8,128)}, f32[96,128]{1,0:T(8,128)S(1)}, u32[]{:S(2)}, u32[]{:S(2)}) %collective-permute-start.1) | collective-permute-done | bytes 49184 | tf_op jit(solution)/shard_map/ppermute | solution.py:408
  62.2 1.4 %copy-done.1 = f32[16,2,16,256]{3,2,1,0:T(8,128)S(1)} copy-done((f32[16,2,16,256]{3,2,1,0:T(8,128)S(1)}, f32[16,2,16,256]{3,2,1,0:T(8,128)}, u32[]{:S(2)}) %copy-start.1) | copy-done | bytes 524312
  63.6 0.8 copy-done.2
  64.4 7.7 %all-to-all-start.1 = ((f32[16,32,256]{2,1,0:T(8,128)}), f32[16,32,256]{2,1,0:T(8,128)S(1)}, u32[]{:S(2)}, u32[]{:S(2)}) async-start(f32[16,32,256]{2,1,0:T(8,128)} %bitcast.15), calls=%async_computation.1 | async-start | bytes 1048576 | tf_op jit(solution)/shard_map/all_to_all | solution.py:415
  72.2 1.3 %collective-permute-start.5 = (f32[16,256]{1,0:T(8,128)S(1)}, f32[16,256]{1,0:T(8,128)S(1)}, u32[]{:S(2)}, u32[]{:S(2)}) collective-permute-start(f32[16,256]{1,0:T(8,128)S(1)} %copy-done.13), channel_id=1, source_target_pairs={{16,0},{48,32},{80,64},{112,96},{144,128},{176,160},{208,192},{240... | collective-permute-start | bytes 49160 | tf_op jit(solution)/shard_map/ppermute | solution.py:406
  73.5 7.3 %shard_map.106 = (f32[2,512,256]{2,1,0:T(8,128)}, f32[32,128]{1,0:T(8,128)}, f32[32,128]{1,0:T(8,128)}) custom-call(f32[2048,128]{1,0:T(8,128)} %bitcast.14, bf16[2,2,512,512]{3,2,1,0:T(8,128)(2,1)} %constant.11.clone.y_fwd, bf16[2,256,512]{2,1,0:T(8,128)(2,1)} %constant.12.clone.z_fwd, f32[256,128]{1,0:T(8,128)} %bitcast.20, f32[256,128]{1,0:T(8,128)} %bitcast.23, ...), custom_call_target="tpu_custom_call" | custom-call | flops 3000000000 | bytes 6291456 | tf_op jit(solution)/shard_map/pallas_call | solution.py:369
  80.8 0.2 collective-permute-done.5.amp_row256
  81.0 1.5 %all-to-all-done.1 = f32[16,32,256]{2,1,0:T(8,128)S(1)} async-done(((f32[16,32,256]{2,1,0:T(8,128)}), f32[16,32,256]{2,1,0:T(8,128)S(1)}, u32[]{:S(2)}, u32[]{:S(2)}) %all-to-all-start.1) | async-done | bytes 524320 | tf_op jit(solution)/shard_map/all_to_all | solution.py:415
  82.4 0.8 copy-done.11
  83.3 3.8 %shard_map.108 = f32[768,128]{1,0:T(8,128)} custom-call(f32[2,512,256]{2,1,0:T(8,128)} %get-tuple-element.14.spectrum, f32[16,2,16,256]{3,2,1,0:T(8,128)} %bitcast.25, f32[16,256]{1,0:T(8,128)} %copy-done.10, f32[16,256]{1,0:T(8,128)} %copy-done.12, bf16[2,256,256]{2,1,0:T(8,128)(2,1)} %constant.13.clone.z_inv, bf16[2,2,512,512]{3,2,1,0:T(8,128)(2,1)} %constant.11.clone.y_fwd), custom_call_target="tpu_custom_call" | custom-call | tf_op jit(solution)/shard_map/pallas_call | solution.py:369
  87.1 0.0 copy-start.4
  87.1 0.0 copy-start.5
  87.1 0.0 copy-start.7
  87.1 0.0 copy-start.9
  87.1 7.3 %all-to-all-start.2 = ((f32[256,1,384]{2,1,0:T(1,128)}), f32[256,1,384]{2,1,0:T(1,128)S(1)}, u32[]{:S(2)}, u32[]{:S(2)}) async-start(f32[256,1,384]{2,1,0:T(1,128)} %bitcast.26), calls=%async_computation.2 | async-start | bytes 786432 | tf_op jit(solution)/shard_map/all_to_all | solution.py:430
  94.5 3.8 %collective-permute-start.6 = (f32[32,128]{1,0:T(8,128)S(1)}, f32[32,128]{1,0:T(8,128)S(1)}, u32[]{:S(2)}, u32[]{:S(2)}) collective-permute-start(f32[32,128]{1,0:T(8,128)S(1)} %copy-done.15), channel_id=1, source_target_pairs={{0,32},{32,64},{64,96},{96,128},{128,160},{160,192},{192,224},{1,3... | collective-permute-start | bytes 49160 | tf_op jit(solution)/shard_map/ppermute | solution.py:432
  98.3 1.9 %collective-permute-start.7 = (f32[32,128]{1,0:T(8,128)S(1)}, f32[32,128]{1,0:T(8,128)S(1)}, u32[]{:S(2)}, u32[]{:S(2)}) collective-permute-start(f32[32,128]{1,0:T(8,128)S(1)} %copy-done.14), channel_id=1, source_target_pairs={{32,0},{64,32},{96,64},{128,96},{160,128},{192,160},{224,192},{33,... | collective-permute-start | bytes 49160 | tf_op jit(solution)/shard_map/ppermute | solution.py:433
  100.2 4.1 %collective-permute-done.7.hi_x = f32[32,128]{1,0:T(8,128)S(1)} collective-permute-done((f32[32,128]{1,0:T(8,128)S(1)}, f32[32,128]{1,0:T(8,128)S(1)}, u32[]{:S(2)}, u32[]{:S(2)}) %collective-permute-start.7) | collective-permute-done | bytes 16416 | tf_op jit(solution)/shard_map/ppermute | solution.py:433
  104.3 9.1 %all-to-all-done.2 = f32[256,1,384]{2,1,0:T(1,128)S(1)} async-done(((f32[256,1,384]{2,1,0:T(1,128)}), f32[256,1,384]{2,1,0:T(1,128)S(1)}, u32[]{:S(2)}, u32[]{:S(2)}) %all-to-all-start.2) | async-done | bytes 393248 | tf_op jit(solution)/shard_map/all_to_all | solution.py:430
  113.4 0.8 shard_map.109
  114.2 11.5 %all_to_all.36 = f32[8,64,128]{2,1,0:T(8,128)S(1)} all-to-all(f32[8,64,128]{2,1,0:T(8,128)S(1)} %bitcast.18), channel_id=1, replica_groups=mesh['ga'=8,'ba'=32] {'ga'}, dimensions={0} | all-to-all | bytes 524288 | tf_op jit(solution)/shard_map/all_to_all | solution.py:438
  125.7 1.4 %shard_map.110 = (f32[256,128]{1,0:T(8,128)}, f32[256,128]{1,0:T(8,128)}) custom-call(f32[512,128]{1,0:T(8,128)S(1)} %bitcast.17, f32[256,128]{1,0:T(8,128)S(1)} %bitcast.21, f32[256,128]{1,0:T(8,128)S(1)} %bitcast.24, f32[96,128]{1,0:T(8,128)S(1)} %copy-done.7, f32[96,128]{1,0:T(8,128)S(1)} %copy-done.9, f32[32,128]{1,0:T(8,128)S(1)} %collective-permute-done.6.lo_x, ...), custom_call_target="tpu_custom_call" | custom-call | tf_op jit(solution)/shard_map/pallas_call | solution.py:369
  (30 shorter events, 0.1 us)
Async XLA Ops:
  4.3 57.8 %all-to-all-start = ((f32[256,8,128]{2,1,0:T(8,128)}), f32[256,8,128]{2,1,0:T(8,128)S(1)}, u32[]{:S(2)}, u32[]{:S(2)}) async-start(f32[256,8,128]{2,1,0:T(8,128)} %bitcast.27), calls=%async_computation | async-start | bytes 2097152 | tf_op jit(solution)/shard_map/all_to_all | solution.py:396
  23.3 38.9 %collective-permute-start.2 = (f32[16,16,256]{2,1,0:T(8,128)}, f32[16,16,256]{2,1,0:T(8,128)S(1)}, u32[]{:S(2)}, u32[]{:S(2)}) collective-permute-start(f32[16,16,256]{2,1,0:T(8,128)} %get-tuple-element.16), channel_id=1, source_target_pairs={{0,1},{1,0},{2,3},{3,2},{4,5},{5,4},{6,7},{7,6},{8,9},{9,8},{10,11... | collective-permute-start | bytes 786440 | tf_op jit(solution)/shard_map/ppermute | solution.py:402
  29.6 15.8 %collective-permute-start = (f32[96,128]{1,0:T(8,128)}, f32[96,128]{1,0:T(8,128)S(1)}, u32[]{:S(2)}, u32[]{:S(2)}) collective-permute-start(f32[96,128]{1,0:T(8,128)} %get-tuple-element.12), channel_id=1, source_target_pairs={{0,1},{1,2},{2,3},{3,4},{4,5},{5,6},{6,7},{7,8},{8,9},{9,10},{10,1... | collective-permute-start | bytes 147464 | tf_op jit(solution)/shard_map/ppermute | solution.py:409
  31.5 30.6 %collective-permute-start.1 = (f32[96,128]{1,0:T(8,128)}, f32[96,128]{1,0:T(8,128)S(1)}, u32[]{:S(2)}, u32[]{:S(2)}) collective-permute-start(f32[96,128]{1,0:T(8,128)} %get-tuple-element.13), channel_id=1, source_target_pairs={{1,0},{2,1},{3,2},{4,3},{5,4},{6,5},{7,6},{8,7},{9,8},{10,9},{11,1... | collective-permute-start | bytes 147464 | tf_op jit(solution)/shard_map/ppermute | solution.py:408
  32.8 1.3 %collective-permute-start.4 = (f32[16,256]{1,0:T(8,128)}, f32[16,256]{1,0:T(8,128)S(1)}, u32[]{:S(2)}, u32[]{:S(2)}) collective-permute-start(f32[16,256]{1,0:T(8,128)} %get-tuple-element.17), channel_id=1, source_target_pairs={{17,144},{19,146},{21,148},{23,150},{25,152},{27,154},{29,156},{31... | collective-permute-start | bytes 49160 | tf_op jit(solution)/shard_map/ppermute | solution.py:405
  33.5 0.7 collective-permute-start.3
  34.2 46.6 %copy-start.10 = (f32[16,256]{1,0:T(8,128)}, f32[16,256]{1,0:T(8,128)S(1)}, u32[]{:S(2)}) copy-start(f32[16,256]{1,0:T(8,128)S(1)} %collective-permute-done.3.zero_near.amp_row0) | copy-start | bytes 49156
  45.4 28.0 %copy-start.6 = (f32[96,128]{1,0:T(8,128)}, f32[96,128]{1,0:T(8,128)S(1)}, u32[]{:S(2)}) copy-start(f32[96,128]{1,0:T(8,128)S(1)} %collective-permute-done.lo_halo) | copy-start | bytes 147460
  62.1 11.3 %copy-start.8 = (f32[96,128]{1,0:T(8,128)}, f32[96,128]{1,0:T(8,128)S(1)}, u32[]{:S(2)}) copy-start(f32[96,128]{1,0:T(8,128)S(1)} %collective-permute-done.1.hi_halo) | copy-start | bytes 147460
  62.1 11.3 %copy-start = (f32[256,8,128]{2,1,0:T(8,128)}, f32[256,8,128]{2,1,0:T(8,128)S(1)}, u32[]{:S(2)}) copy-start(f32[256,8,128]{2,1,0:T(8,128)S(1)} %all-to-all-done) | copy-start | bytes 3145732
  62.1 1.4 %copy-start.1 = (f32[16,2,16,256]{3,2,1,0:T(8,128)S(1)}, f32[16,2,16,256]{3,2,1,0:T(8,128)}, u32[]{:S(2)}) copy-start(f32[16,2,16,256]{3,2,1,0:T(8,128)} %get-tuple-element.15.keep) | copy-start | bytes 1572868
  63.6 8.6 %copy-start.13 = (f32[16,256]{1,0:T(8,128)S(1)}, f32[16,256]{1,0:T(8,128)}, u32[]{:S(2)}) copy-start(f32[16,256]{1,0:T(8,128)} %get-tuple-element.17) | copy-start | bytes 49156
  63.6 0.8 copy-start.2
  64.4 18.0 %all-to-all-start.1 = ((f32[16,32,256]{2,1,0:T(8,128)}), f32[16,32,256]{2,1,0:T(8,128)S(1)}, u32[]{:S(2)}, u32[]{:S(2)}) async-start(f32[16,32,256]{2,1,0:T(8,128)} %bitcast.15), calls=%async_computation.1 | async-start | bytes 1048576 | tf_op jit(solution)/shard_map/all_to_all | solution.py:415
  72.2 8.8 %collective-permute-start.5 = (f32[16,256]{1,0:T(8,128)S(1)}, f32[16,256]{1,0:T(8,128)S(1)}, u32[]{:S(2)}, u32[]{:S(2)}) collective-permute-start(f32[16,256]{1,0:T(8,128)S(1)} %copy-done.13), channel_id=1, source_target_pairs={{16,0},{48,32},{80,64},{112,96},{144,128},{176,160},{208,192},{240... | collective-permute-start | bytes 49160 | tf_op jit(solution)/shard_map/ppermute | solution.py:406
  81.0 1.5 %copy-start.12 = (f32[16,256]{1,0:T(8,128)}, f32[16,256]{1,0:T(8,128)S(1)}, u32[]{:S(2)}) copy-start(f32[16,256]{1,0:T(8,128)S(1)} %collective-permute-done.5.amp_row256) | copy-start | bytes 49156
  82.4 0.8 copy-start.11
  83.3 11.2 %copy-start.15 = (f32[32,128]{1,0:T(8,128)S(1)}, f32[32,128]{1,0:T(8,128)}, u32[]{:S(2)}) copy-start(f32[32,128]{1,0:T(8,128)} %get-tuple-element.18) | copy-start | bytes 49156
  83.3 15.0 %copy-start.14 = (f32[32,128]{1,0:T(8,128)S(1)}, f32[32,128]{1,0:T(8,128)}, u32[]{:S(2)}) copy-start(f32[32,128]{1,0:T(8,128)} %get-tuple-element.19) | copy-start | bytes 49156
  83.3 30.1 %copy-start.3 = (bf16[2,320,512]{2,1,0:T(8,128)(2,1)S(1)}, bf16[2,320,512]{2,1,0:T(8,128)(2,1)}, u32[]{:S(2)}) copy-start(bf16[2,320,512]{2,1,0:T(8,128)(2,1)} %constant.14.clone.table) | copy-start | bytes 1966084
  87.1 38.6 %copy-start.4 = (f32[32,8,128]{2,1,0:T(8,128)S(1)}, f32[32,8,128]{2,1,0:T(8,128)}, u32[]{:S(2)}) copy-start(f32[32,8,128]{2,1,0:T(8,128)} %param.12) | copy-start | bytes 393220
  87.1 38.6 %copy-start.5 = (f32[32,8,128]{2,1,0:T(8,128)S(1)}, f32[32,8,128]{2,1,0:T(8,128)}, u32[]{:S(2)}) copy-start(f32[32,8,128]{2,1,0:T(8,128)} %param.11) | copy-start | bytes 393220
  87.1 38.6 %copy-start.7 = (f32[96,128]{1,0:T(8,128)S(1)}, f32[96,128]{1,0:T(8,128)}, u32[]{:S(2)}) copy-start(f32[96,128]{1,0:T(8,128)} %copy-done.6) | copy-start | bytes 147460
  87.1 38.6 %copy-start.9 = (f32[96,128]{1,0:T(8,128)S(1)}, f32[96,128]{1,0:T(8,128)}, u32[]{:S(2)}) copy-start(f32[96,128]{1,0:T(8,128)} %copy-done.8) | copy-start | bytes 147460
  87.1 26.2 %all-to-all-start.2 = ((f32[256,1,384]{2,1,0:T(1,128)}), f32[256,1,384]{2,1,0:T(1,128)S(1)}, u32[]{:S(2)}, u32[]{:S(2)}) async-start(f32[256,1,384]{2,1,0:T(1,128)} %bitcast.26), calls=%async_computation.2 | async-start | bytes 786432 | tf_op jit(solution)/shard_map/all_to_all | solution.py:430
  94.5 5.7 %collective-permute-start.6 = (f32[32,128]{1,0:T(8,128)S(1)}, f32[32,128]{1,0:T(8,128)S(1)}, u32[]{:S(2)}, u32[]{:S(2)}) collective-permute-start(f32[32,128]{1,0:T(8,128)S(1)} %copy-done.15), channel_id=1, source_target_pairs={{0,32},{32,64},{64,96},{96,128},{128,160},{160,192},{192,224},{1,3... | collective-permute-start | bytes 49160 | tf_op jit(solution)/shard_map/ppermute | solution.py:432
  98.3 6.0 %collective-permute-start.7 = (f32[32,128]{1,0:T(8,128)S(1)}, f32[32,128]{1,0:T(8,128)S(1)}, u32[]{:S(2)}, u32[]{:S(2)}) collective-permute-start(f32[32,128]{1,0:T(8,128)S(1)} %copy-done.14), channel_id=1, source_target_pairs={{32,0},{64,32},{96,64},{128,96},{160,128},{192,160},{224,192},{33,... | collective-permute-start | bytes 49160 | tf_op jit(solution)/shard_map/ppermute | solution.py:433

commit v8 on v7

--- a/solution.py
+++ b/solution.py
@@ -55,7 +55,8 @@
     cos, sin = trig(np.maximum(kx, 0), np.arange(EX), EX)
     wide_re, wide_im = cos.copy(), -sin
     wide_re[packed], wide_im[packed] = alternating, 1.0
-    x_fwd = np.concatenate([wide_re, wide_im])
+    x_fwd = np.stack([wide_re, wide_im]).reshape(2, BA // 2, 2, GA, EX).transpose(0, 2, 1, 3, 4)
+    x_fwd = x_fwd.reshape(2 * DEVS, EX)[:, : EX // 2]
 
     y_fwd = np.stack(trig(np.arange(EY), np.arange(EY), EY))
 
@@ -98,13 +99,18 @@
     copies[0].wait()
     for part in range(2):
         copies[1 + part].wait()
-        rows = split(noise_in[256 * part : 256 * part + 256, :])
-        for c in range(2):
-            own = slice(256 * c, 256 * c + 256)
-            result = dot3((table_in[0, own, :], table_in[1, own, :]), rows, 1)
-            for q in range(2):
-                at = pl.ds(4 * c + 2 * part + q, DEVS, stride=8)
-                out[at, :] = result[:, 128 * q : 128 * q + 128]
+        rows = slice(256 * part, 256 * part + 256)
+        early, late = noise_in[rows, 0:256], noise_in[rows, 256:512]
+        for parity, value in enumerate((early + late, early - late)):
+            folded = split(value)
+            for c in range(2):
+                own = slice(256 * c + 128 * parity, 256 * c + 128 * parity + 128)
+                result = dot3((table_in[0, own, :], table_in[1, own, :]), folded, 1)
+                for pair in range(BA // 2):
+                    for q in range(2):
+                        first = 8 * GA * (2 * pair + parity) + 4 * c + 2 * part + q
+                        tile = result[GA * pair : GA * pair + GA, 128 * q : 128 * q + 128]
+                        out[pl.ds(first, GA, stride=8), :] = tile
     pltpu.sync_copy(out, sent)
 
 
@@ -397,7 +403,7 @@
     half, plane = (BA // 2, 16, EZ), (BA // 2, 2, 16, EZ)
     keep, give, amp_first, below, above = kernel_call(
         edges_kernel, [plane, half, (16, EZ), (96, AZ), (96, AZ)], [amplitude, head, recharge],
-        [memory((16, 40, EZ), f32), sems((1,))], held=(0,),
+        [memory((16, 40, EZ), f32), sems((1,))], held=(0,), vmem=8 * 2**20,
     )
     other = lax.ppermute(give, "ba", [(i, i ^ 1) for i in range(BA)])
     zero_near = lax.ppermute(amp_first, "ga", [(0, PACKED_GA)])

time: 128 us -> 126 us (0.984)
  local copies, waits for them, and re-layouts: 3.08 us -> 0.88 us
  waiting for transfers between devices: 42.8 us -> 44.8 us
  Pallas kernels: 20.3 us -> 18.9 us
    unnamed x32, local copies, waits for them, and re-layouts: 3.08 us -> 0.88 us
    ppermute x1, waiting for transfers between devices: 11.2 us -> 13.2 us  [body(): lo_halo = lax.ppermute(above, 'ba', up)]
    pallas_call x7, Pallas kernels: 20.3 us -> 18.9 us  [kernel_call(): pl.pallas_call(kernel, out_shape=[jax.ShapeDtypeStruct(shape, f32) for sh...]
  transfers between devices with their start and end apart: 11 -> 11, of which waited for: 6 -> 6; matrix products, arithmetic and copies ran while one was open for 0% -> 0% of each run, Pallas kernels for 8% -> 7%
where the time goes in v8:
time: 126 us
  starting transfers between devices  48.6 us (39%)
  waiting for transfers between devices  44.8 us (36%)
  Pallas kernels  18.9 us (15%)
  blocking collectives  11.5 us (9%)
    pallas_call x7, Pallas kernels, kernel_call(): pl.pallas_call(kernel, out_shape=[jax.ShapeDtypeStruct(shape, f32) for sh...  18.9 us
    ppermute x1, waiting for transfers between devices, body(): hi_halo = lax.ppermute(below, 'ba', down)  16.8 us
    all_to_all x1, starting transfers between devices, body(): got = lax.all_to_all(sent, ('ba', 'ga'), 0, 0, tiled=True)  15.7 us
    ppermute x1, waiting for transfers between devices, body(): lo_halo = lax.ppermute(above, 'ba', up)  13.2 us
    all_to_all x1, blocking collectives, body(): got = lax.all_to_all(sent, 'ga', 0, 0, tiled=True)  11.5 us
    all_to_all x1, waiting for transfers between devices, body(): lax.all_to_all(sent, ('ba', 'ga'), 0, 0, tiled=True).reshape(3 * DEVS, AZ)  9.1 us
    all_to_all x1, starting transfers between devices, body(): lax.all_to_all(amp_sent.reshape(EY, EZ), 'ba', 0, 0, tiled=True, axis_ind...  7.72 us
    all_to_all x1, starting transfers between devices, body(): lax.all_to_all(sent, ('ba', 'ga'), 0, 0, tiled=True).reshape(3 * DEVS, AZ)  7.31 us
  transfers between devices with their start and end apart: 11, of which 6 were waited for; matrix products, arithmetic and copies ran while one was open for 0% of the time, Pallas kernels for 7%

profile of v8, /device:TPU:1, one launch (start us, length us, event | category | flops | bytes accessed | tf_op | source)
XLA Modules:
  0.0 125.6 jit_solution(1079619157311926428)
XLA Ops:
  0.6 0.0 copy-start.3
  0.7 0.0 copy-start.5
  0.7 3.6 %shard_map.104 = f32[2048,128]{1,0:T(8,128)} custom-call(f32[512,512]{1,0:T(8,128)} %bitcast.27, bf16[2,512,256]{2,1,0:T(8,128)(2,1)} %constant.10.clone.table), custom_call_target="tpu_custom_call" | custom-call | flops 1000000000 | bytes 6291456 | tf_op jit(solution)/shard_map/pallas_call | solution.py:375
  4.3 15.7 %all-to-all-start = ((f32[256,8,128]{2,1,0:T(8,128)}), f32[256,8,128]{2,1,0:T(8,128)S(1)}, u32[]{:S(2)}, u32[]{:S(2)}) async-start(f32[256,8,128]{2,1,0:T(8,128)} %bitcast.26), calls=%async_computation | async-start | bytes 2097152 | tf_op jit(solution)/shard_map/all_to_all | solution.py:402
  20.0 1.2 shard_map.105
  21.2 6.3 %collective-permute-start.2 = (f32[16,16,256]{2,1,0:T(8,128)S(1)}, f32[16,16,256]{2,1,0:T(8,128)S(1)}, u32[]{:S(2)}, u32[]{:S(2)}) collective-permute-start(f32[16,16,256]{2,1,0:T(8,128)S(1)} %get-tuple-element.16), channel_id=1, source_target_pairs={{0,1},{1,0},{2,3},{3,2},{4,5},{5,4},{6,7},{7,6},{8,9},{9,8},{10,11... | collective-permute-start | bytes 786440 | tf_op jit(solution)/shard_map/ppermute | solution.py:408
  27.5 1.9 %collective-permute-start = (f32[96,128]{1,0:T(8,128)S(1)}, f32[96,128]{1,0:T(8,128)S(1)}, u32[]{:S(2)}, u32[]{:S(2)}) collective-permute-start(f32[96,128]{1,0:T(8,128)S(1)} %get-tuple-element.12), channel_id=1, source_target_pairs={{0,1},{1,2},{2,3},{3,4},{4,5},{5,6},{6,7},{7,8},{8,9},{9,10},{10,1... | collective-permute-start | bytes 147464 | tf_op jit(solution)/shard_map/ppermute | solution.py:415
  29.4 1.3 %collective-permute-start.1 = (f32[96,128]{1,0:T(8,128)S(1)}, f32[96,128]{1,0:T(8,128)S(1)}, u32[]{:S(2)}, u32[]{:S(2)}) collective-permute-start(f32[96,128]{1,0:T(8,128)S(1)} %get-tuple-element.13), channel_id=1, source_target_pairs={{1,0},{2,1},{3,2},{4,3},{5,4},{6,5},{7,6},{8,7},{9,8},{10,9},{11,1... | collective-permute-start | bytes 147464 | tf_op jit(solution)/shard_map/ppermute | solution.py:414
  30.7 0.7 collective-permute-start.4
  31.4 0.7 collective-permute-start.3
  32.1 13.2 %collective-permute-done.lo_halo = f32[96,128]{1,0:T(8,128)S(1)} collective-permute-done((f32[96,128]{1,0:T(8,128)S(1)}, f32[96,128]{1,0:T(8,128)S(1)}, u32[]{:S(2)}, u32[]{:S(2)}) %collective-permute-start) | collective-permute-done | bytes 49184 | tf_op jit(solution)/shard_map/ppermute | solution.py:415
  45.3 16.8 %collective-permute-done.1.hi_halo = f32[96,128]{1,0:T(8,128)S(1)} collective-permute-done((f32[96,128]{1,0:T(8,128)S(1)}, f32[96,128]{1,0:T(8,128)S(1)}, u32[]{:S(2)}, u32[]{:S(2)}) %collective-permute-start.1) | collective-permute-done | bytes 49184 | tf_op jit(solution)/shard_map/ppermute | solution.py:414
  62.1 0.8 shard_map.107
  62.9 7.7 %all-to-all-start.1 = ((f32[16,32,256]{2,1,0:T(8,128)}), f32[16,32,256]{2,1,0:T(8,128)S(1)}, u32[]{:S(2)}, u32[]{:S(2)}) async-start(f32[16,32,256]{2,1,0:T(8,128)} %bitcast.5), calls=%async_computation.1 | async-start | bytes 1048576 | tf_op jit(solution)/shard_map/all_to_all | solution.py:421
  70.6 1.3 %collective-permute-start.5 = (f32[16,256]{1,0:T(8,128)S(1)}, f32[16,256]{1,0:T(8,128)S(1)}, u32[]{:S(2)}, u32[]{:S(2)}) collective-permute-start(f32[16,256]{1,0:T(8,128)S(1)} %get-tuple-element.17), channel_id=1, source_target_pairs={{16,0},{48,32},{80,64},{112,96},{144,128},{176,160},{208,192},{240... | collective-permute-start | bytes 49160 | tf_op jit(solution)/shard_map/ppermute | solution.py:412
  72.0 7.3 %shard_map.106 = (f32[2,512,256]{2,1,0:T(8,128)}, f32[32,128]{1,0:T(8,128)}, f32[32,128]{1,0:T(8,128)}) custom-call(f32[2048,128]{1,0:T(8,128)} %bitcast.14, bf16[2,2,512,512]{3,2,1,0:T(8,128)(2,1)} %constant.11.clone.y_fwd, bf16[2,256,512]{2,1,0:T(8,128)(2,1)} %constant.12.clone.z_fwd, f32[256,128]{1,0:T(8,128)} %bitcast.18, f32[256,128]{1,0:T(8,128)} %bitcast.21, ...), custom_call_target="tpu_custom_call" | custom-call | flops 3000000000 | bytes 6291456 | tf_op jit(solution)/shard_map/pallas_call | solution.py:375
  79.3 0.2 collective-permute-done.5.amp_row256
  79.5 1.5 %all-to-all-done.1 = f32[16,32,256]{2,1,0:T(8,128)S(1)} async-done(((f32[16,32,256]{2,1,0:T(8,128)}), f32[16,32,256]{2,1,0:T(8,128)S(1)}, u32[]{:S(2)}, u32[]{:S(2)}) %all-to-all-start.1) | async-done | bytes 524320 | tf_op jit(solution)/shard_map/all_to_all | solution.py:421
  80.9 0.8 copy-done.12
  81.7 3.8 %shard_map.108 = f32[768,128]{1,0:T(8,128)} custom-call(f32[2,512,256]{2,1,0:T(8,128)} %get-tuple-element.14.spectrum, f32[16,2,16,256]{3,2,1,0:T(8,128)} %bitcast.24, f32[16,256]{1,0:T(8,128)} %copy-done.11, f32[16,256]{1,0:T(8,128)} %copy-done.13, bf16[2,256,256]{2,1,0:T(8,128)(2,1)} %constant.13.clone.z_inv, bf16[2,2,512,512]{3,2,1,0:T(8,128)(2,1)} %constant.11.clone.y_fwd), custom_call_target="tpu_custom_call" | custom-call | tf_op jit(solution)/shard_map/pallas_call | solution.py:375
  85.6 0.0 copy-start.4
  85.6 0.0 copy-start.6
  85.6 0.0 copy-start.8
  85.6 0.0 copy-start.10
  85.6 7.3 %all-to-all-start.2 = ((f32[256,1,384]{2,1,0:T(1,128)}), f32[256,1,384]{2,1,0:T(1,128)S(1)}, u32[]{:S(2)}, u32[]{:S(2)}) async-start(f32[256,1,384]{2,1,0:T(1,128)} %bitcast.25), calls=%async_computation.2 | async-start | bytes 786432 | tf_op jit(solution)/shard_map/all_to_all | solution.py:436
  92.9 3.8 %collective-permute-start.6 = (f32[32,128]{1,0:T(8,128)S(1)}, f32[32,128]{1,0:T(8,128)S(1)}, u32[]{:S(2)}, u32[]{:S(2)}) collective-permute-start(f32[32,128]{1,0:T(8,128)S(1)} %copy-done.15), channel_id=1, source_target_pairs={{0,32},{32,64},{64,96},{96,128},{128,160},{160,192},{192,224},{1,3... | collective-permute-start | bytes 49160 | tf_op jit(solution)/shard_map/ppermute | solution.py:438
  96.8 1.9 %collective-permute-start.7 = (f32[32,128]{1,0:T(8,128)S(1)}, f32[32,128]{1,0:T(8,128)S(1)}, u32[]{:S(2)}, u32[]{:S(2)}) collective-permute-start(f32[32,128]{1,0:T(8,128)S(1)} %copy-done.14), channel_id=1, source_target_pairs={{32,0},{64,32},{96,64},{128,96},{160,128},{192,160},{224,192},{33,... | collective-permute-start | bytes 49160 | tf_op jit(solution)/shard_map/ppermute | solution.py:439
  98.7 4.1 %collective-permute-done.7.hi_x = f32[32,128]{1,0:T(8,128)S(1)} collective-permute-done((f32[32,128]{1,0:T(8,128)S(1)}, f32[32,128]{1,0:T(8,128)S(1)}, u32[]{:S(2)}, u32[]{:S(2)}) %collective-permute-start.7) | collective-permute-done | bytes 16416 | tf_op jit(solution)/shard_map/ppermute | solution.py:439
  102.8 9.1 %all-to-all-done.2 = f32[256,1,384]{2,1,0:T(1,128)S(1)} async-done(((f32[256,1,384]{2,1,0:T(1,128)}), f32[256,1,384]{2,1,0:T(1,128)S(1)}, u32[]{:S(2)}, u32[]{:S(2)}) %all-to-all-start.2) | async-done | bytes 393248 | tf_op jit(solution)/shard_map/all_to_all | solution.py:436
  111.9 0.8 shard_map.109
  112.7 11.5 %all_to_all.36 = f32[8,64,128]{2,1,0:T(8,128)S(1)} all-to-all(f32[8,64,128]{2,1,0:T(8,128)S(1)} %bitcast.17), channel_id=1, replica_groups=mesh['ga'=8,'ba'=32] {'ga'}, dimensions={0} | all-to-all | bytes 524288 | tf_op jit(solution)/shard_map/all_to_all | solution.py:444
  124.2 1.4 %shard_map.110 = (f32[256,128]{1,0:T(8,128)}, f32[256,128]{1,0:T(8,128)}) custom-call(f32[512,128]{1,0:T(8,128)S(1)} %bitcast.16, f32[256,128]{1,0:T(8,128)S(1)} %bitcast.20, f32[256,128]{1,0:T(8,128)S(1)} %bitcast.23, f32[96,128]{1,0:T(8,128)S(1)} %copy-done.8, f32[96,128]{1,0:T(8,128)S(1)} %copy-done.10, f32[32,128]{1,0:T(8,128)S(1)} %collective-permute-done.6.lo_x, ...), custom_call_target="tpu_custom_call" | custom-call | tf_op jit(solution)/shard_map/pallas_call | solution.py:375
  (30 shorter events, 0.1 us)
Async XLA Ops:
  0.6 19.3 %copy-start.1 = (f32[16,64,256]{2,1,0:T(8,128)S(1)}, f32[16,64,256]{2,1,0:T(8,128)}, u32[]{:S(2)}) copy-start(f32[16,64,256]{2,1,0:T(8,128)} %amp.1) | copy-start | bytes 3145732
  0.6 19.3 %copy-start.3 = (f32[32,8,128]{2,1,0:T(8,128)S(1)}, f32[32,8,128]{2,1,0:T(8,128)}, u32[]{:S(2)}) copy-start(f32[32,8,128]{2,1,0:T(8,128)} %param.12) | copy-start | bytes 393220
  0.7 19.3 %copy-start.5 = (f32[32,8,128]{2,1,0:T(8,128)S(1)}, f32[32,8,128]{2,1,0:T(8,128)}, u32[]{:S(2)}) copy-start(f32[32,8,128]{2,1,0:T(8,128)} %param.11) | copy-start | bytes 393220
  4.3 57.8 %all-to-all-start = ((f32[256,8,128]{2,1,0:T(8,128)}), f32[256,8,128]{2,1,0:T(8,128)S(1)}, u32[]{:S(2)}, u32[]{:S(2)}) async-start(f32[256,8,128]{2,1,0:T(8,128)} %bitcast.26), calls=%async_computation | async-start | bytes 2097152 | tf_op jit(solution)/shard_map/all_to_all | solution.py:402
  21.2 40.9 %collective-permute-start.2 = (f32[16,16,256]{2,1,0:T(8,128)S(1)}, f32[16,16,256]{2,1,0:T(8,128)S(1)}, u32[]{:S(2)}, u32[]{:S(2)}) collective-permute-start(f32[16,16,256]{2,1,0:T(8,128)S(1)} %get-tuple-element.16), channel_id=1, source_target_pairs={{0,1},{1,0},{2,3},{3,2},{4,5},{5,4},{6,7},{7,6},{8,9},{9,8},{10,11... | collective-permute-start | bytes 786440 | tf_op jit(solution)/shard_map/ppermute | solution.py:408
  27.5 17.8 %collective-permute-start = (f32[96,128]{1,0:T(8,128)S(1)}, f32[96,128]{1,0:T(8,128)S(1)}, u32[]{:S(2)}, u32[]{:S(2)}) collective-permute-start(f32[96,128]{1,0:T(8,128)S(1)} %get-tuple-element.12), channel_id=1, source_target_pairs={{0,1},{1,2},{2,3},{3,4},{4,5},{5,6},{6,7},{7,8},{8,9},{9,10},{10,1... | collective-permute-start | bytes 147464 | tf_op jit(solution)/shard_map/ppermute | solution.py:415
  29.4 32.7 %collective-permute-start.1 = (f32[96,128]{1,0:T(8,128)S(1)}, f32[96,128]{1,0:T(8,128)S(1)}, u32[]{:S(2)}, u32[]{:S(2)}) collective-permute-start(f32[96,128]{1,0:T(8,128)S(1)} %get-tuple-element.13), channel_id=1, source_target_pairs={{1,0},{2,1},{3,2},{4,3},{5,4},{6,5},{7,6},{8,7},{9,8},{10,9},{11,1... | collective-permute-start | bytes 147464 | tf_op jit(solution)/shard_map/ppermute | solution.py:414
  30.7 1.3 %collective-permute-start.4 = (f32[16,256]{1,0:T(8,128)S(1)}, f32[16,256]{1,0:T(8,128)S(1)}, u32[]{:S(2)}, u32[]{:S(2)}) collective-permute-start(f32[16,256]{1,0:T(8,128)S(1)} %get-tuple-element.17), channel_id=1, source_target_pairs={{17,144},{19,146},{21,148},{23,150},{25,152},{27,154},{29,156},{31... | collective-permute-start | bytes 49160 | tf_op jit(solution)/shard_map/ppermute | solution.py:411
  31.4 0.7 collective-permute-start.3
  32.1 47.2 %copy-start.11 = (f32[16,256]{1,0:T(8,128)}, f32[16,256]{1,0:T(8,128)S(1)}, u32[]{:S(2)}) copy-start(f32[16,256]{1,0:T(8,128)S(1)} %collective-permute-done.3.zero_near.amp_row0) | copy-start | bytes 49156
  45.3 26.6 %copy-start.7 = (f32[96,128]{1,0:T(8,128)}, f32[96,128]{1,0:T(8,128)S(1)}, u32[]{:S(2)}) copy-start(f32[96,128]{1,0:T(8,128)S(1)} %collective-permute-done.lo_halo) | copy-start | bytes 147460
  62.1 9.8 %copy-start.9 = (f32[96,128]{1,0:T(8,128)}, f32[96,128]{1,0:T(8,128)S(1)}, u32[]{:S(2)}) copy-start(f32[96,128]{1,0:T(8,128)S(1)} %collective-permute-done.1.hi_halo) | copy-start | bytes 147460
  62.1 9.8 %copy-start = (f32[256,8,128]{2,1,0:T(8,128)}, f32[256,8,128]{2,1,0:T(8,128)S(1)}, u32[]{:S(2)}) copy-start(f32[256,8,128]{2,1,0:T(8,128)S(1)} %all-to-all-done) | copy-start | bytes 3145732
  62.9 18.0 %all-to-all-start.1 = ((f32[16,32,256]{2,1,0:T(8,128)}), f32[16,32,256]{2,1,0:T(8,128)S(1)}, u32[]{:S(2)}, u32[]{:S(2)}) async-start(f32[16,32,256]{2,1,0:T(8,128)} %bitcast.5), calls=%async_computation.1 | async-start | bytes 1048576 | tf_op jit(solution)/shard_map/all_to_all | solution.py:421
  70.6 8.8 %collective-permute-start.5 = (f32[16,256]{1,0:T(8,128)S(1)}, f32[16,256]{1,0:T(8,128)S(1)}, u32[]{:S(2)}, u32[]{:S(2)}) collective-permute-start(f32[16,256]{1,0:T(8,128)S(1)} %get-tuple-element.17), channel_id=1, source_target_pairs={{16,0},{48,32},{80,64},{112,96},{144,128},{176,160},{208,192},{240... | collective-permute-start | bytes 49160 | tf_op jit(solution)/shard_map/ppermute | solution.py:412
  79.4 1.5 %copy-start.13 = (f32[16,256]{1,0:T(8,128)}, f32[16,256]{1,0:T(8,128)S(1)}, u32[]{:S(2)}) copy-start(f32[16,256]{1,0:T(8,128)S(1)} %collective-permute-done.5.amp_row256) | copy-start | bytes 49156
  80.9 0.8 copy-start.12
  81.7 11.2 %copy-start.15 = (f32[32,128]{1,0:T(8,128)S(1)}, f32[32,128]{1,0:T(8,128)}, u32[]{:S(2)}) copy-start(f32[32,128]{1,0:T(8,128)} %get-tuple-element.18) | copy-start | bytes 49156
  81.7 15.0 %copy-start.14 = (f32[32,128]{1,0:T(8,128)S(1)}, f32[32,128]{1,0:T(8,128)}, u32[]{:S(2)}) copy-start(f32[32,128]{1,0:T(8,128)} %get-tuple-element.19) | copy-start | bytes 49156
  81.7 30.1 %copy-start.2 = (bf16[2,320,512]{2,1,0:T(8,128)(2,1)S(1)}, bf16[2,320,512]{2,1,0:T(8,128)(2,1)}, u32[]{:S(2)}) copy-start(bf16[2,320,512]{2,1,0:T(8,128)(2,1)} %constant.14.clone.table) | copy-start | bytes 1966084
  85.6 38.6 %copy-start.4 = (f32[32,8,128]{2,1,0:T(8,128)S(1)}, f32[32,8,128]{2,1,0:T(8,128)}, u32[]{:S(2)}) copy-start(f32[32,8,128]{2,1,0:T(8,128)} %param.12) | copy-start | bytes 393220
  85.6 38.6 %copy-start.6 = (f32[32,8,128]{2,1,0:T(8,128)S(1)}, f32[32,8,128]{2,1,0:T(8,128)}, u32[]{:S(2)}) copy-start(f32[32,8,128]{2,1,0:T(8,128)} %param.11) | copy-start | bytes 393220
  85.6 38.6 %copy-start.8 = (f32[96,128]{1,0:T(8,128)S(1)}, f32[96,128]{1,0:T(8,128)}, u32[]{:S(2)}) copy-start(f32[96,128]{1,0:T(8,128)} %copy-done.7) | copy-start | bytes 147460
  85.6 38.6 %copy-start.10 = (f32[96,128]{1,0:T(8,128)S(1)}, f32[96,128]{1,0:T(8,128)}, u32[]{:S(2)}) copy-start(f32[96,128]{1,0:T(8,128)} %copy-done.9) | copy-start | bytes 147460
  85.6 26.2 %all-to-all-start.2 = ((f32[256,1,384]{2,1,0:T(1,128)}), f32[256,1,384]{2,1,0:T(1,128)S(1)}, u32[]{:S(2)}, u32[]{:S(2)}) async-start(f32[256,1,384]{2,1,0:T(1,128)} %bitcast.25), calls=%async_computation.2 | async-start | bytes 786432 | tf_op jit(solution)/shard_map/all_to_all | solution.py:436
  92.9 5.7 %collective-permute-start.6 = (f32[32,128]{1,0:T(8,128)S(1)}, f32[32,128]{1,0:T(8,128)S(1)}, u32[]{:S(2)}, u32[]{:S(2)}) collective-permute-start(f32[32,128]{1,0:T(8,128)S(1)} %copy-done.15), channel_id=1, source_target_pairs={{0,32},{32,64},{64,96},{96,128},{128,160},{160,192},{192,224},{1,3... | collective-permute-start | bytes 49160 | tf_op jit(solution)/shard_map/ppermute | solution.py:438
  96.8 6.0 %collective-permute-start.7 = (f32[32,128]{1,0:T(8,128)S(1)}, f32[32,128]{1,0:T(8,128)S(1)}, u32[]{:S(2)}, u32[]{:S(2)}) collective-permute-start(f32[32,128]{1,0:T(8,128)S(1)} %copy-done.14), channel_id=1, source_target_pairs={{32,0},{64,32},{96,64},{128,96},{160,128},{192,160},{224,192},{33,... | collective-permute-start | bytes 49160 | tf_op jit(solution)/shard_map/ppermute | solution.py:439

commit v9 on v8

--- a/solution.py
+++ b/solution.py
@@ -18,6 +18,7 @@
 XROWS = 40
 CHUNK = XROWS + 24
 VMEM = 60 * 2**20
+VMEM_MIDDLE = 24 * 2**20
 VMEM_END = 16 * 2**20
 f32, bf16 = jnp.float32, jnp.bfloat16
 
@@ -71,7 +72,9 @@
     back_re[:, packed] = alternating[xs][:, None]
     back_im[:, packed] = 1.0
     x_inv = np.concatenate([back_re, back_im], 1) / (EX * EY * EZ)
-    return tuple(split_np(t) for t in (x_fwd, y_fwd, z_fwd, z_inv, x_inv))
+    y_inv = y_fwd[:, :AY]
+    y_fwd = np.concatenate([y_fwd[:, 0::2, : EY // 2], y_fwd[:, 1::2, : EY // 2]], 1)
+    return tuple(split_np(t) for t in (x_fwd, y_fwd, z_fwd, z_inv, y_inv, x_inv))
 
 
 def split(value):
@@ -145,84 +148,81 @@
 
 
 def mirror_of(value):
-    ones = []
-    for size in value.shape:
-        i = lax.broadcasted_iota(jnp.int32, (size, size), 0)
-        j = lax.broadcasted_iota(jnp.int32, (size, size), 1)
-        ones.append((((i + j) == 0) | ((i + j) == size)).astype(bf16))
+    i = lax.broadcasted_iota(jnp.int32, (256, 256), 0)
+    j = lax.broadcasted_iota(jnp.int32, (256, 256), 1)
+    flip = ((i + j) == 256).astype(bf16)
+    turn = (((i + j) == 0) | ((i + j) == 256)).astype(bf16)
+    value = jnp.concatenate([value[256:], value[:256]], 1)
     total = None
     for _ in range(3):
         part = value.astype(bf16)
         value = value - part.astype(f32)
-        part = jnp.dot(ones[0], part, preferred_element_type=f32).astype(bf16)
-        part = jnp.dot(part, ones[1], preferred_element_type=f32)
+        part = jnp.dot(flip, part, preferred_element_type=f32).astype(bf16)
+        part = jnp.concatenate([part[:, :256], part[:, 256:]], 0)
+        part = jnp.dot(part, turn, preferred_element_type=f32)
         total = part if total is None else total + part
     return total
 
 
 def forward_kernel(got, y_fwd, z_fwd, head, rech, lo_halo, hi_halo, spectrum, up, down,
-                   got_in, y_fwd_in, z_fwd_in, rows, held, edge, sems):
-    pairs = [(got, got_in), (y_fwd, y_fwd_in), (z_fwd, z_fwd_in), (head.at[0:16, :], edge.at[0:16, :]),
+                   y_fwd_in, z_fwd_in, rows, edge, sems):
+    pairs = [(y_fwd, y_fwd_in), (z_fwd, z_fwd_in), (head.at[0:16, :], edge.at[0:16, :]),
              (head.at[240:256, :], edge.at[16:32, :]), (rech.at[0:8, :], edge.at[32:40, :]),
              (rech.at[248:256, :], edge.at[40:48, :])]
-    pairs += [(halo.at[x : x + 8, :], edge.at[48 + 16 * i + x // 3 : 56 + 16 * i + x // 3, :])
-              for i, halo in enumerate((lo_halo, hi_halo)) for x in (0, 24)]
     copies = fetch(pairs, sems)
-    copies[0].wait()
     low_half = lax.broadcasted_iota(jnp.int32, (BA, 128), 1) < 64
     for c in range(2):
         for q in range(4):
-            for p in range(4):
-                even = got_in[pl.ds(16 * p + 4 * c + q, BA, stride=64), :]
-                odd = got_in[pl.ds(16 * p + 8 + 4 * c + q, BA, stride=64), :]
-                first = jnp.where(low_half, even, pltpu.roll(odd, 64, 1))
-                second = jnp.where(low_half, pltpu.roll(even, 64, 1), odd)
-                for half, value in enumerate((first, second)):
+            for p in range(2):
+                folds = []
+                for at in (p, p + 2):
+                    even = got[pl.ds(16 * at + 4 * c + q, BA, stride=64), :]
+                    odd = got[pl.ds(16 * at + 8 + 4 * c + q, BA, stride=64), :]
+                    folds.append((jnp.where(low_half, even, pltpu.roll(odd, 64, 1)),
+                                  jnp.where(low_half, pltpu.roll(even, 64, 1), odd)))
+                lanes = slice(128 * p, 128 * p + 128)
+                for half in range(2):
+                    early, late = folds[0][half], folds[1][half]
                     at = slice(256 * c + 128 * half + 32 * q, 256 * c + 128 * half + 32 * q + 32)
-                    high, low = split(value)
-                    rows[0, at, 128 * p : 128 * p + 128] = high
-                    rows[1, at, 128 * p : 128 * p + 128] = low
-    leaving = []
+                    for parity, value in enumerate((early + late, early - late)):
+                        rows[parity, 0, at, lanes], rows[parity, 1, at, lanes] = split(value)
     for part in range(2):
         ky = slice(256 * part, 256 * part + 256)
-        data = (rows[0], rows[1])
+        data = (rows[part, 0], rows[part, 1])
         if part == 0:
-            copies[1].wait()
+            copies[0].wait()
         by_cos = dot3((y_fwd_in[0, 0, ky, :], y_fwd_in[1, 0, ky, :]), data, 1)
         by_sin = dot3((y_fwd_in[0, 1, ky, :], y_fwd_in[1, 1, ky, :]), data, 1)
         real = by_cos[:, :256] + by_sin[:, 256:]
         imag = by_cos[:, 256:] - by_sin[:, :256]
         if part == 0:
-            copies[2].wait()
+            copies[1].wait()
         forward = (z_fwd_in[0], z_fwd_in[1])
         real, imag = dot3(split(real), forward), dot3(split(imag), forward)
         real, imag = real[:, :256] + imag[:, 256:], imag[:, :256] - real[:, 256:]
 
-        held[0, ky, :] = real
-        held[1, ky, :] = imag
-        leaving += fetch([(held.at[:, ky, :], spectrum.at[:, ky, :])], sems.at[pl.ds(11 + part, 1)])
-    for copy in copies[3:]:
+        for i, value in enumerate((real[:, :128], real[:, 128:], imag[:, :128], imag[:, 128:])):
+            spectrum[pl.ds(512 * i + part, 256, stride=2), :] = value
+    for copy in copies[2:]:
         copy.wait()
     corner = lax.broadcasted_iota(jnp.int32, (8, AZ), 0)
-    for out, far, near, rech_at, x in ((up, 16, 24, 40, 15), (down, 8, 0, 32, 0)):
+    for out, far, near, rech_at, x in ((up, 16, 24, 40, 31), (down, 8, 0, 32, 0)):
         out[0:8, :] = edge[far : far + 8, :]
         out[8:16, :] = edge[near : near + 8, :]
         out[16:24, :] = edge[rech_at : rech_at + 8, :]
-        out[24:32, :] = jnp.where(corner == 0, edge[48 + x : 49 + x, :], edge[64 + x : 65 + x, :])
-    for copy in leaving:
-        copy.wait()
-
-
-def inverse_kernel(spectrum, amp, amp_row0, amp_row256, z_inv, y_fwd, sent,
-                   spectrum_in, amp_in, y_fwd_in, z_inv_in, row0_in, row256_in, lines, amps, sems):
+        out[24:32, :] = jnp.where(corner == 0, lo_halo[x : x + 1, :], hi_halo[x : x + 1, :])
+
+
+def inverse_kernel(spectrum, amp, amp_row0, amp_row256, z_inv, y_inv, sent,
+                   amp_in, y_inv_in, z_inv_in, lines, amps, out, sems):
     ga, ba = lax.axis_index("ga"), lax.axis_index("ba")
     packed = (ga == PACKED_GA) & (ba == 0)
     side = lax.rem(ba, 2)
     pairs = [(amp.at[:, 0], amp_in.at[:, side]), (amp.at[:, 1], amp_in.at[:, 1 - side]),
-             (amp_row0, row0_in), (amp_row256, row256_in), (spectrum, spectrum_in), (z_inv, z_inv_in),
-             (y_fwd.at[:, :, 0:256, :], y_fwd_in)]
+             (z_inv, z_inv_in),
+             (y_inv, y_inv_in)]
     copies = fetch(pairs, sems)
-    for i in range(4):
+    for i in range(2):
         copies[i].wait()
 
     @pl.when(packed)
@@ -230,15 +230,15 @@
         held = amp_in[...].reshape(EY, EZ)
         mirror = mirror_of(held)
         ky = lax.broadcasted_iota(jnp.int32, (EY, EZ), 0)
-        amps[...] = jnp.where(ky == 0, row0_in[0:1, :], jnp.where(ky < 256, mirror, held))
-        new = jnp.where(ky == 256, row256_in[0:1, :], jnp.where(ky < 256, held, mirror))
+        amps[...] = jnp.where(ky == 0, amp_row0[0:1, :], jnp.where(ky < 256, mirror, held))
+        new = jnp.where(ky == 256, amp_row256[0:1, :], jnp.where(ky < 256, held, mirror))
         amp_in[...] = new.reshape(amp_in.shape)
 
-    copies[4].wait()
-    copies[5].wait()
+    copies[2].wait()
     for part in range(2):
         ky = slice(256 * part, 256 * part + 256)
-        real, imag = spectrum_in[0, ky, :], spectrum_in[1, ky, :]
+        quarters = [spectrum[512 * i + 256 * part : 512 * i + 256 * part + 256, :] for i in range(4)]
+        real, imag = (jnp.concatenate(quarters[2 * i : 2 * i + 2], 1) for i in range(2))
 
         def back(scale, at):
             table = (z_inv_in[0], z_inv_in[1])
@@ -255,11 +255,11 @@
 
     def inverse(at):
         data = (lines[at, 0], lines[at, 1])
-        by_cos = dot3((y_fwd_in[0, 0], y_fwd_in[1, 0]), data)
-        by_sin = dot3((y_fwd_in[0, 1], y_fwd_in[1, 1]), data)
+        by_cos = dot3((y_inv_in[0, 0], y_inv_in[1, 0]), data)
+        by_sin = dot3((y_inv_in[0, 1], y_inv_in[1, 1]), data)
         return by_cos[:, :AZ] - by_sin[:, AZ:], by_cos[:, AZ:] + by_sin[:, :AZ]
 
-    copies[6].wait()
+    copies[3].wait()
     real, imag = inverse(0)
 
     def store(real, imag):
@@ -272,13 +272,15 @@
             moved = pltpu.roll(second if g % 2 else first, (AY - shift) % AY, 0)
             halo = jnp.where(peer == g, moved, halo)
         for i, rows in enumerate((real, imag, halo)):
-            sent[pl.ds(i, AY, stride=3), :] = rows
+            out[pl.ds(i, AY, stride=3), :] = rows
 
     store(real, imag)
 
     @pl.when(packed)
     def _():
         store(real, inverse(1)[1])
+
+    pltpu.sync_copy(out, sent)
 
 
 def field_kernel(got, table, lo_x, hi_x, sent, table_in, sems):
@@ -369,14 +371,15 @@
         press_out[pl.ds(y, 32, stride=8), :] = staged[4:36, :]
 
 
-def kernel_call(kernel, outs, inputs, scratch=(), held=(), outs_held=(), vmem=VMEM, flops=0, aliases=None):
+def kernel_call(kernel, outs, inputs, scratch=(), held=(), outs_held=(), vmem=VMEM, flops=0, aliases=None, hbm=()):
     whole = pl.BlockSpec(memory_space=pltpu.VMEM)
     there = pl.BlockSpec(memory_space=pl.ANY)
+    pinned = pl.BlockSpec(memory_space=pltpu.HBM)
     return pl.pallas_call(
         kernel,
         out_shape=[jax.ShapeDtypeStruct(shape, f32) for shape in outs],
-        in_specs=[there if i in held else whole for i in range(len(inputs))],
-        out_specs=[there if i in outs_held else whole for i in range(len(outs))],
+        in_specs=[pinned if i in hbm else there if i in held else whole for i in range(len(inputs))],
+        out_specs=[pinned if i in outs_held else whole for i in range(len(outs))],
         scratch_shapes=list(scratch),
         input_output_aliases=aliases or {},
         compiler_params=pltpu.CompilerParams(vmem_limit_bytes=vmem),
@@ -390,20 +393,20 @@
 
 
 def body(noise, amplitude, recharge, head_guess):
-    x_fwd, y_fwd, z_fwd, z_inv, x_inv = (jnp.asarray(t) for t in tables())
+    x_fwd, y_fwd, z_fwd, z_inv, y_inv, x_inv = (jnp.asarray(t) for t in tables())
     recharge = recharge.reshape(256, AZ)
     head = head_guess.reshape(256, AZ)
     memory, sems = pltpu.VMEM, pltpu.SemaphoreType.DMA
     (sent,) = kernel_call(
         enter_kernel, [(8 * DEVS, 128)], [noise.reshape(512, EX), x_fwd],
         [memory((512, EX), f32), memory(x_fwd.shape, bf16), memory((8 * DEVS, 128), f32), sems((3,))],
-        held=(0, 1), outs_held=(0,), flops=10**9,
+        hbm=(0, 1), outs_held=(0,), flops=10**9,
     )
     got = lax.all_to_all(sent, ("ba", "ga"), 0, 0, tiled=True)
     half, plane = (BA // 2, 16, EZ), (BA // 2, 2, 16, EZ)
     keep, give, amp_first, below, above = kernel_call(
         edges_kernel, [plane, half, (16, EZ), (96, AZ), (96, AZ)], [amplitude, head, recharge],
-        [memory((16, 40, EZ), f32), sems((1,))], held=(0,), vmem=8 * 2**20,
+        [memory((16, 40, EZ), f32), sems((1,))], hbm=(0,), vmem=8 * 2**20,
     )
     other = lax.ppermute(give, "ba", [(i, i ^ 1) for i in range(BA)])
     zero_near = lax.ppermute(amp_first, "ga", [(0, PACKED_GA)])
@@ -420,17 +423,17 @@
     halves = [list(range(side, BA, 2)) for side in range(2)]
     amp = lax.all_to_all(amp_sent.reshape(EY, EZ), "ba", 0, 0, tiled=True, axis_index_groups=halves)
     spectrum, to_up, to_down = kernel_call(
-        forward_kernel, [(2, EY, EZ), (32, AZ), (32, AZ)], [got, y_fwd, z_fwd, head, recharge, lo_halo, hi_halo],
-        [memory(value.shape, value.dtype) for value in (got, y_fwd, z_fwd)]
-        + [memory((2, 512, 512), bf16), memory((2, EY, EZ), f32), memory((80, AZ), f32), sems((13,))],
-        held=range(7), outs_held=(0,), flops=3 * 10**9,
+        forward_kernel, [(4 * EY, 128), (32, AZ), (32, AZ)], [got, y_fwd, z_fwd, head, recharge, lo_halo, hi_halo],
+        [memory(value.shape, value.dtype) for value in (y_fwd, z_fwd)]
+        + [memory((2, 2, 512, 256), bf16), memory((48, AZ), f32), sems((6,))],
+        hbm=range(1, 5), flops=3 * 10**9, vmem=VMEM_MIDDLE,
     )
     (sent,) = kernel_call(
         inverse_kernel, [(3 * AY, AZ)],
-        [spectrum, amp.reshape(plane), zero_near, amp_row, z_inv, y_fwd],
-        [memory((2, EY, EZ), f32), memory(plane, f32), memory((2, 2, AY, EY), bf16), memory(z_inv.shape, bf16)]
-        + [memory((16, EZ), f32)] * 2 + [memory((2, 2, EY, 2 * AZ), bf16), memory((EY, EZ), f32), sems((7,))],
-        held=range(6),
+        [spectrum, amp.reshape(plane), zero_near, amp_row, z_inv, y_inv],
+        [memory(plane, f32), memory((2, 2, AY, EY), bf16), memory(z_inv.shape, bf16)]
+        + [memory((2, 2, EY, 2 * AZ), bf16), memory((EY, EZ), f32), memory((3 * AY, AZ), f32), sems((4,))],
+        hbm=(4, 5), outs_held=(0,), vmem=VMEM_MIDDLE,
     )
     sent = sent.reshape(DEVS, 1, 3 * AZ)
     got = lax.all_to_all(sent, ("ba", "ga"), 0, 0, tiled=True).reshape(3 * DEVS, AZ)
@@ -439,7 +442,7 @@
     hi_x = lax.ppermute(to_down, "ga", down)
     (sent,) = kernel_call(
         field_kernel, [(CHUNK * GA, AZ)], [got, x_inv, lo_x, hi_x],
-        [memory(x_inv.shape, bf16), sems((1,))], held=(1, 2, 3), vmem=VMEM_END,
+        [memory(x_inv.shape, bf16), sems((1,))], held=(2, 3), hbm=(1,), vmem=VMEM_END,
     )
     got = lax.all_to_all(sent, "ga", 0, 0, tiled=True)
     ext = pltpu.VMEM((12 * XROWS, AZ), f32)

time: 126 us -> 125 us (level)
  Pallas kernels: 18.9 us -> 13.5 us
  local copies, waits for them, and re-layouts: 0.88 us -> 4.54 us
    pallas_call x7, Pallas kernels: 18.9 us -> 13.5 us  [kernel_call(): pl.pallas_call(kernel, out_shape=[jax.ShapeDtypeStruct(shape, f32) for sh...]
    unnamed x32 -> x20, local copies, waits for them, and re-layouts: 0.88 us -> 4.54 us
  transfers between devices with their start and end apart: 11 -> 11, of which waited for: 6 -> 6; matrix products, arithmetic and copies ran while one was open for 0% -> 0% of each run, Pallas kernels for 7% -> 4%
where the time goes in v9:
time: 125 us; the launch traced here: 124 us
  starting transfers between devices  48.7 us (39%)
  waiting for transfers between devices  45.3 us (36%)
  Pallas kernels  13.5 us (11%)
  blocking collectives  11.5 us (9%)
  local copies, waits for them, and re-layouts  4.54 us (4%)
    ppermute x1, waiting for transfers between devices, body(): hi_halo = lax.ppermute(below, 'ba', down)  16.8 us
    all_to_all x1, starting transfers between devices, body(): got = lax.all_to_all(sent, ('ba', 'ga'), 0, 0, tiled=True)  15.7 us
    pallas_call x7, Pallas kernels, kernel_call(): pl.pallas_call(kernel, out_shape=[jax.ShapeDtypeStruct(shape, f32) for sh...  13.5 us
    ppermute x1, waiting for transfers between devices, body(): lo_halo = lax.ppermute(above, 'ba', up)  13.2 us
    all_to_all x1, blocking collectives, body(): got = lax.all_to_all(sent, 'ga', 0, 0, tiled=True)  11.5 us
    all_to_all x1, waiting for transfers between devices, body(): lax.all_to_all(sent, ('ba', 'ga'), 0, 0, tiled=True).reshape(3 * DEVS, AZ)  9.1 us
    all_to_all x1, starting transfers between devices, body(): lax.all_to_all(amp_sent.reshape(EY, EZ), 'ba', 0, 0, tiled=True, axis_ind...  7.72 us
    all_to_all x1, starting transfers between devices, body(): lax.all_to_all(sent, ('ba', 'ga'), 0, 0, tiled=True).reshape(3 * DEVS, AZ)  7.31 us
  transfers between devices with their start and end apart: 11, of which 6 were waited for; matrix products, arithmetic and copies ran while one was open for 0% of the time, Pallas kernels for 4%

profile of v9, /device:TPU:1, one launch (start us, length us, event | category | flops | bytes accessed | tf_op | source)
XLA Modules:
  0.0 124.4 jit_solution(5677807678859443056)
XLA Ops:
  0.6 3.5 %shard_map.113 = f32[2048,128]{1,0:T(8,128)} custom-call(f32[512,512]{1,0:T(8,128)} %bitcast.26, bf16[2,512,256]{2,1,0:T(8,128)(2,1)} %constant.12.clone.table), custom_call_target="tpu_custom_call" | custom-call | flops 1000000000 | bytes 6291456 | tf_op jit(solution)/shard_map/pallas_call | solution.py:378
  4.2 15.7 %all-to-all-start = ((f32[256,8,128]{2,1,0:T(8,128)}), f32[256,8,128]{2,1,0:T(8,128)S(1)}, u32[]{:S(2)}, u32[]{:S(2)}) async-start(f32[256,8,128]{2,1,0:T(8,128)} %bitcast.25), calls=%async_computation | async-start | bytes 2097152 | tf_op jit(solution)/shard_map/all_to_all | solution.py:405
  19.9 1.2 shard_map.114
  21.1 6.3 %collective-permute-start.2 = (f32[16,16,256]{2,1,0:T(8,128)S(1)}, f32[16,16,256]{2,1,0:T(8,128)S(1)}, u32[]{:S(2)}, u32[]{:S(2)}) collective-permute-start(f32[16,16,256]{2,1,0:T(8,128)S(1)} %get-tuple-element.16), channel_id=1, source_target_pairs={{0,1},{1,0},{2,3},{3,2},{4,5},{5,4},{6,7},{7,6},{8,9},{9,8},{10,11... | collective-permute-start | bytes 786440 | tf_op jit(solution)/shard_map/ppermute | solution.py:411
  27.4 1.9 %collective-permute-start = (f32[96,128]{1,0:T(8,128)S(1)}, f32[96,128]{1,0:T(8,128)S(1)}, u32[]{:S(2)}, u32[]{:S(2)}) collective-permute-start(f32[96,128]{1,0:T(8,128)S(1)} %get-tuple-element.12), channel_id=1, source_target_pairs={{0,1},{1,2},{2,3},{3,4},{4,5},{5,6},{6,7},{7,8},{8,9},{9,10},{10,1... | collective-permute-start | bytes 147464 | tf_op jit(solution)/shard_map/ppermute | solution.py:418
  29.4 1.3 %collective-permute-start.1 = (f32[96,128]{1,0:T(8,128)S(1)}, f32[96,128]{1,0:T(8,128)S(1)}, u32[]{:S(2)}, u32[]{:S(2)}) collective-permute-start(f32[96,128]{1,0:T(8,128)S(1)} %get-tuple-element.13), channel_id=1, source_target_pairs={{1,0},{2,1},{3,2},{4,3},{5,4},{6,5},{7,6},{8,7},{9,8},{10,9},{11,1... | collective-permute-start | bytes 147464 | tf_op jit(solution)/shard_map/ppermute | solution.py:417
  30.7 0.7 collective-permute-start.4
  31.3 0.7 collective-permute-start.3
  32.0 13.2 %collective-permute-done.lo_halo = f32[96,128]{1,0:T(8,128)S(1)} collective-permute-done((f32[96,128]{1,0:T(8,128)S(1)}, f32[96,128]{1,0:T(8,128)S(1)}, u32[]{:S(2)}, u32[]{:S(2)}) %collective-permute-start) | collective-permute-done | bytes 49184 | tf_op jit(solution)/shard_map/ppermute | solution.py:418
  45.2 16.8 %collective-permute-done.1.hi_halo = f32[96,128]{1,0:T(8,128)S(1)} collective-permute-done((f32[96,128]{1,0:T(8,128)S(1)}, f32[96,128]{1,0:T(8,128)S(1)}, u32[]{:S(2)}, u32[]{:S(2)}) %collective-permute-start.1) | collective-permute-done | bytes 49184 | tf_op jit(solution)/shard_map/ppermute | solution.py:417
  62.0 0.7 shard_map.116
  62.8 7.7 %all-to-all-start.1 = ((f32[16,32,256]{2,1,0:T(8,128)}), f32[16,32,256]{2,1,0:T(8,128)S(1)}, u32[]{:S(2)}, u32[]{:S(2)}) async-start(f32[16,32,256]{2,1,0:T(8,128)} %bitcast.5), calls=%async_computation.1 | async-start | bytes 1048576 | tf_op jit(solution)/shard_map/all_to_all | solution.py:424
  70.5 0.0 copy-start
  70.5 0.0 copy-start.7
  70.5 1.4 %collective-permute-start.5 = (f32[16,256]{1,0:T(8,128)S(1)}, f32[16,256]{1,0:T(8,128)S(1)}, u32[]{:S(2)}, u32[]{:S(2)}) collective-permute-start(f32[16,256]{1,0:T(8,128)S(1)} %get-tuple-element.17), channel_id=1, source_target_pairs={{16,0},{48,32},{80,64},{112,96},{144,128},{176,160},{208,192},{240... | collective-permute-start | bytes 49160 | tf_op jit(solution)/shard_map/ppermute | solution.py:415
  72.0 1.2 copy-done.8
  73.2 1.0 copy-done.9
  74.2 3.5 %shard_map.115 = (f32[2048,128]{1,0:T(8,128)S(1)}, f32[32,128]{1,0:T(8,128)S(1)}, f32[32,128]{1,0:T(8,128)S(1)}) custom-call(f32[2048,128]{1,0:T(8,128)S(1)} %bitcast.14, bf16[2,2,512,256]{3,2,1,0:T(8,128)(2,1)S(1)} %copy-done.8, bf16[2,256,512]{2,1,0:T(8,128)(2,1)S(1)} %copy-done.9, f32[256,128]{1,0:T(8,128)S(1)} %bitcast.20, f32[256,128]{1,0:T(8,128)S(1)} %bitcast.23, ...), custom_call_target="tpu_custom_call" | custom-call | flops 3000000000 | bytes 6291456 | tf_op jit(solution)/shard_map/pallas_call | solution.py:378
  77.7 1.0 copy-done.1
  78.7 0.6 collective-permute-done.5.amp_row256
  79.3 1.5 %all-to-all-done.1 = f32[16,32,256]{2,1,0:T(8,128)S(1)} async-done(((f32[16,32,256]{2,1,0:T(8,128)}), f32[16,32,256]{2,1,0:T(8,128)S(1)}, u32[]{:S(2)}, u32[]{:S(2)}) %all-to-all-start.1) | async-done | bytes 524320 | tf_op jit(solution)/shard_map/all_to_all | solution.py:424
  80.8 1.2 copy-done.2
  82.0 2.4 %shard_map.117 = f32[768,128]{1,0:T(8,128)} custom-call(f32[2048,128]{1,0:T(8,128)S(1)} %copy-done.2, f32[16,2,16,256]{3,2,1,0:T(8,128)S(1)} %bitcast.15, f32[16,256]{1,0:T(8,128)S(1)} %collective-permute-done.3.zero_near.amp_row0, f32[16,256]{1,0:T(8,128)S(1)} %collective-permute-done.5.amp_row256, bf16[2,256,256]{2,1,0:T(8,128)(2,1)S(1)} %copy-done.7, ...), custom_call_target="tpu_custom_call" | custom-call | tf_op jit(solution)/shard_map/pallas_call | solution.py:378
  84.4 0.0 copy-start.4
  84.4 7.3 %all-to-all-start.2 = ((f32[256,1,384]{2,1,0:T(1,128)}), f32[256,1,384]{2,1,0:T(1,128)S(1)}, u32[]{:S(2)}, u32[]{:S(2)}) async-start(f32[256,1,384]{2,1,0:T(1,128)} %bitcast.7), calls=%async_computation.2 | async-start | bytes 786432 | tf_op jit(solution)/shard_map/all_to_all | solution.py:439
  91.8 3.8 %collective-permute-start.6 = (f32[32,128]{1,0:T(8,128)S(1)}, f32[32,128]{1,0:T(8,128)S(1)}, u32[]{:S(2)}, u32[]{:S(2)}) collective-permute-start(f32[32,128]{1,0:T(8,128)S(1)} %get-tuple-element.18), channel_id=1, source_target_pairs={{0,32},{32,64},{64,96},{96,128},{128,160},{160,192},{192,224},{1,3... | collective-permute-start | bytes 49160 | tf_op jit(solution)/shard_map/ppermute | solution.py:441
  95.6 1.9 %collective-permute-start.7 = (f32[32,128]{1,0:T(8,128)S(1)}, f32[32,128]{1,0:T(8,128)S(1)}, u32[]{:S(2)}, u32[]{:S(2)}) collective-permute-start(f32[32,128]{1,0:T(8,128)S(1)} %get-tuple-element.19), channel_id=1, source_target_pairs={{32,0},{64,32},{96,64},{128,96},{160,128},{192,160},{224,192},{33,... | collective-permute-start | bytes 49160 | tf_op jit(solution)/shard_map/ppermute | solution.py:442
  97.5 4.1 %collective-permute-done.7.hi_x = f32[32,128]{1,0:T(8,128)S(1)} collective-permute-done((f32[32,128]{1,0:T(8,128)S(1)}, f32[32,128]{1,0:T(8,128)S(1)}, u32[]{:S(2)}, u32[]{:S(2)}) %collective-permute-start.7) | collective-permute-done | bytes 16416 | tf_op jit(solution)/shard_map/ppermute | solution.py:442
  101.6 9.1 %all-to-all-done.2 = f32[256,1,384]{2,1,0:T(1,128)S(1)} async-done(((f32[256,1,384]{2,1,0:T(1,128)}), f32[256,1,384]{2,1,0:T(1,128)S(1)}, u32[]{:S(2)}, u32[]{:S(2)}) %all-to-all-start.2) | async-done | bytes 393248 | tf_op jit(solution)/shard_map/all_to_all | solution.py:439
  110.7 0.8 shard_map.118
  111.5 11.5 %all_to_all.36 = f32[8,64,128]{2,1,0:T(8,128)S(1)} all-to-all(f32[8,64,128]{2,1,0:T(8,128)S(1)} %bitcast.18), channel_id=1, replica_groups=mesh['ga'=8,'ba'=32] {'ga'}, dimensions={0} | all-to-all | bytes 524288 | tf_op jit(solution)/shard_map/all_to_all | solution.py:447
  123.0 1.4 %shard_map.119 = (f32[256,128]{1,0:T(8,128)}, f32[256,128]{1,0:T(8,128)}) custom-call(f32[512,128]{1,0:T(8,128)S(1)} %bitcast.17, f32[256,128]{1,0:T(8,128)S(1)} %bitcast.21, f32[256,128]{1,0:T(8,128)S(1)} %bitcast.24, f32[96,128]{1,0:T(8,128)S(1)} %collective-permute-done.lo_halo, f32[96,128]{1,0:T(8,128)S(1)} %collective-permute-done.1.hi_halo, ...), custom_call_target="tpu_custom_call" | custom-call | tf_op jit(solution)/shard_map/pallas_call | solution.py:378
  (18 shorter events, 0.0 us)
Async XLA Ops:
  4.2 15.7 %copy-start.3 = (f32[16,64,256]{2,1,0:T(8,128)S(1)}, f32[16,64,256]{2,1,0:T(8,128)}, u32[]{:S(2)}) copy-start(f32[16,64,256]{2,1,0:T(8,128)} %amp.1) | copy-start | bytes 3145732
  4.2 15.7 %copy-start.5 = (f32[32,8,128]{2,1,0:T(8,128)S(1)}, f32[32,8,128]{2,1,0:T(8,128)}, u32[]{:S(2)}) copy-start(f32[32,8,128]{2,1,0:T(8,128)} %param.13) | copy-start | bytes 393220
  4.2 15.7 %copy-start.6 = (f32[32,8,128]{2,1,0:T(8,128)S(1)}, f32[32,8,128]{2,1,0:T(8,128)}, u32[]{:S(2)}) copy-start(f32[32,8,128]{2,1,0:T(8,128)} %param.12) | copy-start | bytes 393220
  4.2 57.8 %all-to-all-start = ((f32[256,8,128]{2,1,0:T(8,128)}), f32[256,8,128]{2,1,0:T(8,128)S(1)}, u32[]{:S(2)}, u32[]{:S(2)}) async-start(f32[256,8,128]{2,1,0:T(8,128)} %bitcast.25), calls=%async_computation | async-start | bytes 2097152 | tf_op jit(solution)/shard_map/all_to_all | solution.py:405
  21.1 40.9 %collective-permute-start.2 = (f32[16,16,256]{2,1,0:T(8,128)S(1)}, f32[16,16,256]{2,1,0:T(8,128)S(1)}, u32[]{:S(2)}, u32[]{:S(2)}) collective-permute-start(f32[16,16,256]{2,1,0:T(8,128)S(1)} %get-tuple-element.16), channel_id=1, source_target_pairs={{0,1},{1,0},{2,3},{3,2},{4,5},{5,4},{6,7},{7,6},{8,9},{9,8},{10,11... | collective-permute-start | bytes 786440 | tf_op jit(solution)/shard_map/ppermute | solution.py:411
  27.4 17.8 %collective-permute-start = (f32[96,128]{1,0:T(8,128)S(1)}, f32[96,128]{1,0:T(8,128)S(1)}, u32[]{:S(2)}, u32[]{:S(2)}) collective-permute-start(f32[96,128]{1,0:T(8,128)S(1)} %get-tuple-element.12), channel_id=1, source_target_pairs={{0,1},{1,2},{2,3},{3,4},{4,5},{5,6},{6,7},{7,8},{8,9},{9,10},{10,1... | collective-permute-start | bytes 147464 | tf_op jit(solution)/shard_map/ppermute | solution.py:418
  29.4 32.7 %collective-permute-start.1 = (f32[96,128]{1,0:T(8,128)S(1)}, f32[96,128]{1,0:T(8,128)S(1)}, u32[]{:S(2)}, u32[]{:S(2)}) collective-permute-start(f32[96,128]{1,0:T(8,128)S(1)} %get-tuple-element.13), channel_id=1, source_target_pairs={{1,0},{2,1},{3,2},{4,3},{5,4},{6,5},{7,6},{8,7},{9,8},{10,9},{11,1... | collective-permute-start | bytes 147464 | tf_op jit(solution)/shard_map/ppermute | solution.py:417
  30.7 1.3 %collective-permute-start.4 = (f32[16,256]{1,0:T(8,128)S(1)}, f32[16,256]{1,0:T(8,128)S(1)}, u32[]{:S(2)}, u32[]{:S(2)}) collective-permute-start(f32[16,256]{1,0:T(8,128)S(1)} %get-tuple-element.17), channel_id=1, source_target_pairs={{17,144},{19,146},{21,148},{23,150},{25,152},{27,154},{29,156},{31... | collective-permute-start | bytes 49160 | tf_op jit(solution)/shard_map/ppermute | solution.py:414
  31.3 0.7 collective-permute-start.3
  62.8 18.0 %all-to-all-start.1 = ((f32[16,32,256]{2,1,0:T(8,128)}), f32[16,32,256]{2,1,0:T(8,128)S(1)}, u32[]{:S(2)}, u32[]{:S(2)}) async-start(f32[16,32,256]{2,1,0:T(8,128)} %bitcast.5), calls=%async_computation.1 | async-start | bytes 1048576 | tf_op jit(solution)/shard_map/all_to_all | solution.py:424
  70.5 10.3 %copy-start = (bf16[2,2,256,512]{3,2,1,0:T(8,128)(2,1)S(1)}, bf16[2,2,256,512]{3,2,1,0:T(8,128)(2,1)}, u32[]{:S(2)}) copy-start(bf16[2,2,256,512]{3,2,1,0:T(8,128)(2,1)} %constant.16.clone.y_inv) | copy-start | bytes 3145732
  70.5 10.3 %copy-start.7 = (bf16[2,256,256]{2,1,0:T(8,128)(2,1)S(1)}, bf16[2,256,256]{2,1,0:T(8,128)(2,1)}, u32[]{:S(2)}) copy-start(bf16[2,256,256]{2,1,0:T(8,128)(2,1)} %constant.15.clone.z_inv) | copy-start | bytes 786436
  70.5 8.8 %collective-permute-start.5 = (f32[16,256]{1,0:T(8,128)S(1)}, f32[16,256]{1,0:T(8,128)S(1)}, u32[]{:S(2)}, u32[]{:S(2)}) collective-permute-start(f32[16,256]{1,0:T(8,128)S(1)} %get-tuple-element.17), channel_id=1, source_target_pairs={{16,0},{48,32},{80,64},{112,96},{144,128},{176,160},{208,192},{240... | collective-permute-start | bytes 49160 | tf_op jit(solution)/shard_map/ppermute | solution.py:415
  72.0 1.2 copy-start.8
  73.2 1.0 copy-start.9
  77.7 1.0 copy-start.1
  80.8 1.2 copy-start.2
  84.4 26.3 %copy-start.4 = (bf16[2,320,512]{2,1,0:T(8,128)(2,1)S(1)}, bf16[2,320,512]{2,1,0:T(8,128)(2,1)}, u32[]{:S(2)}) copy-start(bf16[2,320,512]{2,1,0:T(8,128)(2,1)} %constant.17.clone.table) | copy-start | bytes 1966084
  84.4 26.2 %all-to-all-start.2 = ((f32[256,1,384]{2,1,0:T(1,128)}), f32[256,1,384]{2,1,0:T(1,128)S(1)}, u32[]{:S(2)}, u32[]{:S(2)}) async-start(f32[256,1,384]{2,1,0:T(1,128)} %bitcast.7), calls=%async_computation.2 | async-start | bytes 786432 | tf_op jit(solution)/shard_map/all_to_all | solution.py:439
  91.8 5.7 %collective-permute-start.6 = (f32[32,128]{1,0:T(8,128)S(1)}, f32[32,128]{1,0:T(8,128)S(1)}, u32[]{:S(2)}, u32[]{:S(2)}) collective-permute-start(f32[32,128]{1,0:T(8,128)S(1)} %get-tuple-element.18), channel_id=1, source_target_pairs={{0,32},{32,64},{64,96},{96,128},{128,160},{160,192},{192,224},{1,3... | collective-permute-start | bytes 49160 | tf_op jit(solution)/shard_map/ppermute | solution.py:441
  95.6 6.0 %collective-permute-start.7 = (f32[32,128]{1,0:T(8,128)S(1)}, f32[32,128]{1,0:T(8,128)S(1)}, u32[]{:S(2)}, u32[]{:S(2)}) collective-permute-start(f32[32,128]{1,0:T(8,128)S(1)} %get-tuple-element.19), channel_id=1, source_target_pairs={{32,0},{64,32},{96,64},{128,96},{160,128},{192,160},{224,192},{33,... | collective-permute-start | bytes 49160 | tf_op jit(solution)/shard_map/ppermute | solution.py:442

commit v10 on v9

--- a/solution.py
+++ b/solution.py
@@ -74,7 +74,11 @@
     x_inv = np.concatenate([back_re, back_im], 1) / (EX * EY * EZ)
     y_inv = y_fwd[:, :AY]
     y_fwd = np.concatenate([y_fwd[:, 0::2, : EY // 2], y_fwd[:, 1::2, : EY // 2]], 1)
-    return tuple(split_np(t) for t in (x_fwd, y_fwd, z_fwd, z_inv, y_inv, x_inv))
+    z_fwd = z_fwd.reshape(EZ, 2, EZ).transpose(1, 0, 2)
+    forward = np.concatenate([split_np(t).reshape(-1, EZ) for t in (y_fwd, z_fwd)])
+    z_inv = split_np(z_inv)
+    inverse = np.concatenate([split_np(y_inv).reshape(-1, EY), np.concatenate([z_inv[0], z_inv[1]], 1)])
+    return split_np(x_fwd), forward, inverse, split_np(x_inv)
 
 
 def split(value):
@@ -164,9 +168,9 @@
     return total
 
 
-def forward_kernel(got, y_fwd, z_fwd, head, rech, lo_halo, hi_halo, spectrum, up, down,
-                   y_fwd_in, z_fwd_in, rows, edge, sems):
-    pairs = [(y_fwd, y_fwd_in), (z_fwd, z_fwd_in), (head.at[0:16, :], edge.at[0:16, :]),
+def forward_kernel(got, table, head, rech, lo_halo, hi_halo, spectrum, up, down,
+                   rows, edge, sems):
+    pairs = [(head.at[0:16, :], edge.at[0:16, :]),
              (head.at[240:256, :], edge.at[16:32, :]), (rech.at[0:8, :], edge.at[32:40, :]),
              (rech.at[248:256, :], edge.at[40:48, :])]
     copies = fetch(pairs, sems)
@@ -189,21 +193,19 @@
     for part in range(2):
         ky = slice(256 * part, 256 * part + 256)
         data = (rows[part, 0], rows[part, 1])
-        if part == 0:
-            copies[0].wait()
-        by_cos = dot3((y_fwd_in[0, 0, ky, :], y_fwd_in[1, 0, ky, :]), data, 1)
-        by_sin = dot3((y_fwd_in[0, 1, ky, :], y_fwd_in[1, 1, ky, :]), data, 1)
+        by_cos, by_sin = (
+            dot3([table[at : at + 256, :] for at in (512 * c + 256 * part, 1024 + 512 * c + 256 * part)], data, 1)
+            for c in range(2)
+        )
         real = by_cos[:, :256] + by_sin[:, 256:]
         imag = by_cos[:, 256:] - by_sin[:, :256]
-        if part == 0:
-            copies[1].wait()
-        forward = (z_fwd_in[0], z_fwd_in[1])
+        forward = [jnp.concatenate([table[at : at + 256, :], table[at + 256 : at + 512, :]], 1) for at in (2048, 2560)]
         real, imag = dot3(split(real), forward), dot3(split(imag), forward)
         real, imag = real[:, :256] + imag[:, 256:], imag[:, :256] - real[:, 256:]
 
         for i, value in enumerate((real[:, :128], real[:, 128:], imag[:, :128], imag[:, 128:])):
             spectrum[pl.ds(512 * i + part, 256, stride=2), :] = value
-    for copy in copies[2:]:
+    for copy in copies:
         copy.wait()
     corner = lax.broadcasted_iota(jnp.int32, (8, AZ), 0)
     for out, far, near, rech_at, x in ((up, 16, 24, 40, 31), (down, 8, 0, 32, 0)):
@@ -213,14 +215,12 @@
         out[24:32, :] = jnp.where(corner == 0, lo_halo[x : x + 1, :], hi_halo[x : x + 1, :])
 
 
-def inverse_kernel(spectrum, amp, amp_row0, amp_row256, z_inv, y_inv, sent,
-                   amp_in, y_inv_in, z_inv_in, lines, amps, out, sems):
+def inverse_kernel(spectrum, amp, amp_row0, amp_row256, table, sent,
+                   amp_in, lines, amps, out, sems):
     ga, ba = lax.axis_index("ga"), lax.axis_index("ba")
     packed = (ga == PACKED_GA) & (ba == 0)
     side = lax.rem(ba, 2)
-    pairs = [(amp.at[:, 0], amp_in.at[:, side]), (amp.at[:, 1], amp_in.at[:, 1 - side]),
-             (z_inv, z_inv_in),
-             (y_inv, y_inv_in)]
+    pairs = [(amp.at[:, 0], amp_in.at[:, side]), (amp.at[:, 1], amp_in.at[:, 1 - side])]
     copies = fetch(pairs, sems)
     for i in range(2):
         copies[i].wait()
@@ -234,15 +234,14 @@
         new = jnp.where(ky == 256, amp_row256[0:1, :], jnp.where(ky < 256, held, mirror))
         amp_in[...] = new.reshape(amp_in.shape)
 
-    copies[2].wait()
     for part in range(2):
         ky = slice(256 * part, 256 * part + 256)
         quarters = [spectrum[512 * i + 256 * part : 512 * i + 256 * part + 256, :] for i in range(4)]
         real, imag = (jnp.concatenate(quarters[2 * i : 2 * i + 2], 1) for i in range(2))
 
         def back(scale, at):
-            table = (z_inv_in[0], z_inv_in[1])
-            re, im = dot3(split(real * scale), table), dot3(split(imag * scale), table)
+            turn = (table[1024:1280, 0:256], table[1024:1280, 256:512])
+            re, im = dot3(split(real * scale), turn), dot3(split(imag * scale), turn)
             for c, value in enumerate((re[:, :128] - im[:, 128:], im[:, :128] + re[:, 128:])):
                 lanes = slice(128 * c, 128 * c + 128)
                 lines[at, 0, ky, lanes], lines[at, 1, ky, lanes] = split(value)
@@ -255,11 +254,11 @@
 
     def inverse(at):
         data = (lines[at, 0], lines[at, 1])
-        by_cos = dot3((y_inv_in[0, 0], y_inv_in[1, 0]), data)
-        by_sin = dot3((y_inv_in[0, 1], y_inv_in[1, 1]), data)
+        by_cos, by_sin = (
+            dot3([table[at : at + 256, :] for at in (256 * c, 512 + 256 * c)], data) for c in range(2)
+        )
         return by_cos[:, :AZ] - by_sin[:, AZ:], by_cos[:, AZ:] + by_sin[:, :AZ]
 
-    copies[3].wait()
     real, imag = inverse(0)
 
     def store(real, imag):
@@ -393,7 +392,7 @@
 
 
 def body(noise, amplitude, recharge, head_guess):
-    x_fwd, y_fwd, z_fwd, z_inv, y_inv, x_inv = (jnp.asarray(t) for t in tables())
+    x_fwd, forward_table, inverse_table, x_inv = (jnp.asarray(t) for t in tables())
     recharge = recharge.reshape(256, AZ)
     head = head_guess.reshape(256, AZ)
     memory, sems = pltpu.VMEM, pltpu.SemaphoreType.DMA
@@ -423,17 +422,15 @@
     halves = [list(range(side, BA, 2)) for side in range(2)]
     amp = lax.all_to_all(amp_sent.reshape(EY, EZ), "ba", 0, 0, tiled=True, axis_index_groups=halves)
     spectrum, to_up, to_down = kernel_call(
-        forward_kernel, [(4 * EY, 128), (32, AZ), (32, AZ)], [got, y_fwd, z_fwd, head, recharge, lo_halo, hi_halo],
-        [memory(value.shape, value.dtype) for value in (y_fwd, z_fwd)]
-        + [memory((2, 2, 512, 256), bf16), memory((48, AZ), f32), sems((6,))],
-        hbm=range(1, 5), flops=3 * 10**9, vmem=VMEM_MIDDLE,
+        forward_kernel, [(4 * EY, 128), (32, AZ), (32, AZ)], [got, forward_table, head, recharge, lo_halo, hi_halo],
+        [memory((2, 2, 512, 256), bf16), memory((48, AZ), f32), sems((4,))],
+        hbm=(2, 3), flops=3 * 10**9, vmem=VMEM_MIDDLE,
     )
     (sent,) = kernel_call(
         inverse_kernel, [(3 * AY, AZ)],
-        [spectrum, amp.reshape(plane), zero_near, amp_row, z_inv, y_inv],
-        [memory(plane, f32), memory((2, 2, AY, EY), bf16), memory(z_inv.shape, bf16)]
-        + [memory((2, 2, EY, 2 * AZ), bf16), memory((EY, EZ), f32), memory((3 * AY, AZ), f32), sems((4,))],
-        hbm=(4, 5), outs_held=(0,), vmem=VMEM_MIDDLE,
+        [spectrum, amp.reshape(plane), zero_near, amp_row, inverse_table],
+        [memory(plane, f32), memory((2, 2, EY, 2 * AZ), bf16), memory((EY, EZ), f32), memory((3 * AY, AZ), f32), sems((2,))],
+        outs_held=(0,), vmem=VMEM_MIDDLE,
     )
     sent = sent.reshape(DEVS, 1, 3 * AZ)
     got = lax.all_to_all(sent, ("ba", "ga"), 0, 0, tiled=True).reshape(3 * DEVS, AZ)

time: 125 us -> 125 us (level)
  waiting for transfers between devices: 45.3 us -> 46.7 us
    ppermute x1, waiting for transfers between devices: 0.57 us -> 1.99 us  [body(): amp_row = lax.ppermute(amp_first, 'ba', [(BA // 2, 0)])]
    unnamed x20 -> x16, local copies, waits for them, and re-layouts: 4.54 us -> 3.64 us
  transfers between devices with their start and end apart: 11 -> 11, of which waited for: 6 -> 6; matrix products, arithmetic and copies ran while one was open for 0% -> 0% of each run, Pallas kernels for 4% -> 3%
where the time goes in v10:
time: 125 us; the launch traced here: 124 us
  starting transfers between devices  48.5 us (39%)
  waiting for transfers between devices  46.7 us (37%)
  Pallas kernels  12.9 us (10%)
  blocking collectives  11.5 us (9%)
  local copies, waits for them, and re-layouts  3.64 us (3%)
    ppermute x1, waiting for transfers between devices, body(): hi_halo = lax.ppermute(below, 'ba', down)  16.8 us
    all_to_all x1, starting transfers between devices, body(): got = lax.all_to_all(sent, ('ba', 'ga'), 0, 0, tiled=True)  15.7 us
    ppermute x1, waiting for transfers between devices, body(): lo_halo = lax.ppermute(above, 'ba', up)  13.2 us
    pallas_call x7, Pallas kernels, kernel_call(): pl.pallas_call(kernel, out_shape=[jax.ShapeDtypeStruct(shape, f32) for sh...  12.9 us
    all_to_all x1, blocking collectives, body(): got = lax.all_to_all(sent, 'ga', 0, 0, tiled=True)  11.5 us
    all_to_all x1, waiting for transfers between devices, body(): lax.all_to_all(sent, ('ba', 'ga'), 0, 0, tiled=True).reshape(3 * DEVS, AZ)  9.1 us
    all_to_all x1, starting transfers between devices, body(): lax.all_to_all(amp_sent.reshape(EY, EZ), 'ba', 0, 0, tiled=True, axis_ind...  7.72 us
    all_to_all x1, starting transfers between devices, body(): lax.all_to_all(sent, ('ba', 'ga'), 0, 0, tiled=True).reshape(3 * DEVS, AZ)  7.16 us
  transfers between devices with their start and end apart: 11, of which 6 were waited for; matrix products, arithmetic and copies ran while one was open for 0% of the time, Pallas kernels for 3%

profile of v10, /device:TPU:1, one launch (start us, length us, event | category | flops | bytes accessed | tf_op | source)
XLA Modules:
  0.0 124.1 jit_solution(723208925188865088)
XLA Ops:
  0.6 3.5 %shard_map.95 = f32[2048,128]{1,0:T(8,128)} custom-call(f32[512,512]{1,0:T(8,128)} %bitcast.26, bf16[2,512,256]{2,1,0:T(8,128)(2,1)} %constant.8.clone.table), custom_call_target="tpu_custom_call" | custom-call | flops 1000000000 | bytes 6291456 | tf_op jit(solution)/shard_map/pallas_call | solution.py:377
  4.1 0.0 copy-start.3
  4.2 0.0 copy-start.5
  4.2 15.7 %all-to-all-start = ((f32[256,8,128]{2,1,0:T(8,128)}), f32[256,8,128]{2,1,0:T(8,128)S(1)}, u32[]{:S(2)}, u32[]{:S(2)}) async-start(f32[256,8,128]{2,1,0:T(8,128)} %bitcast.25), calls=%async_computation | async-start | bytes 2097152 | tf_op jit(solution)/shard_map/all_to_all | solution.py:404
  19.9 1.2 shard_map.96
  21.1 6.3 %collective-permute-start.2 = (f32[16,16,256]{2,1,0:T(8,128)S(1)}, f32[16,16,256]{2,1,0:T(8,128)S(1)}, u32[]{:S(2)}, u32[]{:S(2)}) collective-permute-start(f32[16,16,256]{2,1,0:T(8,128)S(1)} %get-tuple-element.16), channel_id=1, source_target_pairs={{0,1},{1,0},{2,3},{3,2},{4,5},{5,4},{6,7},{7,6},{8,9},{9,8},{10,11... | collective-permute-start | bytes 786440 | tf_op jit(solution)/shard_map/ppermute | solution.py:410
  27.4 1.9 %collective-permute-start = (f32[96,128]{1,0:T(8,128)S(1)}, f32[96,128]{1,0:T(8,128)S(1)}, u32[]{:S(2)}, u32[]{:S(2)}) collective-permute-start(f32[96,128]{1,0:T(8,128)S(1)} %get-tuple-element.12), channel_id=1, source_target_pairs={{0,1},{1,2},{2,3},{3,4},{4,5},{5,6},{6,7},{7,8},{8,9},{9,10},{10,1... | collective-permute-start | bytes 147464 | tf_op jit(solution)/shard_map/ppermute | solution.py:417
  29.3 1.3 %collective-permute-start.1 = (f32[96,128]{1,0:T(8,128)S(1)}, f32[96,128]{1,0:T(8,128)S(1)}, u32[]{:S(2)}, u32[]{:S(2)}) collective-permute-start(f32[96,128]{1,0:T(8,128)S(1)} %get-tuple-element.13), channel_id=1, source_target_pairs={{1,0},{2,1},{3,2},{4,3},{5,4},{6,5},{7,6},{8,7},{9,8},{10,9},{11,1... | collective-permute-start | bytes 147464 | tf_op jit(solution)/shard_map/ppermute | solution.py:416
  30.6 0.7 collective-permute-start.4
  31.3 0.7 collective-permute-start.3
  32.0 13.2 %collective-permute-done.lo_halo = f32[96,128]{1,0:T(8,128)S(1)} collective-permute-done((f32[96,128]{1,0:T(8,128)S(1)}, f32[96,128]{1,0:T(8,128)S(1)}, u32[]{:S(2)}, u32[]{:S(2)}) %collective-permute-start) | collective-permute-done | bytes 49184 | tf_op jit(solution)/shard_map/ppermute | solution.py:417
  45.2 16.8 %collective-permute-done.1.hi_halo = f32[96,128]{1,0:T(8,128)S(1)} collective-permute-done((f32[96,128]{1,0:T(8,128)S(1)}, f32[96,128]{1,0:T(8,128)S(1)}, u32[]{:S(2)}, u32[]{:S(2)}) %collective-permute-start.1) | collective-permute-done | bytes 49184 | tf_op jit(solution)/shard_map/ppermute | solution.py:416
  62.0 0.7 shard_map.98
  62.7 7.7 %all-to-all-start.1 = ((f32[16,32,256]{2,1,0:T(8,128)}), f32[16,32,256]{2,1,0:T(8,128)S(1)}, u32[]{:S(2)}, u32[]{:S(2)}) async-start(f32[16,32,256]{2,1,0:T(8,128)} %bitcast.5), calls=%async_computation.1 | async-start | bytes 1048576 | tf_op jit(solution)/shard_map/all_to_all | solution.py:423
  70.5 0.0 copy-start
  70.5 1.4 %collective-permute-start.5 = (f32[16,256]{1,0:T(8,128)S(1)}, f32[16,256]{1,0:T(8,128)S(1)}, u32[]{:S(2)}, u32[]{:S(2)}) collective-permute-start(f32[16,256]{1,0:T(8,128)S(1)} %get-tuple-element.17), channel_id=1, source_target_pairs={{16,0},{48,32},{80,64},{112,96},{144,128},{176,160},{208,192},{240... | collective-permute-start | bytes 49160 | tf_op jit(solution)/shard_map/ppermute | solution.py:414
  71.9 0.0 copy-start.7
  71.9 1.4 %copy-done.7 = bf16[3072,256]{1,0:T(8,128)(2,1)S(1)} copy-done((bf16[3072,256]{1,0:T(8,128)(2,1)S(1)}, bf16[3072,256]{1,0:T(8,128)(2,1)}, u32[]{:S(2)}) %copy-start.7) | copy-done | bytes 1572888
  73.3 3.0 %shard_map.97 = (f32[2048,128]{1,0:T(8,128)S(1)}, f32[32,128]{1,0:T(8,128)S(1)}, f32[32,128]{1,0:T(8,128)S(1)}) custom-call(f32[2048,128]{1,0:T(8,128)S(1)} %bitcast.14, bf16[3072,256]{1,0:T(8,128)(2,1)S(1)} %copy-done.7, f32[256,128]{1,0:T(8,128)S(1)} %bitcast.20, f32[256,128]{1,0:T(8,128)S(1)} %bitcast.23, f32[96,128]{1,0:T(8,128)S(1)} %collective-permute-done.lo_halo, ...), custom_call_target="tpu_custom_call" | custom-call | flops 3000000000 | bytes 6291456 | tf_op jit(solution)/shard_map/pallas_call | solution.py:377
  76.3 1.0 copy-done.1
  77.3 2.0 %collective-permute-done.5.amp_row256 = f32[16,256]{1,0:T(8,128)S(1)} collective-permute-done((f32[16,256]{1,0:T(8,128)S(1)}, f32[16,256]{1,0:T(8,128)S(1)}, u32[]{:S(2)}, u32[]{:S(2)}) %collective-permute-start.5) | collective-permute-done | bytes 16416 | tf_op jit(solution)/shard_map/ppermute | solution.py:414
  79.3 1.5 %all-to-all-done.1 = f32[16,32,256]{2,1,0:T(8,128)S(1)} async-done(((f32[16,32,256]{2,1,0:T(8,128)}), f32[16,32,256]{2,1,0:T(8,128)S(1)}, u32[]{:S(2)}, u32[]{:S(2)}) %all-to-all-start.1) | async-done | bytes 524320 | tf_op jit(solution)/shard_map/all_to_all | solution.py:423
  80.8 1.2 copy-done.2
  82.0 2.3 %shard_map.99 = f32[768,128]{1,0:T(8,128)} custom-call(f32[2048,128]{1,0:T(8,128)S(1)} %copy-done.2, f32[16,2,16,256]{3,2,1,0:T(8,128)S(1)} %bitcast.15, f32[16,256]{1,0:T(8,128)S(1)} %collective-permute-done.3.zero_near.amp_row0, f32[16,256]{1,0:T(8,128)S(1)} %collective-permute-done.5.amp_row256, bf16[1280,512]{1,0:T(8,128)(2,1)S(1)} %copy-done), custom_call_target="tpu_custom_call" | custom-call | tf_op jit(solution)/shard_map/pallas_call | solution.py:377
  84.3 7.2 %all-to-all-start.2 = ((f32[256,1,384]{2,1,0:T(1,128)}), f32[256,1,384]{2,1,0:T(1,128)S(1)}, u32[]{:S(2)}, u32[]{:S(2)}) async-start(f32[256,1,384]{2,1,0:T(1,128)} %bitcast.7), calls=%async_computation.2 | async-start | bytes 786432 | tf_op jit(solution)/shard_map/all_to_all | solution.py:436
  91.5 3.8 %collective-permute-start.6 = (f32[32,128]{1,0:T(8,128)S(1)}, f32[32,128]{1,0:T(8,128)S(1)}, u32[]{:S(2)}, u32[]{:S(2)}) collective-permute-start(f32[32,128]{1,0:T(8,128)S(1)} %get-tuple-element.18), channel_id=1, source_target_pairs={{0,32},{32,64},{64,96},{96,128},{128,160},{160,192},{192,224},{1,3... | collective-permute-start | bytes 49160 | tf_op jit(solution)/shard_map/ppermute | solution.py:438
  95.3 1.9 %collective-permute-start.7 = (f32[32,128]{1,0:T(8,128)S(1)}, f32[32,128]{1,0:T(8,128)S(1)}, u32[]{:S(2)}, u32[]{:S(2)}) collective-permute-start(f32[32,128]{1,0:T(8,128)S(1)} %get-tuple-element.19), channel_id=1, source_target_pairs={{32,0},{64,32},{96,64},{128,96},{160,128},{192,160},{224,192},{33,... | collective-permute-start | bytes 49160 | tf_op jit(solution)/shard_map/ppermute | solution.py:439
  97.2 4.1 %collective-permute-done.7.hi_x = f32[32,128]{1,0:T(8,128)S(1)} collective-permute-done((f32[32,128]{1,0:T(8,128)S(1)}, f32[32,128]{1,0:T(8,128)S(1)}, u32[]{:S(2)}, u32[]{:S(2)}) %collective-permute-start.7) | collective-permute-done | bytes 16416 | tf_op jit(solution)/shard_map/ppermute | solution.py:439
  101.3 9.1 %all-to-all-done.2 = f32[256,1,384]{2,1,0:T(1,128)S(1)} async-done(((f32[256,1,384]{2,1,0:T(1,128)}), f32[256,1,384]{2,1,0:T(1,128)S(1)}, u32[]{:S(2)}, u32[]{:S(2)}) %all-to-all-start.2) | async-done | bytes 393248 | tf_op jit(solution)/shard_map/all_to_all | solution.py:436
  110.4 0.8 shard_map.100
  111.2 11.5 %all_to_all.36 = f32[8,64,128]{2,1,0:T(8,128)S(1)} all-to-all(f32[8,64,128]{2,1,0:T(8,128)S(1)} %bitcast.18), channel_id=1, replica_groups=mesh['ga'=8,'ba'=32] {'ga'}, dimensions={0} | all-to-all | bytes 524288 | tf_op jit(solution)/shard_map/all_to_all | solution.py:444
  122.7 1.4 %shard_map.101 = (f32[256,128]{1,0:T(8,128)}, f32[256,128]{1,0:T(8,128)}) custom-call(f32[512,128]{1,0:T(8,128)S(1)} %bitcast.17, f32[256,128]{1,0:T(8,128)S(1)} %bitcast.21, f32[256,128]{1,0:T(8,128)S(1)} %bitcast.24, f32[96,128]{1,0:T(8,128)S(1)} %collective-permute-done.lo_halo, f32[96,128]{1,0:T(8,128)S(1)} %collective-permute-done.1.hi_halo, ...), custom_call_target="tpu_custom_call" | custom-call | tf_op jit(solution)/shard_map/pallas_call | solution.py:377
  (14 shorter events, 0.0 us)
Async XLA Ops:
  4.1 15.7 %copy-start.3 = (f32[16,64,256]{2,1,0:T(8,128)S(1)}, f32[16,64,256]{2,1,0:T(8,128)}, u32[]{:S(2)}) copy-start(f32[16,64,256]{2,1,0:T(8,128)} %amp.1) | copy-start | bytes 3145732
  4.2 15.7 %copy-start.5 = (f32[32,8,128]{2,1,0:T(8,128)S(1)}, f32[32,8,128]{2,1,0:T(8,128)}, u32[]{:S(2)}) copy-start(f32[32,8,128]{2,1,0:T(8,128)} %param.11) | copy-start | bytes 393220
  4.2 15.7 %copy-start.6 = (f32[32,8,128]{2,1,0:T(8,128)S(1)}, f32[32,8,128]{2,1,0:T(8,128)}, u32[]{:S(2)}) copy-start(f32[32,8,128]{2,1,0:T(8,128)} %param.10) | copy-start | bytes 393220
  4.2 57.8 %all-to-all-start = ((f32[256,8,128]{2,1,0:T(8,128)}), f32[256,8,128]{2,1,0:T(8,128)S(1)}, u32[]{:S(2)}, u32[]{:S(2)}) async-start(f32[256,8,128]{2,1,0:T(8,128)} %bitcast.25), calls=%async_computation | async-start | bytes 2097152 | tf_op jit(solution)/shard_map/all_to_all | solution.py:404
  21.1 40.9 %collective-permute-start.2 = (f32[16,16,256]{2,1,0:T(8,128)S(1)}, f32[16,16,256]{2,1,0:T(8,128)S(1)}, u32[]{:S(2)}, u32[]{:S(2)}) collective-permute-start(f32[16,16,256]{2,1,0:T(8,128)S(1)} %get-tuple-element.16), channel_id=1, source_target_pairs={{0,1},{1,0},{2,3},{3,2},{4,5},{5,4},{6,7},{7,6},{8,9},{9,8},{10,11... | collective-permute-start | bytes 786440 | tf_op jit(solution)/shard_map/ppermute | solution.py:410
  27.4 17.8 %collective-permute-start = (f32[96,128]{1,0:T(8,128)S(1)}, f32[96,128]{1,0:T(8,128)S(1)}, u32[]{:S(2)}, u32[]{:S(2)}) collective-permute-start(f32[96,128]{1,0:T(8,128)S(1)} %get-tuple-element.12), channel_id=1, source_target_pairs={{0,1},{1,2},{2,3},{3,4},{4,5},{5,6},{6,7},{7,8},{8,9},{9,10},{10,1... | collective-permute-start | bytes 147464 | tf_op jit(solution)/shard_map/ppermute | solution.py:417
  29.3 32.7 %collective-permute-start.1 = (f32[96,128]{1,0:T(8,128)S(1)}, f32[96,128]{1,0:T(8,128)S(1)}, u32[]{:S(2)}, u32[]{:S(2)}) collective-permute-start(f32[96,128]{1,0:T(8,128)S(1)} %get-tuple-element.13), channel_id=1, source_target_pairs={{1,0},{2,1},{3,2},{4,3},{5,4},{6,5},{7,6},{8,7},{9,8},{10,9},{11,1... | collective-permute-start | bytes 147464 | tf_op jit(solution)/shard_map/ppermute | solution.py:416
  30.6 1.3 %collective-permute-start.4 = (f32[16,256]{1,0:T(8,128)S(1)}, f32[16,256]{1,0:T(8,128)S(1)}, u32[]{:S(2)}, u32[]{:S(2)}) collective-permute-start(f32[16,256]{1,0:T(8,128)S(1)} %get-tuple-element.17), channel_id=1, source_target_pairs={{17,144},{19,146},{21,148},{23,150},{25,152},{27,154},{29,156},{31... | collective-permute-start | bytes 49160 | tf_op jit(solution)/shard_map/ppermute | solution.py:413
  31.3 0.7 collective-permute-start.3
  62.7 18.0 %all-to-all-start.1 = ((f32[16,32,256]{2,1,0:T(8,128)}), f32[16,32,256]{2,1,0:T(8,128)S(1)}, u32[]{:S(2)}, u32[]{:S(2)}) async-start(f32[16,32,256]{2,1,0:T(8,128)} %bitcast.5), calls=%async_computation.1 | async-start | bytes 1048576 | tf_op jit(solution)/shard_map/all_to_all | solution.py:423
  70.5 10.3 %copy-start = (bf16[1280,512]{1,0:T(8,128)(2,1)S(1)}, bf16[1280,512]{1,0:T(8,128)(2,1)}, u32[]{:S(2)}) copy-start(bf16[1280,512]{1,0:T(8,128)(2,1)} %constant.10.clone.table) | copy-start | bytes 3932164
  70.5 8.8 %collective-permute-start.5 = (f32[16,256]{1,0:T(8,128)S(1)}, f32[16,256]{1,0:T(8,128)S(1)}, u32[]{:S(2)}, u32[]{:S(2)}) collective-permute-start(f32[16,256]{1,0:T(8,128)S(1)} %get-tuple-element.17), channel_id=1, source_target_pairs={{16,0},{48,32},{80,64},{112,96},{144,128},{176,160},{208,192},{240... | collective-permute-start | bytes 49160 | tf_op jit(solution)/shard_map/ppermute | solution.py:414
  71.9 1.4 %copy-start.7 = (bf16[3072,256]{1,0:T(8,128)(2,1)S(1)}, bf16[3072,256]{1,0:T(8,128)(2,1)}, u32[]{:S(2)}) copy-start(bf16[3072,256]{1,0:T(8,128)(2,1)} %constant.9.clone.table) | copy-start | bytes 4718596
  76.3 1.0 copy-start.1
  80.8 1.2 copy-start.2
  82.0 28.4 %copy-start.4 = (bf16[2,320,512]{2,1,0:T(8,128)(2,1)S(1)}, bf16[2,320,512]{2,1,0:T(8,128)(2,1)}, u32[]{:S(2)}) copy-start(bf16[2,320,512]{2,1,0:T(8,128)(2,1)} %constant.11.clone.table) | copy-start | bytes 1966084
  84.3 26.1 %all-to-all-start.2 = ((f32[256,1,384]{2,1,0:T(1,128)}), f32[256,1,384]{2,1,0:T(1,128)S(1)}, u32[]{:S(2)}, u32[]{:S(2)}) async-start(f32[256,1,384]{2,1,0:T(1,128)} %bitcast.7), calls=%async_computation.2 | async-start | bytes 786432 | tf_op jit(solution)/shard_map/all_to_all | solution.py:436
  91.5 5.7 %collective-permute-start.6 = (f32[32,128]{1,0:T(8,128)S(1)}, f32[32,128]{1,0:T(8,128)S(1)}, u32[]{:S(2)}, u32[]{:S(2)}) collective-permute-start(f32[32,128]{1,0:T(8,128)S(1)} %get-tuple-element.18), channel_id=1, source_target_pairs={{0,32},{32,64},{64,96},{96,128},{128,160},{160,192},{192,224},{1,3... | collective-permute-start | bytes 49160 | tf_op jit(solution)/shard_map/ppermute | solution.py:438
  95.3 6.0 %collective-permute-start.7 = (f32[32,128]{1,0:T(8,128)S(1)}, f32[32,128]{1,0:T(8,128)S(1)}, u32[]{:S(2)}, u32[]{:S(2)}) collective-permute-start(f32[32,128]{1,0:T(8,128)S(1)} %get-tuple-element.19), channel_id=1, source_target_pairs={{32,0},{64,32},{96,64},{128,96},{160,128},{192,160},{224,192},{33,... | collective-permute-start | bytes 49160 | tf_op jit(solution)/shard_map/ppermute | solution.py:439
